TPU v7x, 32 devices: a whole 2x2x4 slice. The times are simulated.
32 devices in a mesh: groups: 2 (over y), dp: 4 (over z), mp: 2 (over x), teach: 2 (over core).
Axes of the slice: x: 2, y: 2, z: 4, core: 2. Of those that a mesh axis runs over, the one named last changes fastest.
Arguments:
- resid: bfloat16 [16, 256, 1280], P(('groups', 'dp', 'teach')), parts along dimension 0, may hold values from -6 to 6
- gain_mlp: float32 [1280], replicated, may hold values from 0.25 to 1.75
- gain_out: float32 [1280], replicated, may hold values from 0.25 to 1.75
- w_in: bfloat16 [1280, 5120], P(None, 'mp'), may hold values from -0.15625 to 0.15625
- w_out: bfloat16 [5120, 1280], P('mp'), may hold values from -0.078125 to 0.078125
- a_dino: bfloat16 [1280, 1536], P(None, 'mp'), may hold values from -0.15625 to 0.15625
- b_dino: bfloat16 [1536, 1536], P('mp')
- a_sig: bfloat16 [1280, 1152], P(None, 'mp'), may hold values from -0.15625 to 0.15625
- b_sig: bfloat16 [1152, 1152], P('mp')
- dino_feats: bfloat16 [16, 256, 1536], P('groups', ('dp', 'teach'), 'mp'), parts along dimension 0
- sig_feats: bfloat16 [16, 256, 1152], P('groups', ('dp', 'teach'), 'mp'), parts along dimension 0
- owner: int32 [16], P('groups'), parts along dimension 0, may hold values from 0 to 7, each once
Outputs:
- grad_w_in: float32 [2560, 5120], P(('groups', 'dp', 'teach'), 'mp'), parts along dimension 0
- grad_w_out: float32 [10240, 1280], P(('groups', 'mp'), ('dp', 'teach')), parts along dimension 0
- grad_a_dino: float32 [2560, 1536], P(('groups', 'dp', 'teach'), 'mp'), parts along dimension 0
- grad_b_dino: float32 [3072, 1536], P(('groups', 'mp'), ('dp', 'teach')), parts along dimension 0
- grad_a_sig: float32 [2560, 1152], P(('groups', 'dp', 'teach'), 'mp'), parts along dimension 0
- grad_b_sig: float32 [2304, 1152], P(('groups', 'mp'), ('dp', 'teach')), parts along dimension 0
There are 2 independent parts, one for each index of `groups`. A program takes and returns all parts, laid end to end along the dimension named above; an argument that names none is the same for every part. Nothing has to cross between parts.
Inputs may be any that keep to these rules, and one draw needn't show every extreme that they name: owner is a permutation of the images of a group.
All inputs are finite; a program needn't handle non-finite values.
Results may differ from a plain program's by a relative error of at most 0.022.
Values may be sent and summed in bfloat16 or wider, within the bound.
No kernel may reach another device: no remote copies, remote signals or barrier semaphores. Data moves between devices by JAX's collectives and lax.ppermute only.
A program may use at most 128 MiB of HBM per device.

v0:
```python
import math

import jax
import jax.numpy as jnp
from jax import lax
from jax.sharding import PartitionSpec as P

EPS = 1e-06


def layer_norm(values, gain):
    center = values - jnp.mean(values, axis=-1, keepdims=True)
    spread = jnp.mean(center * center, axis=-1, keepdims=True)
    return center * lax.rsqrt(spread + EPS) * gain


def norm_back(values, gain, upstream):
    center = values - jnp.mean(values, axis=-1, keepdims=True)
    recip = lax.rsqrt(jnp.mean(center * center, axis=-1, keepdims=True) + EPS)
    unit = center * recip
    scaled = upstream * gain
    return recip * (
        scaled
        - jnp.mean(scaled, axis=-1, keepdims=True)
        - unit * jnp.mean(scaled * unit, axis=-1, keepdims=True)
    )


def gelu_tanh(values):
    return jax.nn.gelu(values, approximate=True)


def gelu_back(values, upstream):
    _, pullback = jax.vjp(gelu_tanh, values)
    return pullback(upstream)[0]


def cosine_back(predicted, target, sq_pred, cross, sq_target, channels, factor):
    norm_pred = sq_pred + channels * EPS
    norm_target = sq_target + channels * EPS
    recip = lax.rsqrt(norm_pred * norm_target)
    cosine = cross * recip
    return factor * (
        predicted
        - target
        - channels * (target * recip[:, None] - (cosine / norm_pred)[:, None] * predicted)
    )


def contract_rows(left, right):
    return lax.dot_general(
        left, right, (((0,), (0,)), ((), ())), preferred_element_type=jnp.float32
    )


def contract_cols(left, right):
    return lax.dot_general(
        left, right, (((1,), (1,)), ((), ())), preferred_element_type=jnp.float32
    )


def per_device(
    resid,
    gain_mlp,
    gain_out,
    w_in,
    w_out,
    a_dino,
    b_dino,
    a_sig,
    b_sig,
    dino_feats,
    sig_feats,
    owner,
):
    n_chips = lax.axis_size("dp")
    n_cores = lax.axis_size("teach")
    images_here = resid.shape[0]
    patches = resid.shape[1]
    width = resid.shape[2]
    rows = images_here * patches
    factor = 1.0 / math.sqrt(n_chips * n_cores * rows)
    total_images = owner.shape[0]
    inverse = (
        jnp.zeros((total_images,), jnp.int32)
        .at[owner]
        .set(jnp.arange(total_images, dtype=jnp.int32))
    )
    send_dino = jnp.take(dino_feats, inverse, axis=0)
    send_sig = jnp.take(sig_feats, inverse, axis=0)
    recv_dino, recv_sig = (
        lax.all_to_all(send_dino, ("dp", "teach"), split_axis=0, concat_axis=1, tiled=True),
        lax.all_to_all(send_sig, ("dp", "teach"), split_axis=0, concat_axis=1, tiled=True),
    )
    teacher_dino = recv_dino.reshape(rows, -1).astype(jnp.float32)
    teacher_sig = recv_sig.reshape(rows, -1).astype(jnp.float32)
    source = resid.reshape(rows, width).astype(jnp.float32)
    normed = layer_norm(source, gain_mlp).astype(jnp.bfloat16)
    pre_act = jnp.dot(normed, w_in, preferred_element_type=jnp.float32)
    hidden = gelu_tanh(pre_act).astype(jnp.bfloat16)
    stream = source + lax.psum(
        jnp.dot(hidden, w_out, preferred_element_type=jnp.float32).astype(jnp.bfloat16), "mp"
    ).astype(jnp.float32)
    summary = layer_norm(stream, gain_out).astype(jnp.bfloat16)
    pre_dino = jnp.dot(summary, a_dino, preferred_element_type=jnp.float32)
    act_dino = gelu_tanh(pre_dino).astype(jnp.bfloat16)
    pre_sig = jnp.dot(summary, a_sig, preferred_element_type=jnp.float32)
    act_sig = gelu_tanh(pre_sig).astype(jnp.bfloat16)
    pred_dino, pred_sig = (
        lax.psum_scatter(
            jnp.dot(act_dino, b_dino, preferred_element_type=jnp.float32).astype(jnp.bfloat16),
            "mp",
            scatter_dimension=1,
            tiled=True,
        ).astype(jnp.float32),
        lax.psum_scatter(
            jnp.dot(act_sig, b_sig, preferred_element_type=jnp.float32).astype(jnp.bfloat16),
            "mp",
            scatter_dimension=1,
            tiled=True,
        ).astype(jnp.float32),
    )
    stats = lax.psum(
        (
            jnp.sum(pred_dino * pred_dino, axis=-1),
            jnp.sum(pred_dino * teacher_dino, axis=-1),
            jnp.sum(teacher_dino * teacher_dino, axis=-1),
            jnp.sum(pred_sig * pred_sig, axis=-1),
            jnp.sum(pred_sig * teacher_sig, axis=-1),
            jnp.sum(teacher_sig * teacher_sig, axis=-1),
        ),
        "mp",
    )
    back_dino = cosine_back(
        pred_dino, teacher_dino, stats[0], stats[1], stats[2], b_dino.shape[1], factor
    ).astype(jnp.bfloat16)
    back_sig = cosine_back(
        pred_sig, teacher_sig, stats[3], stats[4], stats[5], b_sig.shape[1], factor
    ).astype(jnp.bfloat16)
    full_dino, full_sig = (
        lax.all_gather(back_dino, "mp", axis=1, tiled=True),
        lax.all_gather(back_sig, "mp", axis=1, tiled=True),
    )
    grad_b_d = contract_rows(act_dino, full_dino)
    grad_b_s = contract_rows(act_sig, full_sig)
    down_dino = gelu_back(pre_dino, contract_cols(full_dino, b_dino)).astype(jnp.bfloat16)
    down_sig = gelu_back(pre_sig, contract_cols(full_sig, b_sig)).astype(jnp.bfloat16)
    grad_a_d = contract_rows(summary, down_dino)
    grad_a_s = contract_rows(summary, down_sig)
    adaptor_sums = (
        lax.psum_scatter(
            grad_a_d.astype(jnp.bfloat16), ("dp", "teach"), scatter_dimension=0, tiled=True
        ).astype(jnp.float32),
        lax.psum_scatter(
            grad_b_d.astype(jnp.bfloat16), ("dp", "teach"), scatter_dimension=1, tiled=True
        ).astype(jnp.float32),
        lax.psum_scatter(
            grad_a_s.astype(jnp.bfloat16), ("dp", "teach"), scatter_dimension=0, tiled=True
        ).astype(jnp.float32),
        lax.psum_scatter(
            grad_b_s.astype(jnp.bfloat16), ("dp", "teach"), scatter_dimension=1, tiled=True
        ).astype(jnp.float32),
    )
    upstream = lax.psum(
        (contract_cols(down_dino, a_dino) + contract_cols(down_sig, a_sig)).astype(jnp.bfloat16),
        "mp",
    ).astype(jnp.float32)
    back_stream = norm_back(stream, gain_out, upstream).astype(jnp.bfloat16)
    grad_wo = contract_rows(hidden, back_stream)
    back_hidden = gelu_back(pre_act, contract_cols(back_stream, w_out)).astype(jnp.bfloat16)
    grad_wi = contract_rows(normed, back_hidden)
    block_sums = (
        lax.psum_scatter(
            grad_wi.astype(jnp.bfloat16), ("dp", "teach"), scatter_dimension=0, tiled=True
        ).astype(jnp.float32),
        lax.psum_scatter(
            grad_wo.astype(jnp.bfloat16), ("dp", "teach"), scatter_dimension=1, tiled=True
        ).astype(jnp.float32),
    )
    return (
        block_sums[0],
        block_sums[1],
        adaptor_sums[0],
        adaptor_sums[1],
        adaptor_sums[2],
        adaptor_sums[3],
    )


def solution(mesh):
    placed = (
        P(("groups", "dp", "teach"), None, None),
        P(),
        P(),
        P(None, "mp"),
        P("mp", None),
        P(None, "mp"),
        P("mp", None),
        P(None, "mp"),
        P("mp", None),
        P("groups", ("dp", "teach"), "mp"),
        P("groups", ("dp", "teach"), "mp"),
        P("groups"),
    )
    return jax.shard_map(
        per_device,
        mesh=mesh,
        in_specs=placed,
        out_specs=(
            P(("groups", "dp", "teach"), "mp"),
            P(("groups", "mp"), ("dp", "teach")),
            P(("groups", "dp", "teach"), "mp"),
            P(("groups", "mp"), ("dp", "teach")),
            P(("groups", "dp", "teach"), "mp"),
            P(("groups", "mp"), ("dp", "teach")),
        ),
        check_vma=False,
    )
```

profile of v0, /device:TPU:0, one launch (start us, length us, event | category | flops | bytes accessed | tf_op | source)
XLA Modules:
  0.0 465.9 jit_solution(2068013766392554938)
XLA Ops:
  7.2 1.4 convert_reduce_fusion
  8.7 1.6 fusion.12
  10.2 5.2 %fusion.64 = f32[256,2560]{1,0:T(8,128)S(1)} fusion(bf16[1280,2560]{1,0:T(8,128)(2,1)} %param.15, bf16[1,256,1280]{2,1,0:T(8,128)(2,1)} %param.12, f32[1280]{0:T(1024)} %param.13, f32[256]{0:T(256)S(1)} %add_rsqrt_fusion.1, f32[256]{0:T(256)S(1)} %broadcast_multiply_fusion.3), kind=kOutput, calls=%fused_computation.118 | convolution fusion | flops 1679360000 | bytes 9837568 | tf_op jit(solution)/shard_map/dot_general | solution.py:99
  15.4 1.5 copy-done.21
  16.9 3.2 convolution_convert_fusion.7
  20.2 0.6 scatter_custom_fusion
  20.8 33.6 %all-reduce.4.cloned.1.call-done = bf16[256,1280]{1,0:T(8,128)(2,1)} async-done(((bf16[256,1280]{1,0:T(8,128)(2,1)}), bf16[256,1280]{1,0:T(8,128)(2,1)}) %all-reduce.4.cloned.1.call-update) | async-done | bytes 655376 | tf_op jit(solution)/shard_map/psum | solution.py:101
  54.4 1.4 fusion.24
  55.9 0.3 multiply_reduce_fusion.1
  56.2 0.3 multiply_convert_fusion.2
  56.6 0.8 copy-done.2
  57.4 0.6 fusion.68
  58.0 0.8 copy-done.9
  58.8 1.6 convolution_convert_fusion.8
  60.5 1.6 gather_fusion.1
  62.1 2.4 fusion.67
  64.6 0.9 copy-done.14
  65.5 1.7 convolution_convert_fusion.6
  67.2 0.8 broadcast_select_fusion.1
  68.1 4.6 all-to-all-start.1
  72.7 2.3 gather_fusion
  75.0 1.8 broadcast_select_fusion
  76.8 7.0 %all-to-all-done.1 = bf16[8,32,576]{2,1,0:T(8,128)(2,1)S(1)} async-done(((bf16[8,32,576]{2,1,0:T(8,128)(2,1)}), bf16[8,32,576]{2,1,0:T(8,128)(2,1)S(1)}, u32[]{:S(2)}, u32[]{:S(2)}) %all-to-all-start.1) | async-done | bytes 294944 | tf_op jit(solution)/shard_map/all_to_all | solution.py:93
  83.8 0.7 copy-done.7
  84.5 3.5 all-to-all-start
  88.1 1.1 multiply_reduce_fusion.2
  89.3 1.9 copy.19
  91.2 9.3 %all-to-all-done = bf16[8,32,768]{2,1,0:T(8,128)(2,1)S(1)} async-done(((bf16[8,32,768]{2,1,0:T(8,128)(2,1)}), bf16[8,32,768]{2,1,0:T(8,128)(2,1)S(1)}, u32[]{:S(2)}, u32[]{:S(2)}) %all-to-all-start) | async-done | bytes 393248 | tf_op jit(solution)/shard_map/all_to_all | solution.py:92
  100.7 1.3 fusion.51
  102.0 1.2 fusion.36
  103.3 5.0 %all-reduce = (f32[256]{0:T(256)S(1)}, f32[256]{0:T(256)S(1)}, f32[256]{0:T(256)S(1)}, f32[256]{0:T(256)S(1)}, f32[256]{0:T(256)S(1)}, /*index=5*/f32[256]{0:T(256)S(1)}) all-reduce(f32[256]{0:T(256)S(1)} %get-tuple-element.11, f32[256]{0:T(256)S(1)} %get-tuple-element.10, ...), channel_id=1, replica_groups=mesh['groups'=2,'dp'=4,'mp'=2,'teach'=2] {'mp'}, use_global_device_ids=true, to_apply=%region_19.20 | all-reduce | flops 1536 | bytes 12288 | tf_op jit(solution)/shard_map/psum | solution.py:123
  108.3 1.4 fusion.50
  109.7 8.1 %all_gather.7 = bf16[256,1152]{0,1:T(8,128)(2,1)S(1)} all-gather(bf16[256,576]{0,1:T(8,128)(2,1)S(1)} %fusion.50), channel_id=1, replica_groups=mesh['groups'=2,'dp'=4,'mp'=2,'teach'=2] {'mp'}, dimensions={1}, use_global_device_ids=true | all-gather | bytes 884736 | tf_op jit(solution)/shard_map/all_gather | solution.py:142
  117.8 0.8 fusion.47
  118.6 0.4 copy-done.11
  119.0 0.4 fusion.35
  119.4 9.4 %all_gather.6 = bf16[256,1536]{1,0:T(8,128)(2,1)S(1)} all-gather(bf16[256,768]{1,0:T(8,128)(2,1)S(1)} %fusion.35), channel_id=1, replica_groups=mesh['groups'=2,'dp'=4,'mp'=2,'teach'=2] {'mp'}, dimensions={1}, use_global_device_ids=true | all-gather | bytes 1179648 | tf_op jit(solution)/shard_map/all_gather | solution.py:141
  128.8 0.9 copy-done.13
  129.7 1.1 fusion.32
  130.8 0.3 copy-done.6
  131.1 0.7 fusion.69
  131.8 0.8 copy-done.4
  132.6 1.6 fusion.7
  134.3 3.1 convolution_convert_fusion.4
  137.4 3.1 convolution_convert_fusion.5
  140.6 3.1 convolution_convert_fusion.2
  143.8 3.7 convolution_convert_fusion.3
  147.6 17.1 %all-reduce.6.cloned.1.call-done = bf16[256,1280]{1,0:T(8,128)(2,1)} async-done(((bf16[256,1280]{1,0:T(8,128)(2,1)}), bf16[256,1280]{1,0:T(8,128)(2,1)}) %all-reduce.6.cloned.1.call-update) | async-done | bytes 655376 | tf_op jit(solution)/shard_map/psum | solution.py:164
  164.6 1.8 fusion.18
  166.5 11.4 %convolution_convert_fusion.1 = bf16[1280,2560]{1,0:T(8,128)(2,1)} fusion(f32[256,2560]{1,0:T(8,128)} %copy-done.21, bf16[1,256,1280]{2,1,0:T(8,128)(2,1)S(1)} %copy-done.1, f32[1280]{0:T(1024)S(1)} %copy-done.19, f32[256]{0:T(256)S(1)} %add_rsqrt_fusion.1, f32[256]{0:T(256)S(1)} %broadcast_multiply_fusion.3, bf16[2560,1280]{1,0:T(8,128)(2,1)} %param.16, ...), kind=kOutput, calls=%fused_computation.4 | convolution fusion | flops 3377397760 | bytes 17711104 | tf_op jit(solution)/shard_map/dot_general | solution.py:51
  177.9 0.3 reduce-scatter.15.cloned.1.call-start
  178.1 7.3 %convolution_convert_fusion = bf16[2560,1280]{0,1:T(8,128)(2,1)} fusion(f32[256,2560]{1,0:T(8,128)} %copy-done.21, bf16[256,1280]{1,0:T(8,128)(2,1)} %all-reduce.6.cloned.1.call-done, bf16[256,1280]{1,0:T(8,128)(2,1)} %all-reduce.4.cloned.1.call-done, bf16[1,256,1280]{2,1,0:T(8,128)(2,1)S(1)} %copy-done.1, f32[256]{0:T(256)S(1)} %broadcast_multiply_fusion, ...), kind=kOutput, calls=%fused_computation.3 | convolution fusion | flops 1690828800 | bytes 11150336 | tf_op jit(solution)/shard_map/dot_general | solution.py:51
  185.5 15.8 %reduce-scatter.23.cloned.1.call-done = bf16[576,144]{0,1:T(8,128)(2,1)} async-done(((bf16[576,1152]{0,1:T(8,128)(2,1)}), bf16[576,144]{0,1:T(8,128)(2,1)}) %reduce-scatter.23.cloned.1.call-update) | async-done | bytes 165904 | tf_op jit(solution)/shard_map/reduce_scatter | solution.py:160
  201.3 1.7 convert_element_type.157
  203.0 33.7 %reduce-scatter.21.cloned.1.call-done = bf16[160,576]{1,0:T(8,128)(2,1)} async-done(((bf16[1280,576]{1,0:T(8,128)(2,1)}), bf16[160,576]{1,0:T(8,128)(2,1)}) %reduce-scatter.21.cloned.1.call-update) | async-done | bytes 184336 | tf_op jit(solution)/shard_map/reduce_scatter | solution.py:157
  236.7 1.7 convert_element_type.155
  238.4 34.1 %reduce-scatter.17.cloned.1.call-done = bf16[160,768]{1,0:T(8,128)(2,1)} async-done(((bf16[1280,768]{1,0:T(8,128)(2,1)}), bf16[160,768]{1,0:T(8,128)(2,1)}) %reduce-scatter.17.cloned.1.call-update) | async-done | bytes 245776 | tf_op jit(solution)/shard_map/reduce_scatter | solution.py:151
  272.5 1.8 convert_element_type.151
  274.3 35.7 %reduce-scatter.19.cloned.1.call-done = bf16[768,192]{0,1:T(8,128)(2,1)} async-done(((bf16[768,1536]{0,1:T(8,128)(2,1)}), bf16[768,192]{0,1:T(8,128)(2,1)}) %reduce-scatter.19.cloned.1.call-update) | async-done | bytes 294928 | tf_op jit(solution)/shard_map/reduce_scatter | solution.py:154
  309.9 1.8 convert_element_type.153
  311.7 71.9 %reduce-scatter.13.cloned.1.call-done = bf16[160,2560]{1,0:T(8,128)(2,1)} async-done(((bf16[1280,2560]{1,0:T(8,128)(2,1)}), bf16[160,2560]{1,0:T(8,128)(2,1)}) %reduce-scatter.13.cloned.1.call-update) | async-done | bytes 819216 | tf_op jit(solution)/shard_map/reduce_scatter | solution.py:173
  383.6 2.5 convert_element_type.147
  386.1 70.5 %reduce-scatter.15.cloned.1.call-done = bf16[2560,160]{0,1:T(8,128)(2,1)} async-done(((bf16[2560,1280]{0,1:T(8,128)(2,1)}), bf16[2560,160]{0,1:T(8,128)(2,1)}) %reduce-scatter.15.cloned.1.call-update) | async-done | bytes 819216 | tf_op jit(solution)/shard_map/reduce_scatter | solution.py:176
  456.6 2.5 convert_element_type.149
  (76 shorter events, 1.1 us)
Async XLA Ops:
  7.2 58.3 %copy-start = (bf16[768,1536]{1,0:T(8,128)(2,1)S(1)}, bf16[768,1536]{1,0:T(8,128)(2,1)}, u32[]{:S(2)}) copy-start(bf16[768,1536]{1,0:T(8,128)(2,1)} %param.18) | copy-start | bytes 7077892
  7.2 47.3 %all-reduce.4.cloned.1.call-start = ((), (), s32[]{:S(2)}) async-start(), calls=%async_computation.10 | async-start | bytes 1310720 | tf_op jit(solution)/shard_map/psum | solution.py:101
  8.6 8.3 %slice-start = ((s8[6553600]{0:T(1024)(128)(4,1)}), s8[4194304]{0:T(1024)(128)(4,1)S(1)}, s32[]{:S(2)}) async-start(s8[6553600]{0:T(1024)(128)(4,1)} %bitcast.71), calls=%async_computation.20 | async-start | bytes 8388608
  10.2 6.7 %slice-start.1 = ((s8[6553600]{0:T(1024)(128)(4,1)}), s8[2359296]{0:T(1024)(128)(4,1)S(1)}, s32[]{:S(2)}) async-start(s8[6553600]{0:T(1024)(128)(4,1)} %bitcast.71), calls=%async_computation.21 | async-start | bytes 4718592
  15.4 1.5 copy-start.21
  16.9 3.3 copy-start.20
  16.9 37.5 %copy-start.1 = (bf16[1,256,1280]{2,1,0:T(8,128)(2,1)S(1)}, bf16[1,256,1280]{2,1,0:T(8,128)(2,1)}, u32[]{:S(2)}) copy-start(bf16[1,256,1280]{2,1,0:T(8,128)(2,1)} %param.12) | copy-start | bytes 1966084
  20.1 36.1 %copy-start.16 = (f32[1280]{0:T(1024)S(1)}, f32[1280]{0:T(1024)}, u32[]{:S(2)}) copy-start(f32[1280]{0:T(1024)} %param.14) | copy-start | bytes 15364
  20.1 80.6 %reduce-scatter.11.cloned.1.call-start = ((), (), s32[]{:S(2)}) async-start(), calls=%async_computation.12 | async-start | bytes 884736 | tf_op jit(solution)/shard_map/reduce_scatter | solution.py:116
  54.4 1.4 copy-start.3
  55.9 1.5 copy-start.5
  56.6 0.8 copy-start.2
  57.4 1.4 copy-start.17
  58.0 0.8 copy-start.9
  60.5 41.6 %reduce-scatter.9.cloned.1.call-start = ((), (), s32[]{:S(2)}) async-start(), calls=%async_computation.11 | async-start | bytes 1179648 | tf_op jit(solution)/shard_map/reduce_scatter | solution.py:110
  64.6 0.9 copy-start.14
  68.1 15.8 %all-to-all-start.1 = ((bf16[8,32,576]{2,1,0:T(8,128)(2,1)}), bf16[8,32,576]{2,1,0:T(8,128)(2,1)S(1)}, u32[]{:S(2)}, u32[]{:S(2)}) async-start(bf16[8,32,576]{2,1,0:T(8,128)(2,1)} %broadcast_select_fusion.1), calls=%async_computation.3 | async-start | bytes 655360 | tf_op jit(solution)/shard_map/all_to_all | solution.py:93
  83.8 0.7 copy-start.7
  84.5 15.9 %all-to-all-start = ((bf16[8,32,768]{2,1,0:T(8,128)(2,1)}), bf16[8,32,768]{2,1,0:T(8,128)(2,1)S(1)}, u32[]{:S(2)}, u32[]{:S(2)}) async-start(bf16[8,32,768]{2,1,0:T(8,128)(2,1)} %broadcast_select_fusion), calls=%async_computation.1 | async-start | bytes 786432 | tf_op jit(solution)/shard_map/all_to_all | solution.py:92
  88.0 76.6 %all-reduce.6.cloned.1.call-start = ((), (), s32[]{:S(2)}) async-start(), calls=%async_computation.13 | async-start | bytes 1310720 | tf_op jit(solution)/shard_map/psum | solution.py:164
  108.3 9.6 %copy-start.10 = (f32[256,576]{0,1:T(8,128)S(1)}, f32[256,576]{0,1:T(8,128)}, u32[]{:S(2)}) copy-start(f32[256,576]{0,1:T(8,128)} %copy-done.9) | copy-start | bytes 1769476
  108.3 9.6 %copy-start.18 = (bf16[576,1152]{1,0:T(8,128)(2,1)S(1)}, bf16[576,1152]{1,0:T(8,128)(2,1)}, u32[]{:S(2)}) copy-start(bf16[576,1152]{1,0:T(8,128)(2,1)} %param.20) | copy-start | bytes 3981316
  117.8 0.8 copy-start.8
  117.8 1.2 copy-start.11
  118.6 12.2 %copy-start.12 = (bf16[256,576]{0,1:T(8,128)(2,1)}, bf16[256,576]{0,1:T(8,128)(2,1)S(1)}, u32[]{:S(2)}) copy-start(bf16[256,576]{0,1:T(8,128)(2,1)S(1)} %fusion.47) | copy-start | bytes 884740
  118.6 11.1 %copy-start.15 = (f32[256,768]{1,0:T(8,128)S(1)}, f32[256,768]{1,0:T(8,128)}, u32[]{:S(2)}) copy-start(f32[256,768]{1,0:T(8,128)} %copy-done.14) | copy-start | bytes 2359300
  128.8 0.9 copy-start.13
  129.7 1.4 copy-start.6
  131.1 1.5 copy-start.4
  134.3 67.1 %reduce-scatter.23.cloned.1.call-start = ((), (), s32[]{:S(2)}) async-start(), calls=%async_computation.19 | async-start | bytes 1658880 | tf_op jit(solution)/shard_map/reduce_scatter | solution.py:160
  137.4 99.3 %reduce-scatter.21.cloned.1.call-start = ((), (), s32[]{:S(2)}) async-start(), calls=%async_computation.18 | async-start | bytes 1843200 | tf_op jit(solution)/shard_map/reduce_scatter | solution.py:157
  140.6 131.9 %reduce-scatter.17.cloned.1.call-start = ((), (), s32[]{:S(2)}) async-start(), calls=%async_computation.16 | async-start | bytes 2211840 | tf_op jit(solution)/shard_map/reduce_scatter | solution.py:151
  143.7 166.2 %reduce-scatter.19.cloned.1.call-start = ((), (), s32[]{:S(2)}) async-start(), calls=%async_computation.17 | async-start | bytes 2654208 | tf_op jit(solution)/shard_map/reduce_scatter | solution.py:154
  147.5 18.9 %copy-start.19 = (f32[1280]{0:T(1024)S(1)}, f32[1280]{0:T(1024)}, u32[]{:S(2)}) copy-start(f32[1280]{0:T(1024)} %param.13) | copy-start | bytes 15364
  147.5 236.1 %reduce-scatter.13.cloned.1.call-start = ((), (), s32[]{:S(2)}) async-start(), calls=%async_computation.14 | async-start | bytes 7372800 | tf_op jit(solution)/shard_map/reduce_scatter | solution.py:173
  177.9 278.8 %reduce-scatter.15.cloned.1.call-start = ((), (), s32[]{:S(2)}) async-start(), calls=%async_computation.15 | async-start | bytes 7372800 | tf_op jit(solution)/shard_map/reduce_scatter | solution.py:176
Sparse Core Ops, SparseCore 0:
  20.2 34.1 all-reduce.3
  60.6 15.2 reduce-scatter.10
  78.7 17.4 reduce-scatter.8
  134.4 30.2 all-reduce.5
  167.4 33.9 reduce-scatter.22
  204.0 32.6 reduce-scatter.20
  239.0 33.4 reduce-scatter.16
  274.9 34.9 reduce-scatter.18
  312.4 71.2 reduce-scatter.12
  385.9 70.6 reduce-scatter.14
where the time goes:
time: 467 us; the launch traced here: 466 us
  waiting for transfers between devices  329 us (70%)
  matrix products  50.5 us (11%)
  other arithmetic  27.1 us (6%)
  blocking collectives  22.5 us (5%)
  between operations  14.5 us (3%)
  local copies, waits for them, and re-layouts  13.8 us (3%)
  starting transfers between devices  8.7 us (2%)
    reduce_scatter x1, waiting for transfers between devices, per_device(): lax.psum_scatter(grad_wi.astype(jnp.bfloat16), ('dp', 'teach'), scatter_d...  71.9 us
    reduce_scatter x1, waiting for transfers between devices, per_device(): lax.psum_scatter(grad_wo.astype(jnp.bfloat16), ('dp', 'teach'), scatter_d...  70.5 us
    reduce_scatter x1, waiting for transfers between devices, per_device(): lax.psum_scatter(grad_b_d.astype(jnp.bfloat16), ('dp', 'teach'), scatter_...  35.7 us
    reduce_scatter x1, waiting for transfers between devices, per_device(): lax.psum_scatter(grad_a_d.astype(jnp.bfloat16), ('dp', 'teach'), scatter_...  34.1 us
    reduce_scatter x1, waiting for transfers between devices, per_device(): lax.psum_scatter(grad_a_s.astype(jnp.bfloat16), ('dp', 'teach'), scatter_...  33.7 us
    psum x1, waiting for transfers between devices, per_device(): lax.psum(jnp.dot(hidden, w_out, preferred_element_type=jnp.float32).astyp...  33.6 us
    dot_general x6, matrix products, contract_rows(): lax.dot_general(left, right, (((0,), (0,)), ((), ())), preferred_element_...  31.7 us
    psum x1, waiting for transfers between devices, per_device(): lax.psum((contract_cols(down_dino, a_dino) + contract_cols(down_sig, a_si...  17.1 us
  transfers between devices with their start and end apart: 12, of which 10 were waited for; matrix products, arithmetic and copies ran while one was open for 13% of the time, Pallas kernels for 0%

commit v1 on v0

v1 whole, which is shorter than its diff:
```python
import math

import jax
import jax.numpy as jnp
from jax import lax
from jax.sharding import PartitionSpec as P

EPS = 1e-06
ROOT = math.sqrt(2.0 / math.pi)
CUBE = 0.044715


def layer_norm(values, gain):
    center = values - jnp.mean(values, axis=-1, keepdims=True)
    spread = jnp.mean(center * center, axis=-1, keepdims=True)
    return center * lax.rsqrt(spread + EPS) * gain


def norm_back(values, gain, upstream):
    center = values - jnp.mean(values, axis=-1, keepdims=True)
    recip = lax.rsqrt(jnp.mean(center * center, axis=-1, keepdims=True) + EPS)
    unit = center * recip
    scaled = upstream * gain
    return recip * (
        scaled
        - jnp.mean(scaled, axis=-1, keepdims=True)
        - unit * jnp.mean(scaled * unit, axis=-1, keepdims=True)
    )


def gelu_and_slope(values):
    square = values * values
    bend = jnp.tanh(ROOT * values * (1.0 + CUBE * square))
    half = 0.5 * (1.0 + bend)
    slope = half + 0.5 * values * (1.0 - bend * bend) * (ROOT * (1.0 + 3.0 * CUBE * square))
    return (values * half).astype(jnp.bfloat16), slope.astype(jnp.bfloat16)


def cosine_back(predicted, target, channels, factor):
    sq_pred = jnp.sum(predicted * predicted, axis=-1, keepdims=True)
    cross = jnp.sum(predicted * target, axis=-1, keepdims=True)
    sq_target = jnp.sum(target * target, axis=-1, keepdims=True)
    norm_pred = sq_pred + channels * EPS
    norm_target = sq_target + channels * EPS
    recip = lax.rsqrt(norm_pred * norm_target)
    cosine = cross * recip
    return factor * (
        predicted - target - channels * (target * recip - (cosine / norm_pred) * predicted)
    )


def matmul(left, right):
    return jnp.dot(left, right, preferred_element_type=jnp.float32)


def contract_rows(left, right):
    return lax.dot_general(
        left, right, (((0,), (0,)), ((), ())), preferred_element_type=jnp.float32
    )


def contract_cols(left, right):
    return lax.dot_general(
        left, right, (((1,), (1,)), ((), ())), preferred_element_type=jnp.float32
    )


def shift(values, axis):
    count = lax.axis_size(axis)
    return lax.ppermute(values, axis, [(i, (i + 1) % count) for i in range(count)])


def ring_gather(values, axis):
    held = [values]
    for _ in range(lax.axis_size(axis) - 1):
        held.append(shift(held[-1], axis))
    return held


def ring_sum(blocks, axis):
    count = lax.axis_size(axis)
    me = lax.axis_index(axis)

    def block(i):
        return lax.dynamic_index_in_dim(blocks, lax.rem(i + 2 * count, count), 0, keepdims=False)

    held = block(me - 1)
    for step in range(1, count):
        got = shift(held, axis).astype(jnp.float32)
        total = got + block(me - 1 - step).astype(jnp.float32)
        held = total.astype(jnp.bfloat16)
    return total if count > 1 else held.astype(jnp.float32)


def core_sum(blocks):
    count = lax.axis_size("teach")
    if count != 2:
        return lax.psum_scatter(blocks, "teach", scatter_dimension=1, tiled=False)
    me = lax.axis_index("teach")
    mine = lax.dynamic_index_in_dim(blocks, me, 1, keepdims=False)
    theirs = lax.dynamic_index_in_dim(blocks, 1 - me, 1, keepdims=False)
    got = shift(theirs, "teach")
    return (mine.astype(jnp.float32) + got.astype(jnp.float32)).astype(jnp.bfloat16)


def sum_mp(part):
    if lax.axis_size("mp") == 2:
        return part.astype(jnp.float32) + shift(part, "mp").astype(jnp.float32)
    return lax.psum(part, "mp").astype(jnp.float32)


def join_mp(values, axis):
    if lax.axis_size("mp") != 2:
        return lax.all_gather(values, "mp", axis=axis, tiled=True)
    other = shift(values, "mp")
    return in_order(values, other, axis)


def in_order(own, other, axis):
    first = lax.axis_index("mp") == 0
    return jnp.concatenate(
        [jnp.where(first, own, other), jnp.where(first, other, own)], axis=axis
    )


def own_teacher(feats, inverse):
    sent = feats.at[inverse].get(mode="promise_in_bounds", unique_indices=True)
    got = lax.all_to_all(sent, ("dp", "teach"), split_axis=0, concat_axis=1, tiled=True)
    return join_mp(got.reshape(-1, feats.shape[2]), 1)


def gather_back(part, stream, gain):
    if lax.axis_size("mp") != 2:
        own = norm_back(stream, gain, sum_mp(part)).astype(jnp.bfloat16)
        return ring_gather(own, "dp")
    me = lax.axis_index("mp")
    half = part.shape[0] // 2
    mine = lax.dynamic_slice_in_dim(part, me * half, half, 0)
    theirs = lax.dynamic_slice_in_dim(part, (1 - me) * half, half, 0)
    upstream = mine.astype(jnp.float32) + shift(theirs, "mp").astype(jnp.float32)
    rows = lax.dynamic_slice_in_dim(stream, me * half, half, 0)
    back = norm_back(rows, gain, upstream).astype(jnp.bfloat16)
    return [in_order(held, shift(held, "mp"), 0) for held in ring_gather(back, "dp")]


def per_device(
    resid,
    gain_mlp,
    gain_out,
    w_in,
    w_out,
    a_dino,
    b_dino,
    a_sig,
    b_sig,
    dino_feats,
    sig_feats,
    owner,
):
    n_chips = lax.axis_size("dp")
    n_cores = lax.axis_size("teach")
    width = resid.shape[2]
    rows = resid.shape[0] * resid.shape[1]
    factor = 1.0 / math.sqrt(n_chips * n_cores * rows)
    total_images = owner.shape[0]
    chip = lax.axis_index("dp")
    core = lax.axis_index("teach")

    source = resid.reshape(rows, width).astype(jnp.float32)
    normed = layer_norm(source, gain_mlp).astype(jnp.bfloat16)
    all_normed = ring_gather(normed, "dp")

    inverse = (
        jnp.zeros((total_images,), jnp.int32)
        .at[owner]
        .set(jnp.arange(total_images, dtype=jnp.int32))
    )
    teacher_dino = own_teacher(dino_feats, inverse)
    teacher_sig = own_teacher(sig_feats, inverse)

    hidden, slope = gelu_and_slope(matmul(normed, w_in))
    stream = source + sum_mp(matmul(hidden, w_out).astype(jnp.bfloat16))
    summary = layer_norm(stream, gain_out).astype(jnp.bfloat16)

    act_dino, slope_dino = gelu_and_slope(matmul(summary, a_dino))
    act_sig, slope_sig = gelu_and_slope(matmul(summary, a_sig))
    pred_dino = sum_mp(matmul(act_dino, b_dino).astype(jnp.bfloat16))
    pred_sig = sum_mp(matmul(act_sig, b_sig).astype(jnp.bfloat16))

    back_dino = cosine_back(
        pred_dino, teacher_dino.astype(jnp.float32), b_dino.shape[1], factor
    ).astype(jnp.bfloat16)
    back_sig = cosine_back(
        pred_sig, teacher_sig.astype(jnp.float32), b_sig.shape[1], factor
    ).astype(jnp.bfloat16)
    down_dino = (slope_dino * contract_cols(back_dino, b_dino)).astype(jnp.bfloat16)
    down_sig = (slope_sig * contract_cols(back_sig, b_sig)).astype(jnp.bfloat16)
    part = (contract_cols(down_dino, a_dino) + contract_cols(down_sig, a_sig)).astype(
        jnp.bfloat16
    )
    backs = jnp.concatenate(gather_back(part, stream, gain_out), axis=0)

    def blocks(grad):
        return grad.astype(jnp.bfloat16).reshape(n_chips, n_cores, -1, grad.shape[1])

    grad_b_d = blocks(contract_rows(back_dino, act_dino))
    grad_b_s = blocks(contract_rows(back_sig, act_sig))
    wide, narrow = grad_b_d.shape[3], grad_b_s.shape[3]
    cut = grad_b_d.shape[2]
    grad_b = jnp.concatenate(
        [grad_b_d, jnp.pad(grad_b_s, ((0, 0), (0, 0), (0, 0), (0, wide - narrow)))], axis=2
    )
    grad_b = ring_sum(core_sum(grad_b), "dp")
    out_b_d = grad_b[:cut].T
    out_b_s = grad_b[cut:, :narrow].T
    grad_a = jnp.concatenate(
        [contract_rows(summary, down_dino), contract_rows(summary, down_sig)], axis=1
    )
    grad_a = ring_sum(core_sum(blocks(grad_a)), "dp")
    out_a_d = grad_a[:, : down_dino.shape[1]]
    out_a_s = grad_a[:, down_dino.shape[1] :]

    others = jnp.concatenate(all_normed[1:], axis=0)
    other_hidden, other_slope = gelu_and_slope(matmul(others, w_in))
    normeds = jnp.concatenate([normed, others], axis=0)
    hiddens = jnp.concatenate([hidden, other_hidden], axis=0)
    slopes = jnp.concatenate([slope, other_slope], axis=0)
    back_hidden = (slopes * contract_cols(backs, w_out)).astype(jnp.bfloat16)
    share = width // (n_chips * n_cores)

    def shares(values):
        at = chip * n_cores + core
        own = lax.dynamic_slice_in_dim(values, at * share, share, 1)
        peer = chip * n_cores + (1 - core)
        return own, lax.dynamic_slice_in_dim(values, peer * share, share, 1)

    own_n, peer_n = shares(normeds)
    own_s, peer_s = shares(backs)
    sent_out = contract_rows(hiddens, peer_s).astype(jnp.bfloat16)
    got_out = shift(sent_out, "teach")
    sent_in = contract_rows(peer_n, back_hidden).astype(jnp.bfloat16)
    got_in = shift(sent_in, "teach")
    out_wo = contract_rows(hiddens, own_s) + got_out.astype(jnp.float32)
    out_wi = contract_rows(own_n, back_hidden) + got_in.astype(jnp.float32)
    return out_wi, out_wo, out_a_d, out_b_d, out_a_s, out_b_s


def solution(mesh):
    placed = (
        P(("groups", "dp", "teach"), None, None),
        P(),
        P(),
        P(None, "mp"),
        P("mp", None),
        P(None, "mp"),
        P("mp", None),
        P(None, "mp"),
        P("mp", None),
        P("groups", ("dp", "teach"), "mp"),
        P("groups", ("dp", "teach"), "mp"),
        P("groups"),
    )
    return jax.shard_map(
        per_device,
        mesh=mesh,
        in_specs=placed,
        out_specs=(
            P(("groups", "dp", "teach"), "mp"),
            P(("groups", "mp"), ("dp", "teach")),
            P(("groups", "dp", "teach"), "mp"),
            P(("groups", "mp"), ("dp", "teach")),
            P(("groups", "dp", "teach"), "mp"),
            P(("groups", "mp"), ("dp", "teach")),
        ),
        check_vma=False,
    )
```

time: 467 us -> 268 us (0.57)
  waiting for transfers between devices: 329 us -> 135 us
  blocking collectives: 22.5 us -> 0 us
  starting transfers between devices: 8.7 us -> 28.7 us
  between operations: 14.5 us -> 1.37 us
  matrix products: 50.5 us -> 62.2 us
    reduce_scatter x8 -> x0, waiting for transfers between devices: 262 us -> none  [the longest x1 71.9 us: per_device(): lax.psum_scatter(grad_wi.astype(jnp.bfloat16), ('dp', 'teach'), scatter_d...]
    ppermute x0 -> x26, waiting for transfers between devices: none -> 113 us  [shift(): lax.ppermute(values, axis, [(i, (i + 1) % count) for i in range(count)])]
    psum x2 -> x0, waiting for transfers between devices: 50.7 us -> none  [the longest x1 33.6 us: per_device(): lax.psum(jnp.dot(hidden, w_out, preferred_element_type=jnp.float32).astyp...]
    ppermute x0 -> x26, starting transfers between devices: none -> 20.4 us  [shift(): lax.ppermute(values, axis, [(i, (i + 1) % count) for i in range(count)])]
    all_gather x2 -> x0, blocking collectives: 17.5 us -> none  [the longest x1 9.44 us: per_device(): lax.all_gather(back_dino, 'mp', axis=1, tiled=True)]
    dot_general x4 -> x5, matrix products: 4.11 us -> 17.9 us  [contract_cols(): lax.dot_general(left, right, (((1,), (1,)), ((), ())), preferred_element_...]
    dot_general x6 -> x8, matrix products: 31.7 us -> 18.1 us  [contract_rows(): lax.dot_general(left, right, (((0,), (0,)), ((), ())), preferred_element_...]
    dot_general x6 -> x7, matrix products: 14.7 us -> 26.2 us  [matmul(): return jnp.dot(left, right, preferred_element_type=jnp.float32)]
  transfers between devices with their start and end apart: 12 -> 28, of which waited for: 10 -> 13; matrix products, arithmetic and copies ran while one was open for 13% -> 31% of each run, Pallas kernels for 0% -> 0%
where the time goes in v1:
time: 268 us; the launch traced here: 267 us
  waiting for transfers between devices  135 us (50%)
  matrix products  62.2 us (23%)
  starting transfers between devices  28.7 us (11%)
  other arithmetic  22.9 us (9%)
  local copies, waits for them, and re-layouts  17.4 us (6%)
    ppermute x26, waiting for transfers between devices, shift(): lax.ppermute(values, axis, [(i, (i + 1) % count) for i in range(count)])  113 us
    dot_general x7, matrix products, matmul(): return jnp.dot(left, right, preferred_element_type=jnp.float32)  26.2 us
    all_to_all x2, waiting for transfers between devices, own_teacher(): lax.all_to_all(sent, ('dp', 'teach'), split_axis=0, concat_axis=1, tiled=...  21.9 us
    ppermute x26, starting transfers between devices, shift(): lax.ppermute(values, axis, [(i, (i + 1) % count) for i in range(count)])  20.4 us
    dot_general x8, matrix products, contract_rows(): lax.dot_general(left, right, (((0,), (0,)), ((), ())), preferred_element_...  18.1 us
    dot_general x5, matrix products, contract_cols(): lax.dot_general(left, right, (((1,), (1,)), ((), ())), preferred_element_...  17.9 us
    all_to_all x2, starting transfers between devices, own_teacher(): lax.all_to_all(sent, ('dp', 'teach'), split_axis=0, concat_axis=1, tiled=...  8.33 us
  transfers between devices with their start and end apart: 28, of which 13 were waited for; matrix products, arithmetic and copies ran while one was open for 31% of the time, Pallas kernels for 0%

profile of v1, /device:TPU:0, one launch (start us, length us, event | category | flops | bytes accessed | tf_op | source)
XLA Modules:
  0.0 267.4 jit_solution(9321098546850634815)
XLA Ops:
  0.6 1.4 convert_reduce_fusion
  2.1 1.4 fusion.26
  3.5 1.5 fusion.28
  5.0 7.2 %add_convert_fusion.1 = (bf16[256,2560]{1,0:T(8,128)(2,1)}, bf16[256,2560]{1,0:T(8,128)(2,1)S(1)}) fusion(bf16[256,1280]{1,0:T(8,128)(2,1)S(1)} %fusion.28, bf16[1280,2560]{1,0:T(8,128)(2,1)} %param.15), kind=kOutput, calls=%fused_computation.35 | convolution fusion | flops 1690173440 | bytes 9830400 | tf_op jit(solution)/shard_map/dot_general | solution.py:53
  12.3 2.7 %convolution_convert_fusion.7 = bf16[256,1280]{1,0:T(8,128)(2,1)} fusion(bf16[256,2560]{1,0:T(8,128)(2,1)S(1)} %get-tuple-element.19, bf16[2560,1280]{1,0:T(8,128)(2,1)S(1)} %bitcast.111), kind=kOutput, calls=%fused_computation.39 | convolution fusion | flops 1678049280 | bytes 8519680 | tf_op jit(solution)/shard_map/dot_general | solution.py:53
  15.0 2.9 %collective-permute-start.3 = (bf16[256,1280]{1,0:T(8,128)(2,1)}, bf16[256,1280]{1,0:T(8,128)(2,1)}, u32[]{:S(2)}, u32[]{:S(2)}) collective-permute-start(bf16[256,1280]{1,0:T(8,128)(2,1)} %convolution_convert_fusion.7), channel_id=1, source_target_pairs={{0,2},{2,0},{1,3},{3,1},{4,6},{6,4},{5,7},{7,5},{8,10},{10,8},{9,1... | collective-permute-start | bytes 1966088 | tf_op jit(solution)/shard_map/ppermute | solution.py:70
  18.6 1.3 gather_fusion.1
  19.9 4.9 %all-to-all-start.1 = ((bf16[8,32,576]{2,1,0:T(8,128)(2,1)}), bf16[8,32,576]{2,1,0:T(8,128)(2,1)S(1)}, u32[]{:S(2)}, u32[]{:S(2)}) async-start(bf16[8,32,576]{2,1,0:T(8,128)(2,1)} %gather_fusion.1), calls=%async_computation.1 | async-start | bytes 655360 | tf_op jit(solution)/shard_map/all_to_all | solution.py:128
  24.8 2.0 collective-permute-start
  26.8 2.3 gather_fusion
  29.1 20.9 %all-to-all-done.1 = bf16[8,32,576]{2,1,0:T(8,128)(2,1)S(1)} async-done(((bf16[8,32,576]{2,1,0:T(8,128)(2,1)}), bf16[8,32,576]{2,1,0:T(8,128)(2,1)S(1)}, u32[]{:S(2)}, u32[]{:S(2)}) %all-to-all-start.1) | async-done | bytes 294944 | tf_op jit(solution)/shard_map/all_to_all | solution.py:128
  50.7 3.5 %all-to-all-start = ((bf16[8,32,768]{2,1,0:T(8,128)(2,1)}), bf16[8,32,768]{2,1,0:T(8,128)(2,1)S(1)}, u32[]{:S(2)}, u32[]{:S(2)}) async-start(bf16[8,32,768]{2,1,0:T(8,128)(2,1)} %gather_fusion), calls=%async_computation | async-start | bytes 786432 | tf_op jit(solution)/shard_map/all_to_all | solution.py:128
  54.7 1.6 fusion.58
  56.9 1.4 copy-done.6
  59.1 1.7 convolution_convert_fusion.6
  60.8 1.5 collective-permute-start.4
  62.9 1.6 convolution_convert_fusion.8
  65.6 1.0 all-to-all-done
  67.1 1.7 collective-permute-start.1
  68.8 1.1 broadcast_select_fusion.3
  70.0 32.3 %collective-permute-done.5 = bf16[256,768]{1,0:T(8,128)(2,1)S(1)} collective-permute-done((bf16[256,768]{1,0:T(8,128)(2,1)S(1)}, bf16[256,768]{1,0:T(8,128)(2,1)S(1)}, u32[]{:S(2)}, u32[]{:S(2)}) %collective-permute-start.5) | collective-permute-done | bytes 393248 | tf_op jit(solution)/shard_map/ppermute | solution.py:70
  102.3 1.8 broadcast_select_fusion.1
  104.1 2.0 multiply_reduce_fusion.2
  106.1 1.9 fusion.33
  108.1 1.5 fusion.30
  109.5 1.7 convolution_convert_fusion.5
  111.3 2.6 copy.25
  113.9 2.6 convolution_convert_fusion.4
  116.5 2.6 copy.22
  119.1 2.3 fusion.62
  121.4 1.7 collective-permute-start.2
  123.1 2.0 multiply_reduce_fusion
  125.1 2.7 %fusion.29 = bf16[256,768]{1,0:T(8,128)(2,1)S(1)} fusion(bf16[768,1536]{1,0:T(8,128)(2,1)S(1)} %copy-done, f32[256,768]{1,0:T(8,128)S(1)} %copy-done.16, bf16[256,1536]{1,0:T(8,128)(2,1)} %collective-permute-done.4, bf16[256,1536]{1,0:T(8,128)(2,1)} %convolution_convert_fusion.6, f32[256]{0:T(256)S(1)} %get-tuple-element.25, f32[256]{0:T(256)S(1)} %get-tuple-element.24, ...), kind=kOutput, calls=%fused_computation.78 | convolution fusion | flops 613810176 | bytes 5900288 | tf_op jit(solution)/shard_map/dot_general | solution.py:63
  127.9 0.7 convolution_convert_fusion.2
  128.6 0.8 copy-done.7
  130.2 0.9 collective-permute-start.8
  131.1 3.0 %convolution_convert_fusion.3 = bf16[1536,768]{1,0:T(8,128)(2,1)S(1)} fusion(f32[256,768]{1,0:T(8,128)S(1)} %copy-done.16, bf16[256,1536]{1,0:T(8,128)(2,1)} %collective-permute-done.4, bf16[256,1536]{1,0:T(8,128)(2,1)} %convolution_convert_fusion.6, f32[256]{0:T(256)S(1)} %get-tuple-element.25, f32[256]{0:T(256)S(1)} %get-tuple-element.24, ...), kind=kOutput, calls=%fused_computation.25 | convolution fusion | flops 612827136 | bytes 5507072 | tf_op jit(solution)/shard_map/dot_general | solution.py:57
  134.8 1.4 copy-done.4
  136.2 1.4 fusion.12
  137.5 1.6 collective-permute-done.8
  140.2 1.5 collective-permute-start.10
  141.7 11.8 %multiply_convert_fusion.1 = (bf16[768,2560]{1,0:T(8,128)(2,1)S(1)}, bf16[768,2560]{1,0:T(8,128)(2,1)}) fusion(bf16[1280,2560]{1,0:T(8,128)(2,1)S(1)} %bitcast.109, bf16[256,1280]{1,0:T(8,128)(2,1)S(1)} %collective-permute-done.2, bf16[256,1280]{1,0:T(8,128)(2,1)} %collective-permute-done.1, bf16[256,1280]{1,0:T(8,128)(2,1)} %collective-permute-done), kind=kOutput, calls=%fused_computation.6 | convolution fusion | flops 5076418560 | bytes 16384000 | tf_op jit(solution)/shard_map/dot_general | solution.py:53
  153.5 2.4 pad_maximum_fusion.3
  155.8 1.7 collective-permute-start.11
  157.6 1.5 collective-permute-start.12
  159.2 7.9 %collective-permute-done.12 = bf16[128,1280]{1,0:T(8,128)(2,1)S(1)} collective-permute-done((bf16[128,1280]{1,0:T(8,128)(2,1)S(1)}, bf16[128,1280]{1,0:T(8,128)(2,1)S(1)}, u32[]{:S(2)}, u32[]{:S(2)}) %collective-permute-start.12) | collective-permute-done | bytes 327712 | tf_op jit(solution)/shard_map/ppermute | solution.py:70
  167.1 1.2 collective-permute-start.13
  168.5 9.0 %collective-permute-done.14 = bf16[128,1280]{1,0:T(8,128)(2,1)S(1)} collective-permute-done((bf16[128,1280]{1,0:T(8,128)(2,1)S(1)}, bf16[128,1280]{1,0:T(8,128)(2,1)S(1)}, u32[]{:S(2)}, u32[]{:S(2)}) %collective-permute-start.14) | collective-permute-done | bytes 327712 | tf_op jit(solution)/shard_map/ppermute | solution.py:70
  178.2 6.4 %collective-permute-done.15 = bf16[128,1280]{1,0:T(8,128)(2,1)S(1)} collective-permute-done((bf16[128,1280]{1,0:T(8,128)(2,1)S(1)}, bf16[128,1280]{1,0:T(8,128)(2,1)S(1)}, u32[]{:S(2)}, u32[]{:S(2)}) %collective-permute-start.15) | collective-permute-done | bytes 327712 | tf_op jit(solution)/shard_map/ppermute | solution.py:70
  184.8 2.6 convolution_convert_fusion
  187.3 10.7 %multiply_convert_fusion = bf16[1024,2560]{1,0:T(8,128)(2,1)S(1)} fusion(bf16[1024,1280]{1,0:T(8,128)(2,1)} %copy-done.21, bf16[2560,1280]{1,0:T(8,128)(2,1)} %param.16, bf16[768,2560]{1,0:T(8,128)(2,1)} %get-tuple-element.17, bf16[256,2560]{1,0:T(8,128)(2,1)} %get-tuple-element.18), kind=kOutput, calls=%fused_computation.3 | convolution fusion | flops 6726615040 | bytes 19660800 | tf_op jit(solution)/shard_map/dot_general | solution.py:63
  199.4 1.1 convolution_convert_fusion.1
  201.1 12.5 %collective-permute-done.19 = bf16[160,1344]{1,0:T(8,128)(2,1)S(1)} collective-permute-done((bf16[160,1344]{1,0:T(8,128)(2,1)S(1)}, bf16[160,1344]{1,0:T(8,128)(2,1)S(1)}, u32[]{:S(2)}, u32[]{:S(2)}) %collective-permute-start.19) | collective-permute-done | bytes 430112 | tf_op jit(solution)/shard_map/ppermute | solution.py:70
  213.8 10.9 %collective-permute-done.23 = bf16[336,768]{1,0:T(8,128)(2,1)S(1)} collective-permute-done((bf16[336,768]{1,0:T(8,128)(2,1)S(1)}, bf16[336,768]{1,0:T(8,128)(2,1)S(1)}, u32[]{:S(2)}, u32[]{:S(2)}) %collective-permute-start.23) | collective-permute-done | bytes 516128 | tf_op jit(solution)/shard_map/ppermute | solution.py:70
  224.9 4.0 %convolution_add_fusion = f32[2560,160]{0,1:T(8,128)} fusion(bf16[768,2560]{1,0:T(8,128)(2,1)S(1)} %copy-done.26, bf16[256,2560]{1,0:T(8,128)(2,1)S(1)} %copy-done.29, bf16[2560,160]{0,1:T(8,128)(2,1)} %collective-permute-done.17, bf16[1024,1280]{1,0:T(8,128)(2,1)} %copy-done.21, s32[]{:T(128)S(6)} %select_n.110), kind=kOutput, calls=%fused_computation.18 | convolution fusion | flops 850165760 | bytes 8224772 | tf_op jit(solution)/shard_map/dot_general | solution.py:57
  228.8 5.5 %collective-permute-done.20 = bf16[160,1344]{1,0:T(8,128)(2,1)S(1)} collective-permute-done((bf16[160,1344]{1,0:T(8,128)(2,1)S(1)}, bf16[160,1344]{1,0:T(8,128)(2,1)S(1)}, u32[]{:S(2)}, u32[]{:S(2)}) %collective-permute-start.20) | collective-permute-done | bytes 430112 | tf_op jit(solution)/shard_map/ppermute | solution.py:70
  234.5 10.9 %collective-permute-done.24 = bf16[336,768]{1,0:T(8,128)(2,1)S(1)} collective-permute-done((bf16[336,768]{1,0:T(8,128)(2,1)S(1)}, bf16[336,768]{1,0:T(8,128)(2,1)S(1)}, u32[]{:S(2)}, u32[]{:S(2)}) %collective-permute-start.24) | collective-permute-done | bytes 516128 | tf_op jit(solution)/shard_map/ppermute | solution.py:70
  245.6 2.3 convolution_add_fusion.1
  247.9 7.1 %collective-permute-done.21 = bf16[160,1344]{1,0:T(8,128)(2,1)S(1)} collective-permute-done((bf16[160,1344]{1,0:T(8,128)(2,1)S(1)}, bf16[160,1344]{1,0:T(8,128)(2,1)S(1)}, u32[]{:S(2)}, u32[]{:S(2)}) %collective-permute-start.21) | collective-permute-done | bytes 430112 | tf_op jit(solution)/shard_map/ppermute | solution.py:70
  255.1 0.8 slice.20
  255.9 0.8 slice.22
  256.7 9.0 %collective-permute-done.25 = bf16[336,768]{1,0:T(8,128)(2,1)S(1)} collective-permute-done((bf16[336,768]{1,0:T(8,128)(2,1)S(1)}, bf16[336,768]{1,0:T(8,128)(2,1)S(1)}, u32[]{:S(2)}, u32[]{:S(2)}) %collective-permute-start.25) | collective-permute-done | bytes 516128 | tf_op jit(solution)/shard_map/ppermute | solution.py:70
  265.8 0.9 slice_bitcast_fusion
  266.7 0.8 slice_bitcast_fusion.1
  (142 shorter events, 11.9 us)
Async XLA Ops:
  0.6 58.4 %copy-start = (bf16[768,1536]{1,0:T(8,128)(2,1)S(1)}, bf16[768,1536]{1,0:T(8,128)(2,1)}, u32[]{:S(2)}) copy-start(bf16[768,1536]{1,0:T(8,128)(2,1)} %param.18) | copy-start | bytes 7077892
  3.5 8.8 %slice-start.2 = ((s8[6553600]{0:T(1024)(128)(4,1)}), s8[4194304]{0:T(1024)(128)(4,1)S(1)}, s32[]{:S(2)}) async-start(s8[6553600]{0:T(1024)(128)(4,1)} %bitcast.110), calls=%async_computation.4 | async-start | bytes 8388608
  5.0 7.2 %copy-start.10 = (bf16[256,1280]{1,0:T(8,128)(2,1)}, bf16[256,1280]{1,0:T(8,128)(2,1)S(1)}, u32[]{:S(2)}) copy-start(bf16[256,1280]{1,0:T(8,128)(2,1)S(1)} %fusion.28) | copy-start | bytes 1966084
  5.0 7.2 %slice-start.3 = ((s8[6553600]{0:T(1024)(128)(4,1)}), s8[2359296]{0:T(1024)(128)(4,1)S(1)}, s32[]{:S(2)}) async-start(s8[6553600]{0:T(1024)(128)(4,1)} %bitcast.110), calls=%async_computation.5 | async-start | bytes 4718592
  12.2 2.7 %copy-start.27 = (bf16[256,2560]{1,0:T(8,128)(2,1)}, bf16[256,2560]{1,0:T(8,128)(2,1)S(1)}, u32[]{:S(2)}) copy-start(bf16[256,2560]{1,0:T(8,128)(2,1)S(1)} %get-tuple-element.19) | copy-start | bytes 3932164
  12.3 5.7 %copy-start.24 = (s32[8]{0:T(128)S(1)}, s32[8]{0:T(128)}, u32[]{:S(2)}) copy-start(s32[8]{0:T(128)} %param.23) | copy-start | bytes 100
  12.3 6.3 %copy-start.19 = (bf16[8,32,576]{2,1,0:T(8,128)(2,1)S(1)}, bf16[8,32,576]{2,1,0:T(8,128)(2,1)}, u32[]{:S(2)}) copy-start(bf16[8,32,576]{2,1,0:T(8,128)(2,1)} %param.22) | copy-start | bytes 884740
  15.0 39.8 %copy-start.5 = (bf16[1,256,1280]{2,1,0:T(8,128)(2,1)S(1)}, bf16[1,256,1280]{2,1,0:T(8,128)(2,1)}, u32[]{:S(2)}) copy-start(bf16[1,256,1280]{2,1,0:T(8,128)(2,1)} %param.12) | copy-start | bytes 1966084
  15.0 39.7 %collective-permute-start.3 = (bf16[256,1280]{1,0:T(8,128)(2,1)}, bf16[256,1280]{1,0:T(8,128)(2,1)}, u32[]{:S(2)}, u32[]{:S(2)}) collective-permute-start(bf16[256,1280]{1,0:T(8,128)(2,1)} %convolution_convert_fusion.7), channel_id=1, source_target_pairs={{0,2},{2,0},{1,3},{3,1},{4,6},{6,4},{5,7},{7,5},{8,10},{10,8},{9,1... | collective-permute-start | bytes 1966088 | tf_op jit(solution)/shard_map/ppermute | solution.py:70
  19.9 30.1 %all-to-all-start.1 = ((bf16[8,32,576]{2,1,0:T(8,128)(2,1)}), bf16[8,32,576]{2,1,0:T(8,128)(2,1)S(1)}, u32[]{:S(2)}, u32[]{:S(2)}) async-start(bf16[8,32,576]{2,1,0:T(8,128)(2,1)} %gather_fusion.1), calls=%async_computation.1 | async-start | bytes 655360 | tf_op jit(solution)/shard_map/all_to_all | solution.py:128
  24.8 42.4 %collective-permute-start = (bf16[256,1280]{1,0:T(8,128)(2,1)}, bf16[256,1280]{1,0:T(8,128)(2,1)}, u32[]{:S(2)}, u32[]{:S(2)}) collective-permute-start(bf16[256,1280]{1,0:T(8,128)(2,1)} %copy-done.10), channel_id=1, source_target_pairs={{0,4},{4,8},{8,12},{12,0},{1,5},{5,9},{9,13},{13,1},{2,6},{6,10},{... | collective-permute-start | bytes 1966088 | tf_op jit(solution)/shard_map/ppermute | solution.py:70
  49.9 0.7 copy-start.14
  50.7 15.9 %all-to-all-start = ((bf16[8,32,768]{2,1,0:T(8,128)(2,1)}), bf16[8,32,768]{2,1,0:T(8,128)(2,1)S(1)}, u32[]{:S(2)}, u32[]{:S(2)}) async-start(bf16[8,32,768]{2,1,0:T(8,128)(2,1)} %gather_fusion), calls=%async_computation | async-start | bytes 786432 | tf_op jit(solution)/shard_map/all_to_all | solution.py:128
  54.1 2.5 copy-start.20
  54.1 14.7 %collective-permute-start.7 = (bf16[256,576]{1,0:T(8,128)(2,1)}, bf16[256,576]{1,0:T(8,128)(2,1)}, u32[]{:S(2)}, u32[]{:S(2)}) collective-permute-start(bf16[256,576]{1,0:T(8,128)(2,1)} %bitcast.107), channel_id=1, source_target_pairs={{0,2},{2,0},{1,3},{3,1},{4,6},{6,4},{5,7},{7,5},{8,10},{10,8},{9,1... | collective-permute-start | bytes 884744 | tf_op jit(solution)/shard_map/ppermute | solution.py:70
  56.4 9.0 %copy-start.2 = (f32[256,1280]{1,0:T(8,128)}, f32[256,1280]{1,0:T(8,128)S(1)}, u32[]{:S(2)}) copy-start(f32[256,1280]{1,0:T(8,128)S(1)} %get-tuple-element.15) | copy-start | bytes 3932164
  56.4 2.0 copy-start.6
  59.1 1.7 copy-start.15
  59.1 3.2 %copy-start.8 = (bf16[1280,576]{0,1:T(8,128)(2,1)S(1)}, bf16[1280,576]{0,1:T(8,128)(2,1)}, u32[]{:S(2)}) copy-start(bf16[1280,576]{0,1:T(8,128)(2,1)} %param.19) | copy-start | bytes 4423684
  60.8 2.1 copy-start.22
  60.8 62.3 %collective-permute-start.4 = (bf16[256,1536]{1,0:T(8,128)(2,1)}, bf16[256,1536]{1,0:T(8,128)(2,1)}, u32[]{:S(2)}, u32[]{:S(2)}) collective-permute-start(bf16[256,1536]{1,0:T(8,128)(2,1)} %convolution_convert_fusion.6), channel_id=1, source_target_pairs={{0,2},{2,0},{1,3},{3,1},{4,6},{6,4},{5,7},{7,5},{8,10},{10,8},{9,1... | collective-permute-start | bytes 2359304 | tf_op jit(solution)/shard_map/ppermute | solution.py:70
  62.9 2.4 copy-start.17
  64.5 39.6 %collective-permute-start.6 = (bf16[256,1152]{1,0:T(8,128)(2,1)}, bf16[256,1152]{1,0:T(8,128)(2,1)}, u32[]{:S(2)}, u32[]{:S(2)}) collective-permute-start(bf16[256,1152]{1,0:T(8,128)(2,1)} %convolution_convert_fusion.8), channel_id=1, source_target_pairs={{0,2},{2,0},{1,3},{3,1},{4,6},{6,4},{5,7},{7,5},{8,10},{10,8},{9,1... | collective-permute-start | bytes 1769480 | tf_op jit(solution)/shard_map/ppermute | solution.py:70
  66.6 3.4 %copy-start.13 = (bf16[8,32,768]{2,1,0:T(8,128)(2,1)}, bf16[8,32,768]{2,1,0:T(8,128)(2,1)S(1)}, u32[]{:S(2)}) copy-start(bf16[8,32,768]{2,1,0:T(8,128)(2,1)S(1)} %all-to-all-done) | copy-start | bytes 1179652
  66.6 35.7 %collective-permute-start.5 = (bf16[256,768]{1,0:T(8,128)(2,1)S(1)}, bf16[256,768]{1,0:T(8,128)(2,1)S(1)}, u32[]{:S(2)}, u32[]{:S(2)}) collective-permute-start(bf16[256,768]{1,0:T(8,128)(2,1)S(1)} %bitcast.106), channel_id=1, source_target_pairs={{0,2},{2,0},{1,3},{3,1},{4,6},{6,4},{5,7},{7,5},{8,10},{10,8},{9,1... | collective-permute-start | bytes 1179656 | tf_op jit(solution)/shard_map/ppermute | solution.py:70
  67.1 54.3 %collective-permute-start.1 = (bf16[256,1280]{1,0:T(8,128)(2,1)}, bf16[256,1280]{1,0:T(8,128)(2,1)}, u32[]{:S(2)}, u32[]{:S(2)}) collective-permute-start(bf16[256,1280]{1,0:T(8,128)(2,1)} %collective-permute-done), channel_id=1, source_target_pairs={{0,4},{4,8},{8,12},{12,0},{1,5},{5,9},{9,13},{13,1},{2,6},{6,10},{... | collective-permute-start | bytes 1966088 | tf_op jit(solution)/shard_map/ppermute | solution.py:70
  104.1 4.0 %copy-start.18 = (f32[256,576]{0,1:T(8,128)S(1)}, f32[256,576]{0,1:T(8,128)}, u32[]{:S(2)}) copy-start(f32[256,576]{0,1:T(8,128)} %copy-done.17) | copy-start | bytes 1769476
  104.1 4.0 %copy-start.23 = (bf16[576,1152]{1,0:T(8,128)(2,1)S(1)}, bf16[576,1152]{1,0:T(8,128)(2,1)}, u32[]{:S(2)}) copy-start(bf16[576,1152]{1,0:T(8,128)(2,1)} %param.20) | copy-start | bytes 3981316
  119.1 4.0 %copy-start.12 = (bf16[256,768]{1,0:T(8,128)(2,1)S(1)}, bf16[256,768]{1,0:T(8,128)(2,1)}, u32[]{:S(2)}) copy-start(bf16[256,768]{1,0:T(8,128)(2,1)} %get-tuple-element.21) | copy-start | bytes 1179652
  119.1 6.0 %copy-start.16 = (f32[256,768]{1,0:T(8,128)S(1)}, f32[256,768]{1,0:T(8,128)}, u32[]{:S(2)}) copy-start(f32[256,768]{1,0:T(8,128)} %copy-done.15) | copy-start | bytes 2359300
  121.4 20.2 %collective-permute-start.2 = (bf16[256,1280]{1,0:T(8,128)(2,1)}, bf16[256,1280]{1,0:T(8,128)(2,1)S(1)}, u32[]{:S(2)}, u32[]{:S(2)}) collective-permute-start(bf16[256,1280]{1,0:T(8,128)(2,1)} %collective-permute-done.1), channel_id=1, source_target_pairs={{0,4},{4,8},{8,12},{12,0},{1,5},{5,9},{9,13},{13,1},{2,6},{6,10},{... | collective-permute-start | bytes 1966088 | tf_op jit(solution)/shard_map/ppermute | solution.py:70
  127.9 1.5 copy-start.7
  130.2 4.0 %copy-start.9 = (bf16[1152,576]{1,0:T(8,128)(2,1)S(1)}, bf16[1152,576]{1,0:T(8,128)(2,1)}, u32[]{:S(2)}) copy-start(bf16[1152,576]{1,0:T(8,128)(2,1)} %copy.25) | copy-start | bytes 3981316
  130.2 8.9 %collective-permute-start.8 = (bf16[128,1280]{1,0:T(8,128)(2,1)S(1)}, bf16[128,1280]{1,0:T(8,128)(2,1)S(1)}, u32[]{:S(2)}, u32[]{:S(2)}) collective-permute-start(bf16[128,1280]{1,0:T(8,128)(2,1)S(1)} %constant_dynamic-slice_fusion), channel_id=1, source_target_pairs={{0,2},{2,0},{1,3},{3,1},{4,6},{6,4},{5,7},{7,5},{8,10},{10,8},{9,1... | collective-permute-start | bytes 983048 | tf_op jit(solution)/shard_map/ppermute | solution.py:70
  131.1 10.6 %slice-start = ((s8[6553600]{0:T(1024)(128)(4,1)}), s8[4194304]{0:T(1024)(128)(4,1)S(1)}, s32[]{:S(2)}) async-start(s8[6553600]{0:T(1024)(128)(4,1)} %bitcast.108), calls=%async_computation.2 | async-start | bytes 8388608
  134.2 7.5 %slice-start.1 = ((s8[6553600]{0:T(1024)(128)(4,1)}), s8[2359296]{0:T(1024)(128)(4,1)S(1)}, s32[]{:S(2)}) async-start(s8[6553600]{0:T(1024)(128)(4,1)} %bitcast.108), calls=%async_computation.3 | async-start | bytes 4718592
  134.5 1.6 copy-start.4
  134.7 64.0 %collective-permute-start.22 = (bf16[4,336,768]{2,1,0:T(8,128)(2,1)S(1)}, bf16[4,336,768]{2,1,0:T(8,128)(2,1)S(1)}, u32[]{:S(2)}, u32[]{:S(2)}) collective-permute-start(bf16[4,336,768]{2,1,0:T(8,128)(2,1)S(1)} %dynamic-slice_bitcast_fusion), channel_id=1, source_target_pairs={{0,1},{1,0},{2,3},{3,2},{4,5},{5,4},{6,7},{7,6},{8,9},{9,8},{10,11... | collective-permute-start | bytes 6193160 | tf_op jit(solution)/shard_map/ppermute | solution.py:70
  136.2 2.9 %copy-start.3 = (f32[256,1280]{1,0:T(8,128)S(1)}, f32[256,1280]{1,0:T(8,128)}, u32[]{:S(2)}) copy-start(f32[256,1280]{1,0:T(8,128)} %copy-done.2) | copy-start | bytes 3932164
  137.5 60.5 %collective-permute-start.18 = (bf16[4,160,1344]{2,1,0:T(8,128)(2,1)}, bf16[4,160,1344]{2,1,0:T(8,128)(2,1)S(1)}, u32[]{:S(2)}, u32[]{:S(2)}) collective-permute-start(bf16[4,160,1344]{2,1,0:T(8,128)(2,1)} %fusion.12), channel_id=1, source_target_pairs={{0,1},{1,0},{2,3},{3,2},{4,5},{5,4},{6,7},{7,6},{8,9},{9,8},{10,11... | collective-permute-start | bytes 5160968 | tf_op jit(solution)/shard_map/ppermute | solution.py:70
  139.8 13.7 %copy-start.11 = (bf16[256,1280]{1,0:T(8,128)(2,1)S(1)}, bf16[256,1280]{1,0:T(8,128)(2,1)}, u32[]{:S(2)}) copy-start(bf16[256,1280]{1,0:T(8,128)(2,1)} %copy-done.10) | copy-start | bytes 1966084
  139.8 19.3 %collective-permute-start.9 = (bf16[128,1280]{1,0:T(8,128)(2,1)S(1)}, bf16[128,1280]{1,0:T(8,128)(2,1)S(1)}, u32[]{:S(2)}, u32[]{:S(2)}) collective-permute-start(bf16[128,1280]{1,0:T(8,128)(2,1)S(1)} %multiply_convert_fusion.5), channel_id=1, source_target_pairs={{0,2},{2,0},{1,3},{3,1},{4,6},{6,4},{5,7},{7,5},{8,10},{10,8},{9,1... | collective-permute-start | bytes 983048 | tf_op jit(solution)/shard_map/ppermute | solution.py:70
  140.2 15.7 %collective-permute-start.10 = (bf16[128,1280]{1,0:T(8,128)(2,1)S(1)}, bf16[128,1280]{1,0:T(8,128)(2,1)S(1)}, u32[]{:S(2)}, u32[]{:S(2)}) collective-permute-start(bf16[128,1280]{1,0:T(8,128)(2,1)S(1)} %multiply_convert_fusion.5), channel_id=1, source_target_pairs={{0,4},{4,8},{8,12},{12,0},{1,5},{5,9},{9,13},{13,1},{2,6},{6,10},{... | collective-permute-start | bytes 983048 | tf_op jit(solution)/shard_map/ppermute | solution.py:70
  153.5 31.3 %copy-start.25 = (bf16[768,2560]{1,0:T(8,128)(2,1)}, bf16[768,2560]{1,0:T(8,128)(2,1)S(1)}, u32[]{:S(2)}) copy-start(bf16[768,2560]{1,0:T(8,128)(2,1)S(1)} %get-tuple-element.16) | copy-start | bytes 11796484
  155.8 12.5 %collective-permute-start.11 = (bf16[128,1280]{1,0:T(8,128)(2,1)S(1)}, bf16[128,1280]{1,0:T(8,128)(2,1)S(1)}, u32[]{:S(2)}, u32[]{:S(2)}) collective-permute-start(bf16[128,1280]{1,0:T(8,128)(2,1)S(1)} %collective-permute-done.10), channel_id=1, source_target_pairs={{0,2},{2,0},{1,3},{3,1},{4,6},{6,4},{5,7},{7,5},{8,10},{10,8},{9,1... | collective-permute-start | bytes 983048 | tf_op jit(solution)/shard_map/ppermute | solution.py:70
  157.6 9.5 %collective-permute-start.12 = (bf16[128,1280]{1,0:T(8,128)(2,1)S(1)}, bf16[128,1280]{1,0:T(8,128)(2,1)S(1)}, u32[]{:S(2)}, u32[]{:S(2)}) collective-permute-start(bf16[128,1280]{1,0:T(8,128)(2,1)S(1)} %collective-permute-done.10), channel_id=1, source_target_pairs={{0,4},{4,8},{8,12},{12,0},{1,5},{5,9},{9,13},{13,1},{2,6},{6,10},{... | collective-permute-start | bytes 983048 | tf_op jit(solution)/shard_map/ppermute | solution.py:70
  167.1 10.9 %collective-permute-start.13 = (bf16[128,1280]{1,0:T(8,128)(2,1)S(1)}, bf16[128,1280]{1,0:T(8,128)(2,1)S(1)}, u32[]{:S(2)}, u32[]{:S(2)}) collective-permute-start(bf16[128,1280]{1,0:T(8,128)(2,1)S(1)} %collective-permute-done.12), channel_id=1, source_target_pairs={{0,2},{2,0},{1,3},{3,1},{4,6},{6,4},{5,7},{7,5},{8,10},{10,8},{9,1... | collective-permute-start | bytes 983048 | tf_op jit(solution)/shard_map/ppermute | solution.py:70
  168.3 9.2 %collective-permute-start.14 = (bf16[128,1280]{1,0:T(8,128)(2,1)S(1)}, bf16[128,1280]{1,0:T(8,128)(2,1)S(1)}, u32[]{:S(2)}, u32[]{:S(2)}) collective-permute-start(bf16[128,1280]{1,0:T(8,128)(2,1)S(1)} %collective-permute-done.12), channel_id=1, source_target_pairs={{0,4},{4,8},{8,12},{12,0},{1,5},{5,9},{9,13},{13,1},{2,6},{6,10},{... | collective-permute-start | bytes 983048 | tf_op jit(solution)/shard_map/ppermute | solution.py:70
  168.5 16.3 %copy-start.28 = (bf16[256,2560]{1,0:T(8,128)(2,1)S(1)}, bf16[256,2560]{1,0:T(8,128)(2,1)}, u32[]{:S(2)}) copy-start(bf16[256,2560]{1,0:T(8,128)(2,1)} %copy-done.27) | copy-start | bytes 3932164
  177.5 7.1 %collective-permute-start.15 = (bf16[128,1280]{1,0:T(8,128)(2,1)S(1)}, bf16[128,1280]{1,0:T(8,128)(2,1)S(1)}, u32[]{:S(2)}, u32[]{:S(2)}) collective-permute-start(bf16[128,1280]{1,0:T(8,128)(2,1)S(1)} %collective-permute-done.14), channel_id=1, source_target_pairs={{0,2},{2,0},{1,3},{3,1},{4,6},{6,4},{5,7},{7,5},{8,10},{10,8},{9,1... | collective-permute-start | bytes 983048 | tf_op jit(solution)/shard_map/ppermute | solution.py:70
  184.7 2.6 copy-start.21
  187.3 37.5 %collective-permute-start.17 = (bf16[2560,160]{0,1:T(8,128)(2,1)}, bf16[2560,160]{0,1:T(8,128)(2,1)}, u32[]{:S(2)}, u32[]{:S(2)}) collective-permute-start(bf16[2560,160]{0,1:T(8,128)(2,1)} %convolution_convert_fusion), channel_id=1, source_target_pairs={{0,1},{1,0},{2,3},{3,2},{4,5},{5,4},{6,7},{7,6},{8,9},{9,8},{10,11... | collective-permute-start | bytes 2457608 | tf_op jit(solution)/shard_map/ppermute | solution.py:70
  198.6 15.0 %collective-permute-start.19 = (bf16[160,1344]{1,0:T(8,128)(2,1)S(1)}, bf16[160,1344]{1,0:T(8,128)(2,1)S(1)}, u32[]{:S(2)}, u32[]{:S(2)}) collective-permute-start(bf16[160,1344]{1,0:T(8,128)(2,1)S(1)} %dynamic-slice_bitcast_fusion.2), channel_id=1, source_target_pairs={{0,4},{4,8},{8,12},{12,0},{1,5},{5,9},{9,13},{13,1},{2,6},{6,10},{... | collective-permute-start | bytes 1290248 | tf_op jit(solution)/shard_map/ppermute | solution.py:70
  199.3 25.3 %collective-permute-start.23 = (bf16[336,768]{1,0:T(8,128)(2,1)S(1)}, bf16[336,768]{1,0:T(8,128)(2,1)S(1)}, u32[]{:S(2)}, u32[]{:S(2)}) collective-permute-start(bf16[336,768]{1,0:T(8,128)(2,1)S(1)} %dynamic-slice_bitcast_fusion.1), channel_id=1, source_target_pairs={{0,4},{4,8},{8,12},{12,0},{1,5},{5,9},{9,13},{13,1},{2,6},{6,10},{... | collective-permute-start | bytes 1548296 | tf_op jit(solution)/shard_map/ppermute | solution.py:70
  199.4 25.5 %copy-start.26 = (bf16[768,2560]{1,0:T(8,128)(2,1)S(1)}, bf16[768,2560]{1,0:T(8,128)(2,1)}, u32[]{:S(2)}) copy-start(bf16[768,2560]{1,0:T(8,128)(2,1)} %copy-done.25) | copy-start | bytes 11796484
  200.5 24.3 %copy-start.29 = (bf16[256,2560]{1,0:T(8,128)(2,1)S(1)}, bf16[256,2560]{1,0:T(8,128)(2,1)}, u32[]{:S(2)}) copy-start(bf16[256,2560]{1,0:T(8,128)(2,1)} %copy-done.27) | copy-start | bytes 3932164
  200.6 45.0 %collective-permute-start.16 = (bf16[160,2560]{1,0:T(8,128)(2,1)S(1)}, bf16[160,2560]{1,0:T(8,128)(2,1)S(1)}, u32[]{:S(2)}, u32[]{:S(2)}) collective-permute-start(bf16[160,2560]{1,0:T(8,128)(2,1)S(1)} %convolution_convert_fusion.1), channel_id=1, source_target_pairs={{0,1},{1,0},{2,3},{3,2},{4,5},{5,4},{6,7},{7,6},{8,9},{9,8},{10,11... | collective-permute-start | bytes 2457608 | tf_op jit(solution)/shard_map/ppermute | solution.py:70
  213.7 20.6 %collective-permute-start.20 = (bf16[160,1344]{1,0:T(8,128)(2,1)S(1)}, bf16[160,1344]{1,0:T(8,128)(2,1)S(1)}, u32[]{:S(2)}, u32[]{:S(2)}) collective-permute-start(bf16[160,1344]{1,0:T(8,128)(2,1)S(1)} %fusion.41), channel_id=1, source_target_pairs={{0,4},{4,8},{8,12},{12,0},{1,5},{5,9},{9,13},{13,1},{2,6},{6,10},{... | collective-permute-start | bytes 1290248 | tf_op jit(solution)/shard_map/ppermute | solution.py:70
  224.8 20.6 %collective-permute-start.24 = (bf16[336,768]{1,0:T(8,128)(2,1)S(1)}, bf16[336,768]{1,0:T(8,128)(2,1)S(1)}, u32[]{:S(2)}, u32[]{:S(2)}) collective-permute-start(bf16[336,768]{1,0:T(8,128)(2,1)S(1)} %fusion.39), channel_id=1, source_target_pairs={{0,4},{4,8},{8,12},{12,0},{1,5},{5,9},{9,13},{13,1},{2,6},{6,10},{... | collective-permute-start | bytes 1548296 | tf_op jit(solution)/shard_map/ppermute | solution.py:70
  234.4 20.6 %collective-permute-start.21 = (bf16[160,1344]{1,0:T(8,128)(2,1)S(1)}, bf16[160,1344]{1,0:T(8,128)(2,1)S(1)}, u32[]{:S(2)}, u32[]{:S(2)}) collective-permute-start(bf16[160,1344]{1,0:T(8,128)(2,1)S(1)} %fusion.40), channel_id=1, source_target_pairs={{0,4},{4,8},{8,12},{12,0},{1,5},{5,9},{9,13},{13,1},{2,6},{6,10},{... | collective-permute-start | bytes 1290248 | tf_op jit(solution)/shard_map/ppermute | solution.py:70
  245.5 20.2 %collective-permute-start.25 = (bf16[336,768]{1,0:T(8,128)(2,1)S(1)}, bf16[336,768]{1,0:T(8,128)(2,1)S(1)}, u32[]{:S(2)}, u32[]{:S(2)}) collective-permute-start(bf16[336,768]{1,0:T(8,128)(2,1)S(1)} %fusion.38), channel_id=1, source_target_pairs={{0,4},{4,8},{8,12},{12,0},{1,5},{5,9},{9,13},{13,1},{2,6},{6,10},{... | collective-permute-start | bytes 1548296 | tf_op jit(solution)/shard_map/ppermute | solution.py:70
  255.9 11.5 %copy-start.1 = (bf16[768,1536]{1,0:T(8,128)(2,1)S(1)}, bf16[768,1536]{1,0:T(8,128)(2,1)}, u32[]{:S(2)}) copy-start(bf16[768,1536]{1,0:T(8,128)(2,1)} %param.18) | copy-start | bytes 7077892

commit v2 on v1

--- a/solution.py
+++ b/solution.py
@@ -65,31 +65,9 @@
     )
 
 
-def shift(values, axis):
+def shift(values, axis, by=1):
     count = lax.axis_size(axis)
-    return lax.ppermute(values, axis, [(i, (i + 1) % count) for i in range(count)])
-
-
-def ring_gather(values, axis):
-    held = [values]
-    for _ in range(lax.axis_size(axis) - 1):
-        held.append(shift(held[-1], axis))
-    return held
-
-
-def ring_sum(blocks, axis):
-    count = lax.axis_size(axis)
-    me = lax.axis_index(axis)
-
-    def block(i):
-        return lax.dynamic_index_in_dim(blocks, lax.rem(i + 2 * count, count), 0, keepdims=False)
-
-    held = block(me - 1)
-    for step in range(1, count):
-        got = shift(held, axis).astype(jnp.float32)
-        total = got + block(me - 1 - step).astype(jnp.float32)
-        held = total.astype(jnp.bfloat16)
-    return total if count > 1 else held.astype(jnp.float32)
+    return lax.ppermute(values, axis, [(i, (i + by) % count) for i in range(count)])
 
 
 def core_sum(blocks):
@@ -123,24 +101,49 @@
     )
 
 
-def own_teacher(feats, inverse):
-    sent = feats.at[inverse].get(mode="promise_in_bounds", unique_indices=True)
-    got = lax.all_to_all(sent, ("dp", "teach"), split_axis=0, concat_axis=1, tiled=True)
-    return join_mp(got.reshape(-1, feats.shape[2]), 1)
-
-
-def gather_back(part, stream, gain):
+def tie(*values):
+    return lax.optimization_barrier(values)
+
+
+def swap_pair(values, axis):
+    count = lax.axis_size(axis)
+    return lax.ppermute(values, axis, [(i, i ^ 1) for i in range(count)])
+
+
+def paired(values, axis):
+    got = swap_pair(values, axis)
+    even = lax.rem(lax.axis_index(axis), 2) == 0
+    return jnp.concatenate([jnp.where(even, values, got), jnp.where(even, got, values)], axis=0)
+
+
+def first_part(weights, axes):
+    at = 0
+    for axis in reversed(axes):
+        at = at * 2 + lax.rem(lax.axis_index(axis), 2)
+    rows = weights.shape[0] // 2 ** len(axes)
+    return lax.dynamic_slice_in_dim(weights, at * rows, rows, 0)
+
+
+def gather_parts(held, axes):
+    for axis in axes:
+        held = paired(held, axis)
+    return held
+
+
+def back_rows(part, stream, gain):
     if lax.axis_size("mp") != 2:
-        own = norm_back(stream, gain, sum_mp(part)).astype(jnp.bfloat16)
-        return ring_gather(own, "dp")
+        return norm_back(stream, gain, sum_mp(part)).astype(jnp.bfloat16)
     me = lax.axis_index("mp")
     half = part.shape[0] // 2
     mine = lax.dynamic_slice_in_dim(part, me * half, half, 0)
     theirs = lax.dynamic_slice_in_dim(part, (1 - me) * half, half, 0)
     upstream = mine.astype(jnp.float32) + shift(theirs, "mp").astype(jnp.float32)
     rows = lax.dynamic_slice_in_dim(stream, me * half, half, 0)
-    back = norm_back(rows, gain, upstream).astype(jnp.bfloat16)
-    return [in_order(held, shift(held, "mp"), 0) for held in ring_gather(back, "dp")]
+    return norm_back(rows, gain, upstream).astype(jnp.bfloat16)
+
+
+def whole_rows(held):
+    return in_order(held, shift(held, "mp"), 0) if lax.axis_size("mp") == 2 else held
 
 
 def per_device(
@@ -166,39 +169,63 @@
     chip = lax.axis_index("dp")
     core = lax.axis_index("teach")
 
-    source = resid.reshape(rows, width).astype(jnp.float32)
-    normed = layer_norm(source, gain_mlp).astype(jnp.bfloat16)
-    all_normed = ring_gather(normed, "dp")
-
+    two = lax.axis_size("mp") == 2
     inverse = (
         jnp.zeros((total_images,), jnp.int32)
         .at[owner]
         .set(jnp.arange(total_images, dtype=jnp.int32))
     )
-    teacher_dino = own_teacher(dino_feats, inverse)
-    teacher_sig = own_teacher(sig_feats, inverse)
-
+    sent = jnp.concatenate([dino_feats, sig_feats], axis=2)
+    sent = sent.at[inverse].get(mode="promise_in_bounds", unique_indices=True)
+    resid, sent = tie(resid, sent)
+    got = lax.all_to_all(sent, ("dp", "teach"), split_axis=0, concat_axis=1, tiled=True)
+    got = got.reshape(rows, -1)
+    if two:
+        first_b_dino = first_part(b_dino, ("dp", "groups", "teach"))
+        first_b_sig = first_part(b_sig, ("groups", "teach"))
+        resid, first_b_dino, first_b_sig = tie(resid, first_b_dino, first_b_sig)
+        first_b_dino = shift(first_b_dino, "mp")
+        first_b_sig = shift(first_b_sig, "mp")
+    source = resid.reshape(rows, width).astype(jnp.float32)
+    normed = layer_norm(source, gain_mlp).astype(jnp.bfloat16)
+    normed_sent, got = tie(normed, got)
+    others = [shift(normed_sent, "dp", -k) for k in range(1, n_chips)]
     hidden, slope = gelu_and_slope(matmul(normed, w_in))
-    stream = source + sum_mp(matmul(hidden, w_out).astype(jnp.bfloat16))
+    out_part = matmul(hidden, w_out).astype(jnp.bfloat16)
+
+    dino_part = dino_feats.shape[2]
+
+    stream = source + sum_mp(out_part)
     summary = layer_norm(stream, gain_out).astype(jnp.bfloat16)
-
     act_dino, slope_dino = gelu_and_slope(matmul(summary, a_dino))
     act_sig, slope_sig = gelu_and_slope(matmul(summary, a_sig))
-    pred_dino = sum_mp(matmul(act_dino, b_dino).astype(jnp.bfloat16))
-    pred_sig = sum_mp(matmul(act_sig, b_sig).astype(jnp.bfloat16))
-
-    back_dino = cosine_back(
-        pred_dino, teacher_dino.astype(jnp.float32), b_dino.shape[1], factor
-    ).astype(jnp.bfloat16)
-    back_sig = cosine_back(
-        pred_sig, teacher_sig.astype(jnp.float32), b_sig.shape[1], factor
-    ).astype(jnp.bfloat16)
+    if two:
+        peer_act_dino = shift(act_dino, "mp")
+        peer_act_sig = shift(act_sig, "mp")
+        peer_b_dino = gather_parts(first_b_dino, ("dp", "groups", "teach"))
+        peer_b_sig = gather_parts(first_b_sig, ("groups", "teach"))
+        got_sent, summary = tie(got, summary)
+        peer_got = shift(got_sent, "mp")
+        teacher_dino = in_order(got[:, :dino_part], peer_got[:, :dino_part], 1)
+        teacher_sig = in_order(got[:, dino_part:], peer_got[:, dino_part:], 1)
+    else:
+        teacher_dino = join_mp(got[:, :dino_part], 1)
+        teacher_sig = join_mp(got[:, dino_part:], 1)
+    if two:
+        pred_dino = matmul(act_dino, b_dino) + matmul(peer_act_dino, peer_b_dino)
+        pred_sig = matmul(act_sig, b_sig) + matmul(peer_act_sig, peer_b_sig)
+    else:
+        pred_dino = sum_mp(matmul(act_dino, b_dino).astype(jnp.bfloat16))
+        pred_sig = sum_mp(matmul(act_sig, b_sig).astype(jnp.bfloat16))
+
+    back_dino = cosine_back(pred_dino, teacher_dino.astype(jnp.float32), b_dino.shape[1], factor).astype(jnp.bfloat16)
+    back_sig = cosine_back(pred_sig, teacher_sig.astype(jnp.float32), b_sig.shape[1], factor).astype(jnp.bfloat16)
     down_dino = (slope_dino * contract_cols(back_dino, b_dino)).astype(jnp.bfloat16)
     down_sig = (slope_sig * contract_cols(back_sig, b_sig)).astype(jnp.bfloat16)
     part = (contract_cols(down_dino, a_dino) + contract_cols(down_sig, a_sig)).astype(
         jnp.bfloat16
     )
-    backs = jnp.concatenate(gather_back(part, stream, gain_out), axis=0)
+    back = back_rows(part, stream, gain_out)
 
     def blocks(grad):
         return grad.astype(jnp.bfloat16).reshape(n_chips, n_cores, -1, grad.shape[1])
@@ -210,19 +237,40 @@
     grad_b = jnp.concatenate(
         [grad_b_d, jnp.pad(grad_b_s, ((0, 0), (0, 0), (0, 0), (0, wide - narrow)))], axis=2
     )
-    grad_b = ring_sum(core_sum(grad_b), "dp")
-    out_b_d = grad_b[:cut].T
-    out_b_s = grad_b[cut:, :narrow].T
+    chip_b = core_sum(grad_b)
+    back, chip_b = tie(back, chip_b)
     grad_a = jnp.concatenate(
         [contract_rows(summary, down_dino), contract_rows(summary, down_sig)], axis=1
     )
-    grad_a = ring_sum(core_sum(blocks(grad_a)), "dp")
-    out_a_d = grad_a[:, : down_dino.shape[1]]
-    out_a_s = grad_a[:, down_dino.shape[1] :]
-
-    others = jnp.concatenate(all_normed[1:], axis=0)
+    chip_a = core_sum(blocks(grad_a))
+
+    def block(values, i):
+        return lax.dynamic_index_in_dim(values, lax.rem(i + 2 * n_chips, n_chips), 0, keepdims=False)
+
+    def ring_step(held, total, chip_sums, step):
+        got = shift(held, "dp")
+        total = got.astype(jnp.float32) + block(chip_sums, chip - 1 - step).astype(jnp.float32)
+        return total.astype(jnp.bfloat16), total
+
+    held_s = [back]
+    held_b, held_a = block(chip_b, chip - 1), block(chip_a, chip - 1)
+    total_b, total_a = held_b.astype(jnp.float32), held_a.astype(jnp.float32)
+    held_s += [shift(back, "dp", -k) for k in range(1, n_chips)]
+    for step in range(1, n_chips):
+        held_b, total_b = ring_step(held_b, total_b, chip_b, step)
+        if step == 1:
+            held_s[1], held_b, held_a = tie(held_s[1], held_b, held_a)
+        held_a, total_a = ring_step(held_a, total_a, chip_a, step)
+    backs = jnp.concatenate([whole_rows(held) for held in held_s], axis=0)
+    out_b_d = total_b[:cut].T
+    out_b_s = total_b[cut:, :narrow].T
+    out_a_d = total_a[:, : down_dino.shape[1]]
+    out_a_s = total_a[:, down_dino.shape[1] :]
+
+    others = jnp.concatenate(others, axis=0)
+    others, _ = tie(others, held_s[1])
+    normeds = jnp.concatenate([normed, others], axis=0)
     other_hidden, other_slope = gelu_and_slope(matmul(others, w_in))
-    normeds = jnp.concatenate([normed, others], axis=0)
     hiddens = jnp.concatenate([hidden, other_hidden], axis=0)
     slopes = jnp.concatenate([slope, other_slope], axis=0)
     back_hidden = (slopes * contract_cols(backs, w_out)).astype(jnp.bfloat16)

time: 268 us -> 248 us (0.925)
  waiting for transfers between devices: 135 us -> 87.3 us
  starting transfers between devices: 28.7 us -> 39.2 us
  local copies, waits for them, and re-layouts: 17.4 us -> 25.8 us
  matrix products: 62.2 us -> 67.8 us
    ppermute x26 -> x32, waiting for transfers between devices: 113 us -> 87.3 us  [the longest x27 87.2 us: shift(): lax.ppermute(values, axis, [(i, (i + by) % count) for i in range(count)])]
    all_to_all x2 -> x1, waiting for transfers between devices: 21.9 us -> 0.01 us  [per_device(): lax.all_to_all(sent, ('dp', 'teach'), split_axis=0, concat_axis=1, tiled=...]
    ppermute x26 -> x32, starting transfers between devices: 20.4 us -> 35 us  [the longest x27 30.6 us: shift(): lax.ppermute(values, axis, [(i, (i + by) % count) for i in range(count)])]
    dot_general x7 -> x9, matrix products: 26.2 us -> 34.1 us  [matmul(): return jnp.dot(left, right, preferred_element_type=jnp.float32)]
    select_n x1 -> x6, other arithmetic: 0.01 us -> 7.66 us  [the longest x5 7.66 us: paired(): jnp.where(even, values, got)]
    unnamed x68 -> x76, local copies, waits for them, and re-layouts: 4.5 us -> 9.16 us
    concatenate x2 -> x6, other arithmetic: 2.43 us -> 7.05 us  [the longest x3 3.29 us: paired(): jnp.concatenate([jnp.where(even, values, got), jnp.where(even, got, value...]
    all_to_all x2 -> x1, starting transfers between devices: 8.33 us -> 4.21 us  [per_device(): lax.all_to_all(sent, ('dp', 'teach'), split_axis=0, concat_axis=1, tiled=...]
  transfers between devices with their start and end apart: 28 -> 33, of which waited for: 13 -> 10; matrix products, arithmetic and copies ran while one was open for 31% -> 41% of each run, Pallas kernels for 0% -> 0%
where the time goes in v2:
time: 248 us; the launch traced here: 247 us
  waiting for transfers between devices  87.3 us (35%)
  matrix products  67.8 us (27%)
  starting transfers between devices  39.2 us (16%)
  local copies, waits for them, and re-layouts  25.8 us (10%)
  other arithmetic  25.1 us (10%)
    ppermute x27, waiting for transfers between devices, shift(): lax.ppermute(values, axis, [(i, (i + by) % count) for i in range(count)])  87.2 us
    dot_general x9, matrix products, matmul(): return jnp.dot(left, right, preferred_element_type=jnp.float32)  34.1 us
    ppermute x27, starting transfers between devices, shift(): lax.ppermute(values, axis, [(i, (i + by) % count) for i in range(count)])  30.6 us
    dot_general x8, matrix products, contract_rows(): lax.dot_general(left, right, (((0,), (0,)), ((), ())), preferred_element_...  17 us
    dot_general x5, matrix products, contract_cols(): lax.dot_general(left, right, (((1,), (1,)), ((), ())), preferred_element_...  16.7 us
    unnamed x76, local copies, waits for them, and re-layouts  9.16 us
    select_n x5, other arithmetic, paired(): jnp.where(even, values, got)  7.66 us
  transfers between devices with their start and end apart: 33, of which 10 were waited for; matrix products, arithmetic and copies ran while one was open for 41% of the time, Pallas kernels for 0%

profile of v2, /device:TPU:0, one launch (start us, length us, event | category | flops | bytes accessed | tf_op | source)
XLA Modules:
  0.0 246.6 jit_solution(12888737290054177487)
XLA Ops:
  2.1 2.1 pad_maximum_fusion.6
  4.2 2.6 %gather_fusion = bf16[8,32,1344]{2,1,0:T(8,128)(2,1)} fusion(bf16[8,32,1344]{2,1,0:T(8,128)(2,1)} %pad_maximum_fusion.6, s32[1024]{0:T(1024)S(1)} %pad_clamp_fusion), kind=kCustom, calls=%fused_computation | custom fusion | bytes 1376288 | tf_op jit(solution)/shard_map/gather | solution.py:179
  8.5 3.0 %collective-permute-start.5 = (bf16[96,1536]{1,0:T(8,128)(2,1)}, bf16[96,1536]{1,0:T(8,128)(2,1)}, u32[]{:S(2)}, u32[]{:S(2)}) collective-permute-start(bf16[96,1536]{1,0:T(8,128)(2,1)} %constant_dynamic-slice_fusion.2), channel_id=1, source_target_pairs={{0,2},{2,0},{1,3},{3,1},{4,6},{6,4},{5,7},{7,5},{8,10},{10,8},{9,1... | collective-permute-start | bytes 884744 | tf_op jit(solution)/shard_map/ppermute | solution.py:70
  12.5 7.3 %add_convert_fusion.1 = (bf16[256,2560]{1,0:T(8,128)(2,1)}, bf16[256,2560]{1,0:T(8,128)(2,1)S(1)}) fusion(bf16[256,1280]{1,0:T(8,128)(2,1)S(1)} %fusion.28, bf16[1280,2560]{1,0:T(8,128)(2,1)} %param.15), kind=kOutput, calls=%fused_computation.37 | convolution fusion | flops 1690173440 | bytes 9830400 | tf_op jit(solution)/shard_map/dot_general | solution.py:53
  19.8 2.1 collective-permute-start.6
  21.9 2.7 %convolution_convert_fusion.6 = bf16[256,1280]{1,0:T(8,128)(2,1)} fusion(bf16[256,2560]{1,0:T(8,128)(2,1)S(1)} %get-tuple-element.49, bf16[2560,1280]{1,0:T(8,128)(2,1)S(1)} %bitcast.111), kind=kOutput, calls=%fused_computation.41 | convolution fusion | flops 1678049280 | bytes 8519680 | tf_op jit(solution)/shard_map/dot_general | solution.py:53
  24.6 1.5 collective-permute-start.3
  26.1 4.2 %all-to-all-start = ((bf16[8,32,1344]{2,1,0:T(8,128)(2,1)}), bf16[8,32,1344]{2,1,0:T(8,128)(2,1)}, u32[]{:S(2)}, u32[]{:S(2)}) async-start(bf16[8,32,1344]{2,1,0:T(8,128)(2,1)} %gather_fusion), calls=%async_computation | async-start | bytes 1441792 | tf_op jit(solution)/shard_map/all_to_all | solution.py:181
  30.4 1.6 collective-permute-start.12
  32.0 1.1 broadcast_select_fusion.13
  33.7 6.9 %collective-permute-done.3 = bf16[256,1280]{1,0:T(8,128)(2,1)} collective-permute-done((bf16[256,1280]{1,0:T(8,128)(2,1)}, bf16[256,1280]{1,0:T(8,128)(2,1)}, u32[]{:S(2)}, u32[]{:S(2)}) %collective-permute-start.3) | collective-permute-done | bytes 655392 | tf_op jit(solution)/shard_map/ppermute | solution.py:70
  40.6 1.6 fusion.66
  42.8 1.3 copy-done.23
  44.1 1.6 multiply_convert_fusion.6
  45.6 2.8 %fusion.69 = f32[256,1152]{1,0:T(8,128)} fusion(bf16[256,576]{0,1:T(8,128)(2,1)} %get-tuple-element.68, bf16[576,1152]{1,0:T(8,128)(2,1)S(1)} %copy-done.16), kind=kOutput, calls=%fused_computation.185 | convolution fusion | flops 339738624 | bytes 2801664 | tf_op jit(solution)/shard_map/dot_general | solution.py:53
  48.5 1.5 collective-permute-start.10
  50.0 1.7 multiply_convert_fusion.4
  52.5 2.9 %fusion.68 = f32[256,1536]{1,0:T(8,128)} fusion(bf16[256,768]{1,0:T(8,128)(2,1)} %get-tuple-element.71, bf16[768,1536]{1,0:T(8,128)(2,1)S(1)} %copy-done), kind=kOutput, calls=%fused_computation.184 | convolution fusion | flops 603979776 | bytes 4325376 | tf_op jit(solution)/shard_map/dot_general | solution.py:53
  55.5 1.0 broadcast_select_fusion.9
  58.1 1.3 broadcast_select_fusion.5
  59.5 2.3 copy.28
  61.7 1.5 collective-permute-start.9
  63.2 2.4 pad_maximum_fusion.4
  65.8 3.3 %collective-permute-start = (bf16[256,1280]{1,0:T(8,128)(2,1)S(1)}, bf16[256,1280]{1,0:T(8,128)(2,1)}, u32[]{:S(2)}, u32[]{:S(2)}) collective-permute-start(bf16[256,1280]{1,0:T(8,128)(2,1)S(1)} %copy-done.7), channel_id=1, source_target_pairs={{0,12},{4,0},{8,4},{12,8},{1,13},{5,1},{9,5},{13,9},{2,14},{6,2},{... | collective-permute-start | bytes 1966088 | tf_op jit(solution)/shard_map/ppermute | solution.py:70
  69.1 2.4 broadcast_select_fusion.3
  71.5 8.3 %collective-permute-done.9 = bf16[256,1344]{0,1:T(8,128)(2,1)S(1)} collective-permute-done((bf16[256,1344]{0,1:T(8,128)(2,1)}, bf16[256,1344]{0,1:T(8,128)(2,1)S(1)}, u32[]{:S(2)}, u32[]{:S(2)}) %collective-permute-start.9) | collective-permute-done | bytes 688160 | tf_op jit(solution)/shard_map/ppermute | solution.py:70
  79.8 2.6 %collective-permute-start.1 = (bf16[256,1280]{1,0:T(8,128)(2,1)S(1)}, bf16[256,1280]{1,0:T(8,128)(2,1)}, u32[]{:S(2)}, u32[]{:S(2)}) collective-permute-start(bf16[256,1280]{1,0:T(8,128)(2,1)S(1)} %copy-done.7), channel_id=1, source_target_pairs={{0,8},{4,12},{8,0},{12,4},{1,9},{5,13},{9,1},{13,5},{2,10},{6,14},... | collective-permute-start | bytes 1966088 | tf_op jit(solution)/shard_map/ppermute | solution.py:70
  83.1 1.2 copy.40
  85.3 1.5 collective-permute-start.2
  86.8 2.8 %multiply_reduce_fusion.2 = (f32[256]{0:T(256)S(1)}, f32[256]{0:T(256)S(1)}, f32[256]{0:T(256)S(1)}, f32[256,1152]{1,0:T(8,128)S(1)}) fusion(bf16[256,576]{1,0:T(8,128)(2,1)S(1)} %get-tuple-element.59, bf16[256,576]{1,0:T(8,128)(2,1)S(1)} %get-tuple-element.58, f32[256,1152]{1,0:T(8,128)} %fusion.69, bf16[256,576]{0,1:T(8,128)(2,1)} %collective-permute-done.10, ...), kind=kOutput, calls=%fused_computation.91 | convolution fusion | flops 345636096 | bytes 4574208 | tf_op jit(solution)/shard_map/dot_general | solution.py:53
  91.1 1.5 fusion.30
  93.5 2.9 %convolution_convert_fusion.4 = bf16[1280,576]{0,1:T(8,128)(2,1)} fusion(bf16[256,576]{0,1:T(8,128)(2,1)} %fusion.30, bf16[256,1280]{1,0:T(8,128)(2,1)} %copy-done.8), kind=kOutput, calls=%fused_computation.26 | convolution fusion | flops 378224640 | bytes 2424832 | tf_op jit(solution)/shard_map/dot_general | solution.py:57
  96.4 2.6 %copy.34 = bf16[1280,576]{1,0:T(8,128)(2,1)} copy(bf16[1280,576]{0,1:T(8,128)(2,1)} %convolution_convert_fusion.4) | data formatting | bytes 2949120 | tf_op jit(solution)/shard_map/convert.10
  99.0 2.8 %convolution_convert_fusion.5 = bf16[1152,576]{0,1:T(8,128)(2,1)} fusion(bf16[256,576]{0,1:T(8,128)(2,1)} %get-tuple-element.68, bf16[256,1152]{1,0:T(8,128)(2,1)} %copy-done.15), kind=kOutput, calls=%fused_computation.27 | convolution fusion | flops 340402176 | bytes 2211840 | tf_op jit(solution)/shard_map/dot_general | solution.py:57
  101.9 2.6 %copy.31 = bf16[1152,576]{1,0:T(8,128)(2,1)} copy(bf16[1152,576]{0,1:T(8,128)(2,1)} %convolution_convert_fusion.5) | data formatting | bytes 2654208 | tf_op jit(solution)/shard_map/convert_element_type | solution.py:231
  104.5 1.1 broadcast_select_fusion.7
  105.6 2.2 fusion.70
  107.8 1.8 broadcast_select_fusion.1
  109.7 2.1 multiply_reduce_fusion
  111.8 2.3 convolution_convert_fusion.3
  114.1 1.3 fusion.29
  117.0 1.1 copy-done.10
  118.8 1.3 copy-done.19
  120.9 1.5 collective-permute-start.14
  122.4 3.4 %collective-permute-done.1 = bf16[256,1280]{1,0:T(8,128)(2,1)} collective-permute-done((bf16[256,1280]{1,0:T(8,128)(2,1)S(1)}, bf16[256,1280]{1,0:T(8,128)(2,1)}, u32[]{:S(2)}, u32[]{:S(2)}) %collective-permute-start.1) | collective-permute-done | bytes 655392 | tf_op jit(solution)/shard_map/ppermute | solution.py:70
  125.8 1.6 pad_maximum_fusion.3
  127.5 2.4 collective-permute-done.14
  131.7 1.5 collective-permute-start.19
  133.2 2.8 %collective-permute-start.16 = (bf16[128,1280]{1,0:T(8,128)(2,1)S(1)}, bf16[128,1280]{1,0:T(8,128)(2,1)S(1)}, u32[]{:S(2)}, u32[]{:S(2)}) collective-permute-start(bf16[128,1280]{1,0:T(8,128)(2,1)S(1)} %multiply_convert_fusion.5), channel_id=1, source_target_pairs={{0,12},{4,0},{8,4},{12,8},{1,13},{5,1},{9,5},{13,9},{2,14},{6,2},{... | collective-permute-start | bytes 983048 | tf_op jit(solution)/shard_map/ppermute | solution.py:70
  136.8 2.9 %collective-permute-start.17 = (bf16[336,768]{1,0:T(8,128)(2,1)S(1)}, bf16[336,768]{1,0:T(8,128)(2,1)S(1)}, u32[]{:S(2)}, u32[]{:S(2)}) collective-permute-start(bf16[336,768]{1,0:T(8,128)(2,1)S(1)} %dynamic-slice_bitcast_fusion.1), channel_id=1, source_target_pairs={{0,4},{4,8},{8,12},{12,0},{1,5},{5,9},{9,13},{13,1},{2,6},{6,10},{... | collective-permute-start | bytes 1548296 | tf_op jit(solution)/shard_map/ppermute | solution.py:70
  140.0 33.4 %collective-permute-done.21 = bf16[128,1280]{1,0:T(8,128)(2,1)S(1)} collective-permute-done((bf16[128,1280]{1,0:T(8,128)(2,1)S(1)}, bf16[128,1280]{1,0:T(8,128)(2,1)S(1)}, u32[]{:S(2)}, u32[]{:S(2)}) %collective-permute-start.21) | collective-permute-done | bytes 327712 | tf_op jit(solution)/shard_map/ppermute | solution.py:70
  173.4 1.4 collective-permute-start.22
  175.6 1.4 collective-permute-start.27
  177.1 1.2 collective-permute-start.20
  178.2 10.2 %multiply_convert_fusion.1 = (bf16[768,2560]{1,0:T(8,128)(2,1)S(1)}, bf16[768,2560]{1,0:T(8,128)(2,1)}) fusion(bf16[768,1280]{1,0:T(8,128)(2,1)S(1)} %pad_maximum_fusion.3, bf16[1280,2560]{1,0:T(8,128)(2,1)S(1)} %bitcast.109), kind=kOutput, calls=%fused_computation.5 | convolution fusion | flops 5070520320 | bytes 16384000 | tf_op jit(solution)/shard_map/dot_general | solution.py:53
  188.4 6.6 %collective-permute-done.20 = bf16[128,1280]{1,0:T(8,128)(2,1)S(1)} collective-permute-done((bf16[128,1280]{1,0:T(8,128)(2,1)S(1)}, bf16[128,1280]{1,0:T(8,128)(2,1)S(1)}, u32[]{:S(2)}, u32[]{:S(2)}) %collective-permute-start.20) | collective-permute-done | bytes 327712 | tf_op jit(solution)/shard_map/ppermute | solution.py:70
  196.5 1.8 convolution_convert_fusion
  198.4 11.1 %multiply_convert_fusion = bf16[1024,2560]{1,0:T(8,128)(2,1)S(1)} fusion(bf16[1024,1280]{1,0:T(8,128)(2,1)S(1)} %select_dynamic-update-slice_fusion, bf16[2560,1280]{1,0:T(8,128)(2,1)} %param.16, bf16[768,2560]{1,0:T(8,128)(2,1)} %get-tuple-element.47, bf16[256,2560]{1,0:T(8,128)(2,1)S(1)} %copy-done.32), kind=kOutput, calls=%fused_computation.2 | convolution fusion | flops 6726615040 | bytes 19660800 | tf_op jit(solution)/shard_map/dot_general | solution.py:63
  210.0 1.3 convolution_convert_fusion.1
  211.7 12.9 %collective-permute-done.28 = bf16[160,1344]{1,0:T(8,128)(2,1)S(1)} collective-permute-done((bf16[160,1344]{1,0:T(8,128)(2,1)S(1)}, bf16[160,1344]{1,0:T(8,128)(2,1)S(1)}, u32[]{:S(2)}, u32[]{:S(2)}) %collective-permute-start.28) | collective-permute-done | bytes 430112 | tf_op jit(solution)/shard_map/ppermute | solution.py:70
  224.8 10.9 %collective-permute-done.31 = bf16[336,768]{1,0:T(8,128)(2,1)S(1)} collective-permute-done((bf16[336,768]{1,0:T(8,128)(2,1)S(1)}, bf16[336,768]{1,0:T(8,128)(2,1)S(1)}, u32[]{:S(2)}, u32[]{:S(2)}) %collective-permute-start.31) | collective-permute-done | bytes 516128 | tf_op jit(solution)/shard_map/ppermute | solution.py:70
  237.4 2.5 %convert_add_fusion.2 = f32[160,2560]{1,0:T(8,128)} fusion(bf16[160,2560]{1,0:T(8,128)(2,1)S(1)} %collective-permute-done.25, bf16[1024,2560]{1,0:T(8,128)(2,1)S(1)} %multiply_convert_fusion, s32[]{:T(128)S(6)} %select_n.206, bf16[768,1280]{1,0:T(8,128)(2,1)S(1)} %pad_maximum_fusion.3, bf16[256,1280]{1,0:T(8,128)(2,1)S(1)} %copy-done.7), kind=kOutput, calls=%fused_computation.56 | convolution fusion | flops 840335360 | bytes 10321924 | tf_op jit(solution)/shard_map/dot_general | solution.py:57
  239.9 2.7 %convolution_add_fusion = f32[2560,160]{0,1:T(8,128)} fusion(bf16[768,2560]{1,0:T(8,128)(2,1)S(1)} %copy-done.29, bf16[256,2560]{1,0:T(8,128)(2,1)S(1)} %copy-done.31, bf16[2560,160]{0,1:T(8,128)(2,1)S(1)} %collective-permute-done.26, bf16[1024,1280]{1,0:T(8,128)(2,1)S(1)} %select_dynamic-update-slice_fusion, s32[]{:T(128)S(6)} %select_n.206), kind=kOutput, calls=%fused_computation.17 | convolution fusion | flops 850165760 | bytes 8224772 | tf_op jit(solution)/shard_map/dot_general | solution.py:57
  242.6 2.3 collective-permute-done.29
  (174 shorter events, 24.7 us)
Async XLA Ops:
  0.6 6.2 %copy-start = (bf16[768,1536]{1,0:T(8,128)(2,1)S(1)}, bf16[768,1536]{1,0:T(8,128)(2,1)}, u32[]{:S(2)}) copy-start(bf16[768,1536]{1,0:T(8,128)(2,1)} %param.18) | copy-start | bytes 7077892
  2.1 9.5 %copy-start.5 = (bf16[1,256,1280]{2,1,0:T(8,128)(2,1)S(1)}, bf16[1,256,1280]{2,1,0:T(8,128)(2,1)}, u32[]{:S(2)}) copy-start(bf16[1,256,1280]{2,1,0:T(8,128)(2,1)} %param.12) | copy-start | bytes 1966084
  4.2 7.9 %copy-start.25 = (f32[1280]{0:T(1024)S(1)}, f32[1280]{0:T(1024)}, u32[]{:S(2)}) copy-start(f32[1280]{0:T(1024)} %param.13) | copy-start | bytes 15364
  8.5 11.3 %collective-permute-start.5 = (bf16[96,1536]{1,0:T(8,128)(2,1)}, bf16[96,1536]{1,0:T(8,128)(2,1)}, u32[]{:S(2)}, u32[]{:S(2)}) collective-permute-start(bf16[96,1536]{1,0:T(8,128)(2,1)} %constant_dynamic-slice_fusion.2), channel_id=1, source_target_pairs={{0,2},{2,0},{1,3},{3,1},{4,6},{6,4},{5,7},{7,5},{8,10},{10,8},{9,1... | collective-permute-start | bytes 884744 | tf_op jit(solution)/shard_map/ppermute | solution.py:70
  11.6 18.9 %collective-permute-start.11 = (bf16[144,1152]{1,0:T(8,128)(2,1)S(1)}, bf16[144,1152]{1,0:T(8,128)(2,1)}, u32[]{:S(2)}, u32[]{:S(2)}) collective-permute-start(bf16[144,1152]{1,0:T(8,128)(2,1)S(1)} %constant_dynamic-slice_fusion.1), channel_id=1, source_target_pairs={{0,2},{2,0},{1,3},{3,1},{4,6},{6,4},{5,7},{7,5},{8,10},{10,8},{9,1... | collective-permute-start | bytes 995336 | tf_op jit(solution)/shard_map/ppermute | solution.py:70
  12.2 9.8 %slice-start.3 = ((s8[6553600]{0:T(1024)(128)(4,1)}), s8[4194304]{0:T(1024)(128)(4,1)S(1)}, s32[]{:S(2)}) async-start(s8[6553600]{0:T(1024)(128)(4,1)} %bitcast.110), calls=%async_computation.4 | async-start | bytes 8388608
  12.5 7.4 %copy-start.6 = (bf16[256,1280]{1,0:T(8,128)(2,1)}, bf16[256,1280]{1,0:T(8,128)(2,1)S(1)}, u32[]{:S(2)}) copy-start(bf16[256,1280]{1,0:T(8,128)(2,1)S(1)} %fusion.28) | copy-start | bytes 1966084
  12.5 9.5 %slice-start.4 = ((s8[6553600]{0:T(1024)(128)(4,1)}), s8[2359296]{0:T(1024)(128)(4,1)S(1)}, s32[]{:S(2)}) async-start(s8[6553600]{0:T(1024)(128)(4,1)} %bitcast.110), calls=%async_computation.5 | async-start | bytes 4718592
  19.8 4.8 %copy-start.30 = (bf16[256,2560]{1,0:T(8,128)(2,1)}, bf16[256,2560]{1,0:T(8,128)(2,1)S(1)}, u32[]{:S(2)}) copy-start(bf16[256,2560]{1,0:T(8,128)(2,1)S(1)} %get-tuple-element.49) | copy-start | bytes 3932164
  19.8 12.2 %collective-permute-start.6 = (bf16[96,1536]{1,0:T(8,128)(2,1)}, bf16[96,1536]{1,0:T(8,128)(2,1)}, u32[]{:S(2)}, u32[]{:S(2)}) collective-permute-start(bf16[96,1536]{1,0:T(8,128)(2,1)} %collective-permute-done.5), channel_id=1, source_target_pairs={{0,4},{4,0},{8,12},{12,8},{1,5},{5,1},{9,13},{13,9},{2,6},{6,2},{1... | collective-permute-start | bytes 884744 | tf_op jit(solution)/shard_map/ppermute | solution.py:110
  24.6 16.0 %collective-permute-start.3 = (bf16[256,1280]{1,0:T(8,128)(2,1)}, bf16[256,1280]{1,0:T(8,128)(2,1)}, u32[]{:S(2)}, u32[]{:S(2)}) collective-permute-start(bf16[256,1280]{1,0:T(8,128)(2,1)} %convolution_convert_fusion.6), channel_id=1, source_target_pairs={{0,2},{2,0},{1,3},{3,1},{4,6},{6,4},{5,7},{7,5},{8,10},{10,8},{9,1... | collective-permute-start | bytes 1966088 | tf_op jit(solution)/shard_map/ppermute | solution.py:70
  26.1 33.3 %all-to-all-start = ((bf16[8,32,1344]{2,1,0:T(8,128)(2,1)}), bf16[8,32,1344]{2,1,0:T(8,128)(2,1)}, u32[]{:S(2)}, u32[]{:S(2)}) async-start(bf16[8,32,1344]{2,1,0:T(8,128)(2,1)} %gather_fusion), calls=%async_computation | async-start | bytes 1441792 | tf_op jit(solution)/shard_map/all_to_all | solution.py:181
  30.4 25.1 %collective-permute-start.12 = (bf16[144,1152]{1,0:T(8,128)(2,1)}, bf16[144,1152]{1,0:T(8,128)(2,1)S(1)}, u32[]{:S(2)}, u32[]{:S(2)}) collective-permute-start(bf16[144,1152]{1,0:T(8,128)(2,1)} %collective-permute-done.11), channel_id=1, source_target_pairs={{0,16},{16,0},{1,17},{17,1},{2,18},{18,2},{3,19},{19,3},{4,20},{20... | collective-permute-start | bytes 995336 | tf_op jit(solution)/shard_map/ppermute | solution.py:110
  33.1 9.4 %copy-start.24 = (f32[1280]{0:T(1024)S(1)}, f32[1280]{0:T(1024)}, u32[]{:S(2)}) copy-start(f32[1280]{0:T(1024)} %param.14) | copy-start | bytes 15364
  33.2 25.0 %collective-permute-start.7 = (bf16[192,1536]{1,0:T(8,128)(2,1)S(1)}, bf16[192,1536]{1,0:T(8,128)(2,1)S(1)}, u32[]{:S(2)}, u32[]{:S(2)}) collective-permute-start(bf16[192,1536]{1,0:T(8,128)(2,1)S(1)} %pad_maximum_fusion.8), channel_id=1, source_target_pairs={{0,16},{16,0},{1,17},{17,1},{2,18},{18,2},{3,19},{19,3},{4,20},{20... | collective-permute-start | bytes 1769480 | tf_op jit(solution)/shard_map/ppermute | solution.py:110
  42.2 10.1 %copy-start.2 = (f32[256,1280]{1,0:T(8,128)}, f32[256,1280]{1,0:T(8,128)S(1)}, u32[]{:S(2)}) copy-start(f32[256,1280]{1,0:T(8,128)S(1)} %get-tuple-element.45) | copy-start | bytes 3932164
  42.2 1.8 copy-start.23
  44.1 5.9 %copy-start.8 = (bf16[256,1280]{1,0:T(8,128)(2,1)}, bf16[256,1280]{1,0:T(8,128)(2,1)S(1)}, u32[]{:S(2)}) copy-start(bf16[256,1280]{1,0:T(8,128)(2,1)S(1)} %multiply_convert_fusion.3) | copy-start | bytes 1966084
  44.1 1.6 copy-start.16
  45.6 4.3 %copy-start.18 = (bf16[1280,768]{1,0:T(8,128)(2,1)S(1)}, bf16[1280,768]{1,0:T(8,128)(2,1)}, u32[]{:S(2)}) copy-start(bf16[1280,768]{1,0:T(8,128)(2,1)} %param.17) | copy-start | bytes 5898244
  48.5 36.9 %collective-permute-start.10 = (bf16[256,576]{0,1:T(8,128)(2,1)}, bf16[256,576]{0,1:T(8,128)(2,1)}, u32[]{:S(2)}, u32[]{:S(2)}) collective-permute-start(bf16[256,576]{0,1:T(8,128)(2,1)} %get-tuple-element.68), channel_id=1, source_target_pairs={{0,2},{2,0},{1,3},{3,1},{4,6},{6,4},{5,7},{7,5},{8,10},{10,8},{9,1... | collective-permute-start | bytes 884744 | tf_op jit(solution)/shard_map/ppermute | solution.py:70
  51.7 58.0 %collective-permute-start.4 = (bf16[256,768]{1,0:T(8,128)(2,1)}, bf16[256,768]{1,0:T(8,128)(2,1)}, u32[]{:S(2)}, u32[]{:S(2)}) collective-permute-start(bf16[256,768]{1,0:T(8,128)(2,1)} %get-tuple-element.71), channel_id=1, source_target_pairs={{0,2},{2,0},{1,3},{3,1},{4,6},{6,4},{5,7},{7,5},{8,10},{10,8},{9,1... | collective-permute-start | bytes 1179656 | tf_op jit(solution)/shard_map/ppermute | solution.py:70
  58.1 7.7 %collective-permute-start.13 = (bf16[288,1152]{1,0:T(8,128)(2,1)}, bf16[288,1152]{1,0:T(8,128)(2,1)}, u32[]{:S(2)}, u32[]{:S(2)}) collective-permute-start(bf16[288,1152]{1,0:T(8,128)(2,1)} %pad_maximum_fusion.7), channel_id=1, source_target_pairs={{0,1},{1,0},{2,3},{3,2},{4,5},{5,4},{6,7},{7,6},{8,9},{9,8},{10,11... | collective-permute-start | bytes 1990664 | tf_op jit(solution)/shard_map/ppermute | solution.py:110
  59.4 6.4 %copy-start.7 = (bf16[256,1280]{1,0:T(8,128)(2,1)S(1)}, bf16[256,1280]{1,0:T(8,128)(2,1)}, u32[]{:S(2)}) copy-start(bf16[256,1280]{1,0:T(8,128)(2,1)} %copy-done.6) | copy-start | bytes 1966084
  61.7 7.4 %copy-start.14 = (bf16[144,1152]{1,0:T(8,128)(2,1)S(1)}, bf16[144,1152]{1,0:T(8,128)(2,1)}, u32[]{:S(2)}) copy-start(bf16[144,1152]{1,0:T(8,128)(2,1)} %copy-done.13) | copy-start | bytes 995332
  61.7 18.1 %collective-permute-start.9 = (bf16[256,1344]{0,1:T(8,128)(2,1)}, bf16[256,1344]{0,1:T(8,128)(2,1)S(1)}, u32[]{:S(2)}, u32[]{:S(2)}) collective-permute-start(bf16[256,1344]{0,1:T(8,128)(2,1)} %copy.28), channel_id=1, source_target_pairs={{0,2},{2,0},{1,3},{3,1},{4,6},{6,4},{5,7},{7,5},{8,10},{10,8},{9,1... | collective-permute-start | bytes 2064392 | tf_op jit(solution)/shard_map/ppermute | solution.py:70
  65.6 42.2 %collective-permute-start.8 = (bf16[384,1536]{1,0:T(8,128)(2,1)}, bf16[384,1536]{1,0:T(8,128)(2,1)}, u32[]{:S(2)}, u32[]{:S(2)}) collective-permute-start(bf16[384,1536]{1,0:T(8,128)(2,1)} %pad_maximum_fusion.4), channel_id=1, source_target_pairs={{0,1},{1,0},{2,3},{3,2},{4,5},{5,4},{6,7},{7,6},{8,9},{9,8},{10,11... | collective-permute-start | bytes 3538952 | tf_op jit(solution)/shard_map/ppermute | solution.py:110
  65.8 55.0 %collective-permute-start = (bf16[256,1280]{1,0:T(8,128)(2,1)S(1)}, bf16[256,1280]{1,0:T(8,128)(2,1)}, u32[]{:S(2)}, u32[]{:S(2)}) collective-permute-start(bf16[256,1280]{1,0:T(8,128)(2,1)S(1)} %copy-done.7), channel_id=1, source_target_pairs={{0,12},{4,0},{8,4},{12,8},{1,13},{5,1},{9,5},{13,9},{2,14},{6,2},{... | collective-permute-start | bytes 1966088 | tf_op jit(solution)/shard_map/ppermute | solution.py:70
  79.8 2.6 %copy-start.21 = (bf16[256,1344]{0,1:T(8,128)(2,1)}, bf16[256,1344]{0,1:T(8,128)(2,1)S(1)}, u32[]{:S(2)}) copy-start(bf16[256,1344]{0,1:T(8,128)(2,1)S(1)} %collective-permute-done.9) | copy-start | bytes 2064388
  79.8 46.0 %collective-permute-start.1 = (bf16[256,1280]{1,0:T(8,128)(2,1)S(1)}, bf16[256,1280]{1,0:T(8,128)(2,1)}, u32[]{:S(2)}, u32[]{:S(2)}) collective-permute-start(bf16[256,1280]{1,0:T(8,128)(2,1)S(1)} %copy-done.7), channel_id=1, source_target_pairs={{0,8},{4,12},{8,0},{12,4},{1,9},{5,13},{9,1},{13,5},{2,10},{6,14},... | collective-permute-start | bytes 1966088 | tf_op jit(solution)/shard_map/ppermute | solution.py:70
  85.3 40.5 %collective-permute-start.2 = (bf16[256,1280]{1,0:T(8,128)(2,1)S(1)}, bf16[256,1280]{1,0:T(8,128)(2,1)}, u32[]{:S(2)}, u32[]{:S(2)}) collective-permute-start(bf16[256,1280]{1,0:T(8,128)(2,1)S(1)} %copy-done.7), channel_id=1, source_target_pairs={{0,4},{4,8},{8,12},{12,0},{1,5},{5,9},{9,13},{13,1},{2,6},{6,10},{... | collective-permute-start | bytes 1966088 | tf_op jit(solution)/shard_map/ppermute | solution.py:70
  90.2 2.3 copy-start.15
  91.1 1.5 slice-start
  99.0 5.4 %copy-start.22 = (bf16[256,768]{1,0:T(8,128)(2,1)S(1)}, bf16[256,768]{1,0:T(8,128)(2,1)}, u32[]{:S(2)}) copy-start(bf16[256,768]{1,0:T(8,128)(2,1)} %copy.39) | copy-start | bytes 1179652
  104.5 3.4 %copy-start.11 = (bf16[192,1536]{1,0:T(8,128)(2,1)S(1)}, bf16[192,1536]{1,0:T(8,128)(2,1)}, u32[]{:S(2)}) copy-start(bf16[192,1536]{1,0:T(8,128)(2,1)} %get-tuple-element.54) | copy-start | bytes 1769476
  104.5 3.4 %copy-start.12 = (bf16[192,1536]{1,0:T(8,128)(2,1)S(1)}, bf16[192,1536]{1,0:T(8,128)(2,1)}, u32[]{:S(2)}) copy-start(bf16[192,1536]{1,0:T(8,128)(2,1)} %get-tuple-element.55) | copy-start | bytes 1769476
  107.8 1.9 copy-start.20
  111.8 2.3 copy-start.27
  116.9 13.6 %collective-permute-start.18 = (bf16[4,160,1344]{2,1,0:T(8,128)(2,1)S(1)}, bf16[4,160,1344]{2,1,0:T(8,128)(2,1)S(1)}, u32[]{:S(2)}, u32[]{:S(2)}) collective-permute-start(bf16[4,160,1344]{2,1,0:T(8,128)(2,1)S(1)} %fusion.9), channel_id=1, source_target_pairs={{0,1},{1,0},{2,3},{3,2},{4,5},{5,4},{6,7},{7,6},{8,9},{9,8},{10,11... | collective-permute-start | bytes 5160968 | tf_op jit(solution)/shard_map/ppermute | solution.py:70
  118.5 1.5 copy-start.19
  118.7 12.4 %collective-permute-start.15 = (bf16[4,336,768]{2,1,0:T(8,128)(2,1)S(1)}, bf16[4,336,768]{2,1,0:T(8,128)(2,1)S(1)}, u32[]{:S(2)}, u32[]{:S(2)}) collective-permute-start(bf16[4,336,768]{2,1,0:T(8,128)(2,1)S(1)} %dynamic-slice_bitcast_fusion), channel_id=1, source_target_pairs={{0,1},{1,0},{2,3},{3,2},{4,5},{5,4},{6,7},{7,6},{8,9},{9,8},{10,11... | collective-permute-start | bytes 6193160 | tf_op jit(solution)/shard_map/ppermute | solution.py:70
  120.9 9.0 %collective-permute-start.14 = (bf16[128,1280]{1,0:T(8,128)(2,1)S(1)}, bf16[128,1280]{1,0:T(8,128)(2,1)S(1)}, u32[]{:S(2)}, u32[]{:S(2)}) collective-permute-start(bf16[128,1280]{1,0:T(8,128)(2,1)S(1)} %constant_dynamic-slice_fusion), channel_id=1, source_target_pairs={{0,2},{2,0},{1,3},{3,1},{4,6},{6,4},{5,7},{7,5},{8,10},{10,8},{9,1... | collective-permute-start | bytes 983048 | tf_op jit(solution)/shard_map/ppermute | solution.py:70
  122.4 7.5 %copy-start.3 = (f32[256,1280]{1,0:T(8,128)S(1)}, f32[256,1280]{1,0:T(8,128)}, u32[]{:S(2)}) copy-start(f32[256,1280]{1,0:T(8,128)} %copy-done.2) | copy-start | bytes 3932164
  130.6 47.7 %slice-start.1 = ((s8[6553600]{0:T(1024)(128)(4,1)}), s8[4194304]{0:T(1024)(128)(4,1)S(1)}, s32[]{:S(2)}) async-start(s8[6553600]{0:T(1024)(128)(4,1)} %bitcast.108), calls=%async_computation.2 | async-start | bytes 8388608
  131.0 47.2 %slice-start.2 = ((s8[6553600]{0:T(1024)(128)(4,1)}), s8[2359296]{0:T(1024)(128)(4,1)S(1)}, s32[]{:S(2)}) async-start(s8[6553600]{0:T(1024)(128)(4,1)} %bitcast.108), calls=%async_computation.3 | async-start | bytes 4718592
  131.7 8.1 %collective-permute-start.19 = (bf16[128,1280]{1,0:T(8,128)(2,1)S(1)}, bf16[128,1280]{1,0:T(8,128)(2,1)S(1)}, u32[]{:S(2)}, u32[]{:S(2)}) collective-permute-start(bf16[128,1280]{1,0:T(8,128)(2,1)S(1)} %multiply_convert_fusion.5), channel_id=1, source_target_pairs={{0,2},{2,0},{1,3},{3,1},{4,6},{6,4},{5,7},{7,5},{8,10},{10,8},{9,1... | collective-permute-start | bytes 983048 | tf_op jit(solution)/shard_map/ppermute | solution.py:70
  133.2 42.3 %collective-permute-start.16 = (bf16[128,1280]{1,0:T(8,128)(2,1)S(1)}, bf16[128,1280]{1,0:T(8,128)(2,1)S(1)}, u32[]{:S(2)}, u32[]{:S(2)}) collective-permute-start(bf16[128,1280]{1,0:T(8,128)(2,1)S(1)} %multiply_convert_fusion.5), channel_id=1, source_target_pairs={{0,12},{4,0},{8,4},{12,8},{1,13},{5,1},{9,5},{13,9},{2,14},{6,2},{... | collective-permute-start | bytes 983048 | tf_op jit(solution)/shard_map/ppermute | solution.py:70
  136.1 37.3 %collective-permute-start.21 = (bf16[128,1280]{1,0:T(8,128)(2,1)S(1)}, bf16[128,1280]{1,0:T(8,128)(2,1)S(1)}, u32[]{:S(2)}, u32[]{:S(2)}) collective-permute-start(bf16[128,1280]{1,0:T(8,128)(2,1)S(1)} %multiply_convert_fusion.5), channel_id=1, source_target_pairs={{0,8},{4,12},{8,0},{12,4},{1,9},{5,13},{9,1},{13,5},{2,10},{6,14},... | collective-permute-start | bytes 983048 | tf_op jit(solution)/shard_map/ppermute | solution.py:70
  136.1 38.7 %collective-permute-start.23 = (bf16[128,1280]{1,0:T(8,128)(2,1)S(1)}, bf16[128,1280]{1,0:T(8,128)(2,1)S(1)}, u32[]{:S(2)}, u32[]{:S(2)}) collective-permute-start(bf16[128,1280]{1,0:T(8,128)(2,1)S(1)} %multiply_convert_fusion.5), channel_id=1, source_target_pairs={{0,4},{4,8},{8,12},{12,0},{1,5},{5,9},{9,13},{13,1},{2,6},{6,10},{... | collective-permute-start | bytes 983048 | tf_op jit(solution)/shard_map/ppermute | solution.py:70
  136.8 38.7 %collective-permute-start.17 = (bf16[336,768]{1,0:T(8,128)(2,1)S(1)}, bf16[336,768]{1,0:T(8,128)(2,1)S(1)}, u32[]{:S(2)}, u32[]{:S(2)}) collective-permute-start(bf16[336,768]{1,0:T(8,128)(2,1)S(1)} %dynamic-slice_bitcast_fusion.1), channel_id=1, source_target_pairs={{0,4},{4,8},{8,12},{12,0},{1,5},{5,9},{9,13},{13,1},{2,6},{6,10},{... | collective-permute-start | bytes 1548296 | tf_op jit(solution)/shard_map/ppermute | solution.py:70
  173.4 21.8 %collective-permute-start.22 = (bf16[128,1280]{1,0:T(8,128)(2,1)S(1)}, bf16[128,1280]{1,0:T(8,128)(2,1)S(1)}, u32[]{:S(2)}, u32[]{:S(2)}) collective-permute-start(bf16[128,1280]{1,0:T(8,128)(2,1)S(1)} %collective-permute-done.21), channel_id=1, source_target_pairs={{0,2},{2,0},{1,3},{3,1},{4,6},{6,4},{5,7},{7,5},{8,10},{10,8},{9,1... | collective-permute-start | bytes 983048 | tf_op jit(solution)/shard_map/ppermute | solution.py:70
  174.8 20.6 %collective-permute-start.24 = (bf16[128,1280]{1,0:T(8,128)(2,1)S(1)}, bf16[128,1280]{1,0:T(8,128)(2,1)S(1)}, u32[]{:S(2)}, u32[]{:S(2)}) collective-permute-start(bf16[128,1280]{1,0:T(8,128)(2,1)S(1)} %collective-permute-done.23), channel_id=1, source_target_pairs={{0,2},{2,0},{1,3},{3,1},{4,6},{6,4},{5,7},{7,5},{8,10},{10,8},{9,1... | collective-permute-start | bytes 983048 | tf_op jit(solution)/shard_map/ppermute | solution.py:70
  175.6 34.1 %collective-permute-start.30 = (bf16[336,768]{1,0:T(8,128)(2,1)S(1)}, bf16[336,768]{1,0:T(8,128)(2,1)S(1)}, u32[]{:S(2)}, u32[]{:S(2)}) collective-permute-start(bf16[336,768]{1,0:T(8,128)(2,1)S(1)} %fusion.39), channel_id=1, source_target_pairs={{0,4},{4,8},{8,12},{12,0},{1,5},{5,9},{9,13},{13,1},{2,6},{6,10},{... | collective-permute-start | bytes 1548296 | tf_op jit(solution)/shard_map/ppermute | solution.py:70
  175.6 33.8 %collective-permute-start.27 = (bf16[160,1344]{1,0:T(8,128)(2,1)S(1)}, bf16[160,1344]{1,0:T(8,128)(2,1)S(1)}, u32[]{:S(2)}, u32[]{:S(2)}) collective-permute-start(bf16[160,1344]{1,0:T(8,128)(2,1)S(1)} %dynamic-slice_bitcast_fusion.2), channel_id=1, source_target_pairs={{0,4},{4,8},{8,12},{12,0},{1,5},{5,9},{9,13},{13,1},{2,6},{6,10},{... | collective-permute-start | bytes 1290248 | tf_op jit(solution)/shard_map/ppermute | solution.py:70
  177.1 17.9 %collective-permute-start.20 = (bf16[128,1280]{1,0:T(8,128)(2,1)S(1)}, bf16[128,1280]{1,0:T(8,128)(2,1)S(1)}, u32[]{:S(2)}, u32[]{:S(2)}) collective-permute-start(bf16[128,1280]{1,0:T(8,128)(2,1)S(1)} %collective-permute-done.16), channel_id=1, source_target_pairs={{0,2},{2,0},{1,3},{3,1},{4,6},{6,4},{5,7},{7,5},{8,10},{10,8},{9,1... | collective-permute-start | bytes 983048 | tf_op jit(solution)/shard_map/ppermute | solution.py:70
  188.4 7.2 %copy-start.28 = (bf16[768,2560]{1,0:T(8,128)(2,1)}, bf16[768,2560]{1,0:T(8,128)(2,1)S(1)}, u32[]{:S(2)}) copy-start(bf16[768,2560]{1,0:T(8,128)(2,1)S(1)} %get-tuple-element.46) | copy-start | bytes 11796484
  196.5 1.9 copy-start.32
  198.3 41.6 %collective-permute-start.26 = (bf16[2560,160]{0,1:T(8,128)(2,1)S(1)}, bf16[2560,160]{0,1:T(8,128)(2,1)S(1)}, u32[]{:S(2)}, u32[]{:S(2)}) collective-permute-start(bf16[2560,160]{0,1:T(8,128)(2,1)S(1)} %convolution_convert_fusion), channel_id=1, source_target_pairs={{0,1},{1,0},{2,3},{3,2},{4,5},{5,4},{6,7},{7,6},{8,9},{9,8},{10,11... | collective-permute-start | bytes 2457608 | tf_op jit(solution)/shard_map/ppermute | solution.py:70
  209.6 15.0 %collective-permute-start.28 = (bf16[160,1344]{1,0:T(8,128)(2,1)S(1)}, bf16[160,1344]{1,0:T(8,128)(2,1)S(1)}, u32[]{:S(2)}, u32[]{:S(2)}) collective-permute-start(bf16[160,1344]{1,0:T(8,128)(2,1)S(1)} %fusion.41), channel_id=1, source_target_pairs={{0,4},{4,8},{8,12},{12,0},{1,5},{5,9},{9,13},{13,1},{2,6},{6,10},{... | collective-permute-start | bytes 1290248 | tf_op jit(solution)/shard_map/ppermute | solution.py:70
  209.8 25.8 %collective-permute-start.31 = (bf16[336,768]{1,0:T(8,128)(2,1)S(1)}, bf16[336,768]{1,0:T(8,128)(2,1)S(1)}, u32[]{:S(2)}, u32[]{:S(2)}) collective-permute-start(bf16[336,768]{1,0:T(8,128)(2,1)S(1)} %fusion.38), channel_id=1, source_target_pairs={{0,4},{4,8},{8,12},{12,0},{1,5},{5,9},{9,13},{13,1},{2,6},{6,10},{... | collective-permute-start | bytes 1548296 | tf_op jit(solution)/shard_map/ppermute | solution.py:70
  211.3 26.1 %collective-permute-start.25 = (bf16[160,2560]{1,0:T(8,128)(2,1)S(1)}, bf16[160,2560]{1,0:T(8,128)(2,1)S(1)}, u32[]{:S(2)}, u32[]{:S(2)}) collective-permute-start(bf16[160,2560]{1,0:T(8,128)(2,1)S(1)} %convolution_convert_fusion.1), channel_id=1, source_target_pairs={{0,1},{1,0},{2,3},{3,2},{4,5},{5,4},{6,7},{7,6},{8,9},{9,8},{10,11... | collective-permute-start | bytes 2457608 | tf_op jit(solution)/shard_map/ppermute | solution.py:70
  224.7 20.2 %collective-permute-start.29 = (bf16[160,1344]{1,0:T(8,128)(2,1)S(1)}, bf16[160,1344]{1,0:T(8,128)(2,1)S(1)}, u32[]{:S(2)}, u32[]{:S(2)}) collective-permute-start(bf16[160,1344]{1,0:T(8,128)(2,1)S(1)} %fusion.40), channel_id=1, source_target_pairs={{0,4},{4,8},{8,12},{12,0},{1,5},{5,9},{9,13},{13,1},{2,6},{6,10},{... | collective-permute-start | bytes 1290248 | tf_op jit(solution)/shard_map/ppermute | solution.py:70
  237.4 2.5 %copy-start.29 = (bf16[768,2560]{1,0:T(8,128)(2,1)S(1)}, bf16[768,2560]{1,0:T(8,128)(2,1)}, u32[]{:S(2)}) copy-start(bf16[768,2560]{1,0:T(8,128)(2,1)} %copy-done.28) | copy-start | bytes 11796484
  239.9 6.7 %copy-start.1 = (bf16[768,1536]{1,0:T(8,128)(2,1)S(1)}, bf16[768,1536]{1,0:T(8,128)(2,1)}, u32[]{:S(2)}) copy-start(bf16[768,1536]{1,0:T(8,128)(2,1)} %param.18) | copy-start | bytes 7077892
  (7 other events, 8.9 us)

commit v3 on v1

v3 whole, which is shorter than its diff:
```python
import math

import jax
import jax.numpy as jnp
from jax import lax
from jax.experimental import pallas as pl
from jax.experimental.pallas import tpu as pltpu
from jax.sharding import PartitionSpec as P

EPS = 1e-06
ROOT = math.sqrt(2.0 / math.pi)
CUBE = 0.044715


def layer_norm(values, gain):
    center = values - jnp.mean(values, axis=-1, keepdims=True)
    spread = jnp.mean(center * center, axis=-1, keepdims=True)
    return center * lax.rsqrt(spread + EPS) * gain


def norm_back(values, gain, upstream):
    center = values - jnp.mean(values, axis=-1, keepdims=True)
    recip = lax.rsqrt(jnp.mean(center * center, axis=-1, keepdims=True) + EPS)
    unit = center * recip
    scaled = upstream * gain
    return recip * (
        scaled
        - jnp.mean(scaled, axis=-1, keepdims=True)
        - unit * jnp.mean(scaled * unit, axis=-1, keepdims=True)
    )


def gelu_and_slope(values):
    square = values * values
    bend = jnp.tanh(ROOT * values * (1.0 + CUBE * square))
    half = 0.5 * (1.0 + bend)
    slope = half + 0.5 * values * (1.0 - bend * bend) * (ROOT * (1.0 + 3.0 * CUBE * square))
    return (values * half).astype(jnp.bfloat16), slope.astype(jnp.bfloat16)


def tiles(count, step=256):
    return [(at, min(at + step, count)) for at in range(0, count, step)]


def in_vmem(count):
    return [pl.BlockSpec(memory_space=pltpu.VMEM)] * count


def row_dot(left, right):
    return lax.dot_general(
        left, right, (((1,), (1,)), ((), ())), preferred_element_type=jnp.float32
    )


def params(flops, nbytes, room=8):
    return dict(
        compiler_params=pltpu.CompilerParams(vmem_limit_bytes=room * 1024 * 1024),
        cost_estimate=pl.CostEstimate(flops=flops, bytes_accessed=nbytes, transcendentals=0),
    )


def mlp_forward(resid, gain, w_in, w_out):
    rows, width = resid.shape
    units = w_in.shape[1]
    tile = next(t for t in (512, 256, 128, units) if units % t == 0)
    steps = units // tile

    def kernel(resid_ref, gain_ref, w_in_hbm, w_out_hbm, normed_ref, hid_ref, slope_ref, out_ref, w_in_ref, w_out_ref, total, in_sem, out_sem):
        def copies(at):
            cut = pl.ds(at * tile, tile)
            return (
                pltpu.make_async_copy(w_in_hbm.at[:, cut], w_in_ref.at[:, cut], in_sem.at[at]),
                pltpu.make_async_copy(w_out_hbm.at[cut, :], w_out_ref.at[cut, :], out_sem.at[at]),
            )

        for at in range(steps):
            for copy in copies(at):
                copy.start()
        normed_ref[...] = layer_norm(resid_ref[...].astype(jnp.float32), gain_ref[...]).astype(jnp.bfloat16)
        for at in range(steps):
            lo, hi = at * tile, (at + 1) * tile
            into, out_of = copies(at)
            into.wait()
            for left, right in tiles(tile):
                hidden, slope = gelu_and_slope(matmul(normed_ref[...], w_in_ref[:, lo + left : lo + right]))
                hid_ref[:, lo + left : lo + right] = hidden
                slope_ref[:, lo + left : lo + right] = slope
            out_of.wait()
            for left, right in tiles(width):
                value = matmul(hid_ref[:, lo:hi], w_out_ref[lo:hi, left:right])
                if at:
                    value = value + total[:, left:right]
                if at < steps - 1:
                    total[:, left:right] = value
                else:
                    out_ref[:, left:right] = value.astype(jnp.bfloat16)

    shape = lambda *dims: jax.ShapeDtypeStruct(dims, jnp.bfloat16)
    return pl.pallas_call(
        kernel,
        in_specs=in_vmem(2) + [pl.BlockSpec(memory_space=pltpu.HBM)] * 2,
        out_specs=in_vmem(4),
        out_shape=[shape(rows, width), shape(rows, units), shape(rows, units), shape(rows, width)],
        scratch_shapes=[
            pltpu.VMEM((width, units), jnp.bfloat16),
            pltpu.VMEM((units, width), jnp.bfloat16),
            pltpu.VMEM((rows, width), jnp.float32),
            pltpu.SemaphoreType.DMA((steps,)),
            pltpu.SemaphoreType.DMA((steps,)),
        ],
        **params(4 * rows * width * units, 4 * width * units, 54),
    )(resid, gain.reshape(1, -1), w_in, w_out)


def route_features(info, owner, own, peer):
    images, patches, _ = own[0].shape
    n_chips = images // 2
    channels = 2 * sum(part.shape[2] for part in own)

    def kernel(info_ref, owner_ref, own_d, own_s, peer_d, peer_s, mine_ref, theirs_ref):
        core, chip, first = info_ref[0], info_ref[1], info_ref[2] == 0

        def one(image, carry):
            to = owner_ref[image]
            place = lax.rem(to // 2 - chip + n_chips, n_chips)
            pieces = []
            for here, there in ((own_d, peer_d), (own_s, peer_s)):
                a, b = here[image], there[image]
                pieces += [jnp.where(first, a, b), jnp.where(first, b, a)]
            joined = jnp.concatenate(pieces, axis=-1)

            @pl.when(lax.rem(to, 2) == core)
            def _():
                mine_ref[place] = joined

            @pl.when(lax.rem(to, 2) != core)
            def _():
                theirs_ref[place] = joined

            return carry

        lax.fori_loop(0, images, one, 0)

    return pl.pallas_call(
        kernel,
        in_specs=[pl.BlockSpec(memory_space=pltpu.SMEM)] * 2 + in_vmem(4),
        out_specs=in_vmem(2),
        out_shape=[jax.ShapeDtypeStruct((n_chips, patches, channels), jnp.bfloat16)] * 2,
        **params(images * patches * channels, 4 * images * patches * channels),
    )(info, owner, *own, *peer)


def pair_up(mine, theirs):
    n_chips, patches, channels = mine.shape

    def kernel(mine_ref, theirs_ref, *refs):
        for at, ref in enumerate(refs):
            ref[0] = mine_ref[at]
            ref[1] = theirs_ref[at]

    return pl.pallas_call(
        kernel,
        in_specs=in_vmem(2),
        out_specs=in_vmem(n_chips),
        out_shape=[jax.ShapeDtypeStruct((2, patches, channels), jnp.bfloat16)] * n_chips,
        **params(n_chips * patches * channels, 8 * n_chips * patches * channels),
    )(mine, theirs)


def adaptors_forward(resid, addends, gain, a_dino, a_sig, b_dino, b_sig):
    rows, width = resid.shape
    count = len(addends)
    wide, narrow = a_dino.shape[1], a_sig.shape[0]

    def kernel(resid_ref, gain_ref, ad_ref, as_ref, bd_ref, bs_ref, *refs):
        stream = resid_ref[...].astype(jnp.float32)
        added = refs[0][...].astype(jnp.float32)
        for ref in refs[1:count]:
            added = added + ref[...].astype(jnp.float32)
        stream = stream + added
        stream_ref, summary_ref, act_ref, slope_ref, pred_d, pred_s = refs[count:]
        stream_ref[...] = stream
        summary_ref[...] = layer_norm(stream, gain_ref[...]).astype(jnp.bfloat16)
        for lo, hi in tiles(narrow):
            act, slope = gelu_and_slope(row_dot(summary_ref[...], as_ref[lo:hi, :]))
            act_ref[:, wide + lo : wide + hi] = act
            slope_ref[:, wide + lo : wide + hi] = slope
        for lo, hi in tiles(bs_ref.shape[1]):
            pred_s[:, lo:hi] = matmul(act_ref[:, wide:], bs_ref[:, lo:hi]).astype(jnp.bfloat16)
        for lo, hi in tiles(wide):
            act, slope = gelu_and_slope(matmul(summary_ref[...], ad_ref[:, lo:hi]))
            act_ref[:, lo:hi] = act
            slope_ref[:, lo:hi] = slope
        for lo, hi in tiles(bd_ref.shape[1]):
            pred_d[:, lo:hi] = matmul(act_ref[:, :wide], bd_ref[:, lo:hi]).astype(jnp.bfloat16)

    shape = lambda cols, dtype=jnp.bfloat16: jax.ShapeDtypeStruct((rows, cols), dtype)
    work = width * (wide + narrow) + b_dino.size + b_sig.size
    return pl.pallas_call(
        kernel,
        in_specs=in_vmem(6 + count),
        out_specs=in_vmem(6),
        out_shape=[
            shape(width, jnp.float32),
            shape(width),
            shape(wide + narrow),
            shape(wide + narrow),
            shape(b_dino.shape[1]),
            shape(b_sig.shape[1]),
        ],
        **params(2 * rows * work, 2 * work),
    )(resid, gain.reshape(1, -1), a_dino, a_sig, b_dino, b_sig, *addends)


def loss_rows(info_ref, addends, targets, start, back_ref, factor):
    rows, channels = back_ref.shape
    core, chip = info_ref[0], info_ref[1]
    n_from, patches = len(targets), targets[0].shape[-2]

    def block(here, goal):
        goal = goal.astype(jnp.float32)
        value = addends[0][here, :].astype(jnp.float32)
        for ref in addends[1:]:
            value = value + ref[here, :].astype(jnp.float32)
        norm_pred = jnp.sum(value * value, axis=-1, keepdims=True) + channels * EPS
        norm_target = jnp.sum(goal * goal, axis=-1, keepdims=True) + channels * EPS
        recip = lax.rsqrt(norm_pred * norm_target)
        cosine = jnp.sum(value * goal, axis=-1, keepdims=True) * recip
        of_pred = factor * (1.0 + channels * (cosine / norm_pred))
        of_target = factor * (1.0 + channels * recip)
        back_ref[here, :] = (value * of_pred - goal * of_target).astype(jnp.bfloat16)

    for at, ref in enumerate(targets):
        if len(ref.shape) == 2:
            for lo, hi in tiles(rows, 32):
                block(slice(lo, hi), ref[lo:hi, start : start + channels])
            continue
        source = lax.rem(chip - at + n_from, n_from)
        for other in range(2):
            place = 2 * source + (1 - core if other else core)
            here = pl.ds(pl.multiple_of(place * patches, patches), patches)
            block(here, ref[other, :, start : start + channels])


def loss_gradient(info, addends, targets, start, factor):
    rows, channels = addends[0].shape
    count = len(addends)

    def kernel(info_ref, *refs):
        loss_rows(info_ref, refs[:count], refs[count:-1], start, refs[-1], factor)

    return pl.pallas_call(
        kernel,
        in_specs=[pl.BlockSpec(memory_space=pltpu.SMEM)] + in_vmem(count + len(targets)),
        out_specs=pl.BlockSpec(memory_space=pltpu.VMEM),
        out_shape=jax.ShapeDtypeStruct((rows, channels), jnp.bfloat16),
        **params(20 * rows * channels, 8 * rows * channels),
    )(info, *addends, *targets)


def adaptors_back(info, addends, targets, back_s, b_weights, slope, a_weights, factor):
    rows, channels = addends[0].shape
    width = a_weights[0].shape[0]
    units = [w.shape[0] for w in b_weights]
    count = len(addends) + len(targets)

    def kernel(info_ref, *refs):
        back_s, b_d, b_s, slope_ref, a_d, a_s, back_d, down_ref, part_ref = refs[count:]
        loss_rows(info_ref, refs[: len(addends)], refs[len(addends) : count], 0, back_d, factor)
        start = 0
        for back, weights in ((back_d, b_d), (back_s, b_s)):
            for lo, hi in tiles(weights.shape[0]):
                grown = row_dot(back[...], weights[lo:hi, :])
                down = slope_ref[:, start + lo : start + hi].astype(jnp.float32) * grown
                down_ref[:, start + lo : start + hi] = down.astype(jnp.bfloat16)
            start += weights.shape[0]
        for lo, hi in tiles(width):
            total = row_dot(down_ref[:, : units[0]], a_d[lo:hi, :])
            total = total + matmul(down_ref[:, units[0] :], a_s[:, lo:hi])
            part_ref[:, lo:hi] = total.astype(jnp.bfloat16)

    work = sum(u * (w.shape[1] + width) for u, w in zip(units, b_weights))
    shape = lambda cols: jax.ShapeDtypeStruct((rows, cols), jnp.bfloat16)
    return pl.pallas_call(
        kernel,
        in_specs=[pl.BlockSpec(memory_space=pltpu.SMEM)] + in_vmem(count + 6),
        out_specs=in_vmem(3),
        out_shape=[shape(channels), shape(sum(units)), shape(width)],
        **params(2 * rows * work, 2 * work),
    )(info, *addends, *targets, back_s, *b_weights, slope, *a_weights)


def gradient_blocks(core, pairs, n_blocks):
    rows = pairs[0][0].shape[0]
    depths = [left.shape[1] // n_blocks for left, _, _ in pairs]
    depth = max(depths)
    widths = [cols.stop - cols.start for _, _, cols in pairs]
    count = len(pairs)

    def kernel(core_ref, *refs):
        own = core_ref[0]
        mine_ref, theirs_ref = refs[2 * count :]

        def put(value, at, per, start):
            row = at
            while row < at + value.shape[0]:
                block, inside = row // per, row % per
                stop = min(at + value.shape[0], (block + 1) * per)
                piece = value[row - at : stop - at]
                place = (block // 2, slice(inside, inside + stop - row), slice(start, start + value.shape[1]))

                @pl.when(own == block % 2)
                def _():
                    mine_ref[place] = piece

                @pl.when(own != block % 2)
                def _():
                    theirs_ref[place] = piece

                row = stop

        start = 0
        for at, (per, width) in enumerate(zip(depths, widths)):
            left, right, cols = refs[2 * at], refs[2 * at + 1], pairs[at][2]
            if per < depth:
                blank = jnp.zeros((n_blocks // 2, depth - per, width), jnp.bfloat16)
                mine_ref[:, per:, start : start + width] = blank
                theirs_ref[:, per:, start : start + width] = blank
            for lo, hi in tiles(left.shape[1]):
                value = lax.dot_general(
                    left[:, lo:hi], right[:, cols], (((0,), (0,)), ((), ())), preferred_element_type=jnp.float32
                )
                put(value.astype(jnp.bfloat16), lo, per, start)
            start += width

    work = rows * sum(left.shape[1] * width for (left, _, _), width in zip(pairs, widths))
    return pl.pallas_call(
        kernel,
        in_specs=[pl.BlockSpec(memory_space=pltpu.SMEM)] + in_vmem(2 * count),
        out_specs=in_vmem(2),
        out_shape=[jax.ShapeDtypeStruct((n_blocks // 2, depth, sum(widths)), jnp.bfloat16)] * 2,
        **params(2 * work, 2 * n_blocks * depth * sum(widths)),
    )(core.astype(jnp.int32).reshape(1), *[array for pair in pairs for array in pair[:2]])


def matmul(left, right):
    return jnp.dot(left, right, preferred_element_type=jnp.float32)


def contract_rows(left, right):
    return lax.dot_general(
        left, right, (((0,), (0,)), ((), ())), preferred_element_type=jnp.float32
    )


def contract_cols(left, right):
    return lax.dot_general(
        left, right, (((1,), (1,)), ((), ())), preferred_element_type=jnp.float32
    )


def shift(values, axis, by=1):
    count = lax.axis_size(axis)
    return lax.ppermute(values, axis, [(i, (i + by) % count) for i in range(count)])


def addends_mp(part):
    if lax.axis_size("mp") == 2:
        return (part, shift(part, "mp"))
    return (lax.psum(part, "mp"),)


def in_order(own, other, axis):
    first = lax.axis_index("mp") == 0
    return jnp.concatenate(
        [jnp.where(first, own, other), jnp.where(first, other, own)], axis=axis
    )


def tie(*values):
    return lax.optimization_barrier(values)


def back_rows(place, stream, part, other, gain):
    half, width = other.shape

    def kernel(place_ref, stream_ref, part_ref, other_ref, gain_ref, back_ref):
        here = pl.ds(pl.multiple_of(place_ref[0] * half, half), half)
        upstream = part_ref[here, :].astype(jnp.float32) + other_ref[...].astype(jnp.float32)
        back_ref[...] = norm_back(stream_ref[here, :], gain_ref[...], upstream).astype(jnp.bfloat16)

    return pl.pallas_call(
        kernel,
        in_specs=[pl.BlockSpec(memory_space=pltpu.SMEM)] + in_vmem(4),
        out_specs=pl.BlockSpec(memory_space=pltpu.VMEM),
        out_shape=jax.ShapeDtypeStruct((half, width), jnp.bfloat16),
        **params(20 * half * width, 12 * half * width),
    )(place, stream, part, other, gain.reshape(1, -1))


def whole_rows(held):
    return in_order(held, shift(held, "mp"), 0) if lax.axis_size("mp") == 2 else held


def per_device(
    resid,
    gain_mlp,
    gain_out,
    w_in,
    w_out,
    a_dino,
    b_dino,
    a_sig,
    b_sig,
    dino_feats,
    sig_feats,
    owner,
):
    n_chips = lax.axis_size("dp")
    n_cores = lax.axis_size("teach")
    width = resid.shape[2]
    rows = resid.shape[0] * resid.shape[1]
    factor = 1.0 / math.sqrt(n_chips * n_cores * rows)
    total_images = owner.shape[0]
    chip = lax.axis_index("dp")
    core = lax.axis_index("teach")

    two = lax.axis_size("mp") == 2
    resid = resid.reshape(rows, width)
    info = jnp.stack([core, chip, lax.axis_index("mp")]).astype(jnp.int32)
    feats = (dino_feats, sig_feats)
    if two:
        peers = [shift(part, "mp") for part in feats]
    ring_r = [shift(resid, "dp", -1)]
    normed, hidden, slope, out_part = mlp_forward(resid, gain_mlp, w_in, w_out)
    if two:
        *peers, out_part = tie(*peers, out_part)
    out_addends = addends_mp(out_part)
    if n_chips > 2:
        ring_r[0], out_part = tie(ring_r[0], out_part)
        ring_r.append(shift(ring_r[0], "dp", -1))
    if two:
        mine, theirs = route_features(info, owner, feats, peers)
        blocks = pair_up(mine, shift(theirs, "teach"))
        *blocks, arrived = tie(*blocks, out_addends[1])
        out_addends = (out_part, arrived)
        targets = [blocks[0]] + [shift(blocks[k], "dp", k) for k in range(1, n_chips)]
    else:
        images = jnp.arange(total_images, dtype=jnp.int32)
        inverse = jnp.sum(jnp.where(owner[None, :] == images[:, None], images[None, :], 0), axis=1)
        feats = [lax.all_gather(part, "mp", axis=2, tiled=True) for part in feats]
        sent = jnp.concatenate(feats, axis=2)
        sent = sent.at[inverse].get(mode="promise_in_bounds", unique_indices=True)
        got = lax.all_to_all(sent, ("dp", "teach"), split_axis=0, concat_axis=1, tiled=True)
        targets = [got.reshape(rows, -1)]

    a_sig_t = a_sig.T
    n_units = b_dino.shape[0]
    stream, summary, act, slope_t, pred_dino, pred_sig = adaptors_forward(
        resid, out_addends, gain_out, a_dino, a_sig_t, b_dino, b_sig
    )
    if n_chips > 2:
        ring_r[1], *_ = tie(ring_r[1], *targets, pred_dino)
    while len(ring_r) < n_chips - 1:
        ring_r.append(shift(ring_r[-1], "dp", -1))
    sig_addends, dino_addends = addends_mp(pred_sig), addends_mp(pred_dino)
    back_sig = loss_gradient(info, sig_addends, targets, b_dino.shape[1], factor)

    n_blocks = n_chips * n_cores
    cols_d, cols_s = slice(0, n_units), slice(n_units, n_units + b_sig.shape[0])
    back_dino, down, part = adaptors_back(
        info, dino_addends, targets, back_sig, (b_dino, b_sig), slope_t, (a_dino, a_sig_t), factor
    )
    ring_r[-1], part = tie(ring_r[-1], part)
    mine_b, theirs_b = gradient_blocks(core, [(back_dino, act, cols_d), (back_sig, act, cols_s)], n_blocks)
    if two:
        half = rows // 2
        place = lax.axis_index("mp").astype(jnp.int32).reshape(1)
        other = shift(lax.dynamic_slice_in_dim(part, (1 - place[0]) * half, half, 0), "mp")
        other, theirs_b = tie(other, theirs_b)
        back = back_rows(place, stream, part, other, gain_out)
    else:
        back = norm_back(stream, gain_out, addends_mp(part)[0].astype(jnp.float32)).astype(jnp.bfloat16)
    down, back = tie(down, back)
    mine_a, theirs_a = gradient_blocks(core, [(summary, down, slice(0, down.shape[1]))], n_blocks)

    def chip_block(sums, i):
        return lax.dynamic_index_in_dim(sums, lax.rem(i + 2 * n_chips, n_chips), 0, keepdims=False)

    def core_sum(mine, theirs):
        got = shift(theirs, "teach")
        return (mine.astype(jnp.float32) + got.astype(jnp.float32)).astype(jnp.bfloat16)

    def block(i):
        return jnp.concatenate([chip_block(chip_b, i), chip_block(chip_a, i)], axis=0)

    chip_b, chip_a = core_sum(mine_b, theirs_b), core_sum(mine_a, theirs_a)
    held = block(chip - 1)
    def add_block(got, step):
        total = got.astype(jnp.float32) + block(chip - 1 - step).astype(jnp.float32)
        return total, total.astype(jnp.bfloat16)

    held_s = [back, shift(back, "dp", -1)]
    held_s[1], held = tie(held_s[1], held)
    for step in range(2, n_chips):
        rows_in, sums_in = tie(shift(held_s[-1], "dp", -1), shift(held, "dp"))
        total, held = add_block(sums_in, step - 1)
        held_s.append(rows_in)
    total, held = add_block(shift(held, "dp"), n_chips - 1)
    total_b, total_a = total[: chip_b.shape[1]], total[chip_b.shape[1] :]
    backs = jnp.concatenate([whole_rows(rows_half) for rows_half in held_s], axis=0)
    depth_d, depth_s = (b.shape[1] // n_blocks for b in (b_dino, b_sig))
    out_a_d, out_a_s = total_a[:, cols_d], total_a[:, cols_s]
    out_b_d, out_b_s = total_b[:depth_d, cols_d].T, total_b[:depth_s, cols_s].T

    *others, _ = tie(*ring_r, held_s[1])
    others = jnp.concatenate(others, axis=0).astype(jnp.float32)
    others = layer_norm(others, gain_mlp).astype(jnp.bfloat16)
    normeds = jnp.concatenate([normed, others], axis=0)
    other_hidden, other_slope = gelu_and_slope(matmul(others, w_in))
    hiddens = jnp.concatenate([hidden, other_hidden], axis=0)
    slopes = jnp.concatenate([slope, other_slope], axis=0)
    back_hidden = (slopes * contract_cols(backs, w_out)).astype(jnp.bfloat16)
    share = width // (n_chips * n_cores)

    def shares(values):
        at = chip * n_cores + core
        own = lax.dynamic_slice_in_dim(values, at * share, share, 1)
        peer = chip * n_cores + (1 - core)
        return own, lax.dynamic_slice_in_dim(values, peer * share, share, 1)

    own_n, peer_n = shares(normeds)
    own_s, peer_s = shares(backs)
    sent_out = contract_rows(hiddens, peer_s).astype(jnp.bfloat16)
    got_out = shift(sent_out, "teach")
    sent_in = contract_rows(peer_n, back_hidden).astype(jnp.bfloat16)
    got_in = shift(sent_in, "teach")
    out_wo = contract_rows(hiddens, own_s) + got_out.astype(jnp.float32)
    out_wi = contract_rows(own_n, back_hidden) + got_in.astype(jnp.float32)
    return out_wi, out_wo, out_a_d, out_b_d, out_a_s, out_b_s


def solution(mesh):
    placed = (
        P(("groups", "dp", "teach"), None, None),
        P(),
        P(),
        P(None, "mp"),
        P("mp", None),
        P(None, "mp"),
        P("mp", None),
        P(None, "mp"),
        P("mp", None),
        P("groups", ("dp", "teach"), "mp"),
        P("groups", ("dp", "teach"), "mp"),
        P("groups"),
    )
    return jax.shard_map(
        per_device,
        mesh=mesh,
        in_specs=placed,
        out_specs=(
            P(("groups", "dp", "teach"), "mp"),
            P(("groups", "mp"), ("dp", "teach")),
            P(("groups", "dp", "teach"), "mp"),
            P(("groups", "mp"), ("dp", "teach")),
            P(("groups", "dp", "teach"), "mp"),
            P(("groups", "mp"), ("dp", "teach")),
        ),
        check_vma=False,
    )
```

time: 268 us -> 221 us (0.82)
  waiting for transfers between devices: 135 us -> 84.3 us
  Pallas kernels: 0 us -> 33.1 us
  matrix products: 62.2 us -> 29.9 us
  starting transfers between devices: 28.7 us -> 43.2 us
  other arithmetic: 22.9 us -> 11.7 us
    pallas_call x0 -> x9, Pallas kernels: none -> 33.1 us  [the longest x1 11.1 us: mlp_forward(): pl.pallas_call(kernel, in_specs=in_vmem(2) + [pl.BlockSpec(memory_space=p...]
    ppermute x26 -> x27, waiting for transfers between devices: 113 us -> 84.3 us  [shift(): lax.ppermute(values, axis, [(i, (i + by) % count) for i in range(count)])]
    ppermute x26 -> x27, starting transfers between devices: 20.4 us -> 43.2 us  [shift(): lax.ppermute(values, axis, [(i, (i + by) % count) for i in range(count)])]
    all_to_all x2 -> x0, waiting for transfers between devices: 21.9 us -> none  [own_teacher(): lax.all_to_all(sent, ('dp', 'teach'), split_axis=0, concat_axis=1, tiled=...]
    dot_general x7 -> x1, matrix products: 26.2 us -> 10.8 us  [matmul(): return jnp.dot(left, right, preferred_element_type=jnp.float32)]
    dot_general x8 -> x4, matrix products: 18.1 us -> 9.4 us  [contract_rows(): lax.dot_general(left, right, (((0,), (0,)), ((), ())), preferred_element_...]
    all_to_all x2 -> x0, starting transfers between devices: 8.33 us -> none  [own_teacher(): lax.all_to_all(sent, ('dp', 'teach'), split_axis=0, concat_axis=1, tiled=...]
    dot_general x5 -> x1, matrix products: 17.9 us -> 9.64 us  [contract_cols(): lax.dot_general(left, right, (((1,), (1,)), ((), ())), preferred_element_...]
  transfers between devices with their start and end apart: 28 -> 27, of which waited for: 13 -> 10; matrix products, arithmetic and copies ran while one was open for 31% -> 20% of each run, Pallas kernels for 0% -> 13%
where the time goes in v3:
time: 221 us
  waiting for transfers between devices  84.3 us (38%)
  starting transfers between devices  43.2 us (20%)
  Pallas kernels  33.1 us (15%)
  matrix products  29.9 us (14%)
  local copies, waits for them, and re-layouts  17.4 us (8%)
  other arithmetic  11.7 us (5%)
    ppermute x27, waiting for transfers between devices, shift(): lax.ppermute(values, axis, [(i, (i + by) % count) for i in range(count)])  84.3 us
    ppermute x27, starting transfers between devices, shift(): lax.ppermute(values, axis, [(i, (i + by) % count) for i in range(count)])  43.2 us
    unnamed x74, local copies, waits for them, and re-layouts  12.6 us
    pallas_call x1, Pallas kernels, mlp_forward(): pl.pallas_call(kernel, in_specs=in_vmem(2) + [pl.BlockSpec(memory_space=p...  11.1 us
    dot_general x1, matrix products, matmul(): return jnp.dot(left, right, preferred_element_type=jnp.float32)  10.8 us
    dot_general x1, matrix products, contract_cols(): lax.dot_general(left, right, (((1,), (1,)), ((), ())), preferred_element_...  9.64 us
    dot_general x4, matrix products, contract_rows(): lax.dot_general(left, right, (((0,), (0,)), ((), ())), preferred_element_...  9.4 us
    pallas_call x2, Pallas kernels, gradient_blocks(): pl.pallas_call(kernel, in_specs=[pl.BlockSpec(memory_space=pltpu.SMEM)] +...  8.78 us
  transfers between devices with their start and end apart: 27, of which 10 were waited for; matrix products, arithmetic and copies ran while one was open for 20% of the time, Pallas kernels for 13%

profile of v3, /device:TPU:0, one launch (start us, length us, event | category | flops | bytes accessed | tf_op | source)
XLA Modules:
  0.0 220.8 jit_solution(16043590067019089017)
XLA Ops:
  0.6 3.0 %collective-permute-start.2 = (bf16[8,32,576]{2,1,0:T(8,128)(2,1)}, bf16[8,32,576]{2,1,0:T(8,128)(2,1)S(1)}, u32[]{:S(2)}, u32[]{:S(2)}) collective-permute-start(bf16[8,32,576]{2,1,0:T(8,128)(2,1)} %own_s.1), channel_id=1, source_target_pairs={{0,2},{2,0},{1,3},{3,1},{4,6},{6,4},{5,7},{7,5},{8,10},{10,8},{9,1... | collective-permute-start | bytes 884744 | tf_op jit(solution)/shard_map/ppermute | solution.py:364
  3.7 4.1 %collective-permute-start = (bf16[256,1280]{1,0:T(8,128)(2,1)}, bf16[256,1280]{1,0:T(8,128)(2,1)}, u32[]{:S(2)}, u32[]{:S(2)}) collective-permute-start(bf16[256,1280]{1,0:T(8,128)(2,1)} %bitcast.33), channel_id=1, source_target_pairs={{0,12},{4,0},{8,4},{12,8},{1,13},{5,1},{9,5},{13,9},{2,14},{6,2},{... | collective-permute-start | bytes 1966088 | tf_op jit(solution)/shard_map/ppermute | solution.py:364
  7.8 1.3 reshape.39.gain_ref
  9.2 11.1 %shard_map.163 = (bf16[256,1280]{1,0:T(8,128)(2,1)}, bf16[256,2560]{1,0:T(8,128)(2,1)}, bf16[256,2560]{1,0:T(8,128)(2,1)}, bf16[256,1280]{1,0:T(8,128)(2,1)}) custom-call(bf16[256,1280]{1,0:T(8,128)(2,1)} %bitcast.34, f32[1,1280]{1,0:T(1,128)} %reshape.39.gain_ref, bf16[1280,2560]{1,0:T(8,128)(2,1)} %w_in_hbm.1, bf16[2560,1280]{1,0:T(8,128)(2,1)} %w_out_hbm.1), custom_call_target="tpu_custom_call" | custom-call | flops 3355443200 | bytes 13107200 | tf_op jit(solution)/shard_map/pallas_call | solution.py:99
  20.3 1.3 shard_map.164
  21.7 1.6 collective-permute-start.5
  23.3 3.5 %collective-permute-start.3 = (bf16[256,1280]{1,0:T(8,128)(2,1)}, bf16[256,1280]{1,0:T(8,128)(2,1)}, u32[]{:S(2)}, u32[]{:S(2)}) collective-permute-start(bf16[256,1280]{1,0:T(8,128)(2,1)} %collective-permute-done), channel_id=1, source_target_pairs={{0,12},{4,0},{8,4},{12,8},{1,13},{5,1},{9,5},{13,9},{2,14},{6,2},{... | collective-permute-start | bytes 1966088 | tf_op jit(solution)/shard_map/ppermute | solution.py:364
  26.9 12.2 %collective-permute-done.5.refs_1_ = bf16[256,1280]{1,0:T(8,128)(2,1)S(1)} collective-permute-done((bf16[256,1280]{1,0:T(8,128)(2,1)}, bf16[256,1280]{1,0:T(8,128)(2,1)S(1)}, u32[]{:S(2)}, u32[]{:S(2)}) %collective-permute-start.5) | collective-permute-done | bytes 655392 | tf_op jit(solution)/shard_map/ppermute | solution.py:364
  39.1 1.5 collective-permute-start.6
  40.6 2.6 %collective-permute-start.7 = (bf16[2,32,2688]{2,1,0:T(8,128)(2,1)S(1)}, bf16[2,32,2688]{2,1,0:T(8,128)(2,1)S(1)}, u32[]{:S(2)}, u32[]{:S(2)}) collective-permute-start(bf16[2,32,2688]{2,1,0:T(8,128)(2,1)S(1)} %get-tuple-element.69), channel_id=1, source_target_pairs={{0,8},{4,12},{8,0},{12,4},{1,9},{5,13},{9,1},{13,5},{2,10},{6,14},... | collective-permute-start | bytes 1032200 | tf_op jit(solution)/shard_map/ppermute | solution.py:364
  43.2 1.3 collective-permute-start.8
  44.5 1.1 copy-done.17
  45.6 4.5 %shard_map.166 = (f32[256,1280]{1,0:T(8,128)S(1)}, bf16[256,1280]{1,0:T(8,128)(2,1)S(1)}, bf16[256,1344]{1,0:T(8,128)(2,1)S(1)}, bf16[256,1344]{1,0:T(8,128)(2,1...) custom-call(bf16[256,1280]{1,0:T(8,128)(2,1)S(1)} %bitcast.35, f32[1,1280]{1,0:T(1,128)S(1)} %reshape.40.gain_ref, ...), custom_call_target="tpu_custom_call" | custom-call | flops 1824522240 | bytes 7127040 | tf_op jit(solution)/shard_map/pallas_call | solution.py:199
  50.2 1.1 copy-done.13
  51.2 0.9 copy-done.15
  52.1 0.9 copy-done.21
  53.0 0.8 copy-done.23
  53.8 1.5 collective-permute-start.10
  55.3 0.5 collective-permute-start.11
  55.9 9.6 %collective-permute-done.7.refs_4_ = bf16[2,32,2688]{2,1,0:T(8,128)(2,1)S(1)} collective-permute-done((bf16[2,32,2688]{2,1,0:T(8,128)(2,1)S(1)}, bf16[2,32,2688]{2,1,0:T(8,128)(2,1)S(1)}, u32[]{:S(2)}, u32[]{:S(2)}) %collective-permute-start.7) | collective-permute-done | bytes 344096 | tf_op jit(solution)/shard_map/ppermute | solution.py:364
  65.5 0.7 copy-done.10
  66.2 9.6 %collective-permute-start.9 = (bf16[256,1280]{1,0:T(8,128)(2,1)}, bf16[256,1280]{1,0:T(8,128)(2,1)}, u32[]{:S(2)}, u32[]{:S(2)}) collective-permute-start(bf16[256,1280]{1,0:T(8,128)(2,1)} %collective-permute-done.3), channel_id=1, source_target_pairs={{0,12},{4,0},{8,4},{12,8},{1,13},{5,1},{9,5},{13,9},{2,14},{6,2},{... | collective-permute-start | bytes 1966088 | tf_op jit(solution)/shard_map/ppermute | solution.py:364
  75.8 9.3 %collective-permute-done.11.refs_1_ = bf16[256,1152]{1,0:T(8,128)(2,1)} collective-permute-done((bf16[256,1152]{1,0:T(8,128)(2,1)}, bf16[256,1152]{1,0:T(8,128)(2,1)}, u32[]{:S(2)}, u32[]{:S(2)}) %collective-permute-start.11) | collective-permute-done | bytes 589856 | tf_op jit(solution)/shard_map/ppermute | solution.py:364
  85.2 1.0 copy-done.11
  86.2 1.9 shard_map.167.refs_6_.refs_2_
  88.1 1.4 copy-done.4
  89.5 1.3 copy-done.6
  90.8 4.9 %shard_map.168 = (bf16[256,1536]{1,0:T(8,128)(2,1)S(1)}, bf16[256,1344]{1,0:T(8,128)(2,1)S(1)}, bf16[256,1280]{1,0:T(8,128)(2,1)S(1)}) custom-call(s32[3]{0:T(128)S(1)} %pad_add_fusion.info_ref, bf16[256,1536]{1,0:T(8,128)(2,1)} %get-tuple-element.73.refs_0_, bf16[256,1536]{1,0:T(8,128)(2,1)} %collective-permute-done.10.refs_1_, ...), custom_call_target="tpu_custom_call" | custom-call | flops 1824522240 | bytes 7127040 | tf_op jit(solution)/shard_map/pallas_call | solution.py:284
  95.8 1.6 collective-permute-start.12
  97.4 5.2 %shard_map.169 = (bf16[4,192,1344]{2,1,0:T(8,128)(2,1)S(1)}, bf16[4,192,1344]{2,1,0:T(8,128)(2,1)}) custom-call(s32[1]{0:T(128)} %bitcast.1.core_ref, bf16[256,1536]{1,0:T(8,128)(2,1)S(1)} %get-tuple-element.82.refs_0_, bf16[256,1344]{1,0:T(8,128)(2,1)S(1)} %copy-done.22, bf16[256,1152]{1,0:T(8,128)(2,1)S(1)} %shard_map.167.refs_6_.refs_2_, ...), custom_call_target="tpu_custom_call" | custom-call | flops 943718400 | bytes 4128768 | tf_op jit(solution)/shard_map/pallas_call | solution.py:337
  102.6 0.9 collective-permute-done.12.other_ref
  104.0 3.6 %shard_map.171 = (bf16[4,160,1344]{2,1,0:T(8,128)(2,1)S(1)}, bf16[4,160,1344]{2,1,0:T(8,128)(2,1)}) custom-call(s32[1]{0:T(128)} %bitcast.1.core_ref, bf16[256,1280]{1,0:T(8,128)(2,1)S(1)} %copy-done.24, bf16[256,1344]{1,0:T(8,128)(2,1)S(1)} %get-tuple-element.90.refs_1_), custom_call_target="tpu_custom_call" | custom-call | flops 880803840 | bytes 3440640 | tf_op jit(solution)/shard_map/pallas_call | solution.py:337
  107.6 1.2 copy-done.8
  108.9 1.5 collective-permute-start.16
  111.0 7.9 %collective-permute-done.16 = bf16[128,1280]{1,0:T(8,128)(2,1)S(1)} collective-permute-done((bf16[128,1280]{1,0:T(8,128)(2,1)S(1)}, bf16[128,1280]{1,0:T(8,128)(2,1)S(1)}, u32[]{:S(2)}, u32[]{:S(2)}) %collective-permute-start.16) | collective-permute-done | bytes 327712 | tf_op jit(solution)/shard_map/ppermute | solution.py:364
  119.2 1.9 add_convert_fusion.2
  121.3 2.1 add_convert_fusion.1
  123.7 0.7 collective-permute-start.18
  124.5 1.5 collective-permute-start.17
  125.9 1.8 convert_reduce_fusion
  127.8 2.1 fusion.2
  129.9 2.1 fusion.4
  132.1 1.6 collective-permute-start.19
  133.7 10.8 %multiply_convert_fusion.1 = (bf16[768,2560]{1,0:T(8,128)(2,1)}, bf16[768,2560]{1,0:T(8,128)(2,1)}) fusion(bf16[768,1280]{1,0:T(8,128)(2,1)S(1)} %fusion.4, bf16[1280,2560]{1,0:T(8,128)(2,1)S(1)} %bitcast.37), kind=kOutput, calls=%fused_computation.1 | convolution fusion | flops 5070520320 | bytes 16384000 | tf_op jit(solution)/shard_map/dot_general | solution.py:347
  144.7 12.2 %collective-permute-done.19 = bf16[352,1344]{1,0:T(8,128)(2,1)S(1)} collective-permute-done((bf16[352,1344]{1,0:T(8,128)(2,1)S(1)}, bf16[352,1344]{1,0:T(8,128)(2,1)S(1)}, u32[]{:S(2)}, u32[]{:S(2)}) %collective-permute-start.19) | collective-permute-done | bytes 946208 | tf_op jit(solution)/shard_map/ppermute | solution.py:364
  156.9 1.4 collective-permute-start.20
  158.6 1.7 collective-permute-start.22
  160.3 5.1 %collective-permute-done.20 = bf16[128,1280]{1,0:T(8,128)(2,1)S(1)} collective-permute-done((bf16[128,1280]{1,0:T(8,128)(2,1)S(1)}, bf16[128,1280]{1,0:T(8,128)(2,1)S(1)}, u32[]{:S(2)}, u32[]{:S(2)}) %collective-permute-start.20) | collective-permute-done | bytes 327712 | tf_op jit(solution)/shard_map/ppermute | solution.py:364
  165.6 20.4 %collective-permute-done.21 = bf16[128,1280]{1,0:T(8,128)(2,1)S(1)} collective-permute-done((bf16[128,1280]{1,0:T(8,128)(2,1)S(1)}, bf16[128,1280]{1,0:T(8,128)(2,1)S(1)}, u32[]{:S(2)}, u32[]{:S(2)}) %collective-permute-start.21) | collective-permute-done | bytes 327712 | tf_op jit(solution)/shard_map/ppermute | solution.py:364
  186.0 1.1 collective-permute-start.23
  187.4 1.9 collective-permute-start.26
  189.3 3.8 %collective-permute-done.23 = bf16[128,1280]{1,0:T(8,128)(2,1)S(1)} collective-permute-done((bf16[128,1280]{1,0:T(8,128)(2,1)S(1)}, bf16[128,1280]{1,0:T(8,128)(2,1)S(1)}, u32[]{:S(2)}, u32[]{:S(2)}) %collective-permute-start.23) | collective-permute-done | bytes 327712 | tf_op jit(solution)/shard_map/ppermute | solution.py:364
  193.3 1.8 convolution_convert_fusion
  195.2 1.0 slice-done.2
  196.2 0.7 slice-done.3
  197.3 9.6 %multiply_convert_fusion = bf16[1024,2560]{1,0:T(8,128)(2,1)S(1)} fusion(bf16[1024,1280]{1,0:T(8,128)(2,1)} %copy-done.26, bf16[2560,1280]{1,0:T(8,128)(2,1)S(1)} %bitcast.39, bf16[768,2560]{1,0:T(8,128)(2,1)} %get-tuple-element.105, bf16[256,2560]{1,0:T(8,128)(2,1)S(1)} %copy-done.30), kind=kOutput, calls=%fused_computation | convolution fusion | flops 6726615040 | bytes 19660800 | tf_op jit(solution)/shard_map/dot_general | solution.py:357
  206.9 1.3 convolution_convert_fusion.1
  208.3 2.8 %collective-permute-done.26 = bf16[352,1344]{1,0:T(8,128)(2,1)S(1)} collective-permute-done((bf16[352,1344]{1,0:T(8,128)(2,1)S(1)}, bf16[352,1344]{1,0:T(8,128)(2,1)S(1)}, u32[]{:S(2)}, u32[]{:S(2)}) %collective-permute-start.26) | collective-permute-done | bytes 946208 | tf_op jit(solution)/shard_map/ppermute | solution.py:364
  211.4 0.8 slice_bitcast_fusion.1
  212.1 0.8 slice.24
  212.9 0.8 slice.22
  213.7 0.9 slice_bitcast_fusion
  214.6 3.8 %convolution_add_fusion = f32[2560,160]{0,1:T(8,128)} fusion(bf16[768,2560]{1,0:T(8,128)(2,1)S(1)} %copy-done.32, bf16[256,2560]{1,0:T(8,128)(2,1)S(1)} %copy-done.29, bf16[2560,160]{0,1:T(8,128)(2,1)S(1)} %collective-permute-done.25, bf16[1024,1280]{1,0:T(8,128)(2,1)} %copy-done.26, s32[]{:T(128)S(6)} %select_n.67), kind=kOutput, calls=%fused_computation.14 | convolution fusion | flops 850165760 | bytes 8224772 | tf_op jit(solution)/shard_map/dot_general | solution.py:351
  218.4 2.5 %convert_add_fusion.1 = f32[160,2560]{1,0:T(8,128)} fusion(bf16[160,2560]{1,0:T(8,128)(2,1)S(1)} %collective-permute-done.24, bf16[1024,2560]{1,0:T(8,128)(2,1)S(1)} %multiply_convert_fusion, s32[]{:T(128)S(6)} %select_n.67, bf16[768,1280]{1,0:T(8,128)(2,1)S(1)} %fusion.4, bf16[256,1280]{1,0:T(8,128)(2,1)S(1)} %copy-done.25), kind=kOutput, calls=%fused_computation.26 | convolution fusion | flops 840335360 | bytes 10321924 | tf_op jit(solution)/shard_map/dot_general | solution.py:351
  (110 shorter events, 4.0 us)
Async XLA Ops:
  0.6 19.6 %collective-permute-start.2 = (bf16[8,32,576]{2,1,0:T(8,128)(2,1)}, bf16[8,32,576]{2,1,0:T(8,128)(2,1)S(1)}, u32[]{:S(2)}, u32[]{:S(2)}) collective-permute-start(bf16[8,32,576]{2,1,0:T(8,128)(2,1)} %own_s.1), channel_id=1, source_target_pairs={{0,2},{2,0},{1,3},{3,1},{4,6},{6,4},{5,7},{7,5},{8,10},{10,8},{9,1... | collective-permute-start | bytes 884744 | tf_op jit(solution)/shard_map/ppermute | solution.py:364
  3.6 16.7 %collective-permute-start.1 = (bf16[8,32,768]{2,1,0:T(8,128)(2,1)}, bf16[8,32,768]{2,1,0:T(8,128)(2,1)S(1)}, u32[]{:S(2)}, u32[]{:S(2)}) collective-permute-start(bf16[8,32,768]{2,1,0:T(8,128)(2,1)} %own_d.1), channel_id=1, source_target_pairs={{0,2},{2,0},{1,3},{3,1},{4,6},{6,4},{5,7},{7,5},{8,10},{10,8},{9,1... | collective-permute-start | bytes 1179656 | tf_op jit(solution)/shard_map/ppermute | solution.py:364
  3.7 19.6 %collective-permute-start = (bf16[256,1280]{1,0:T(8,128)(2,1)}, bf16[256,1280]{1,0:T(8,128)(2,1)}, u32[]{:S(2)}, u32[]{:S(2)}) collective-permute-start(bf16[256,1280]{1,0:T(8,128)(2,1)} %bitcast.33), channel_id=1, source_target_pairs={{0,12},{4,0},{8,4},{12,8},{1,13},{5,1},{9,5},{13,9},{2,14},{6,2},{... | collective-permute-start | bytes 1966088 | tf_op jit(solution)/shard_map/ppermute | solution.py:364
  9.1 11.2 %copy-start.18 = (bf16[8,32,768]{2,1,0:T(8,128)(2,1)S(1)}, bf16[8,32,768]{2,1,0:T(8,128)(2,1)}, u32[]{:S(2)}) copy-start(bf16[8,32,768]{2,1,0:T(8,128)(2,1)} %own_d.1) | copy-start | bytes 1179652
  9.1 11.2 %copy-start.19 = (bf16[8,32,576]{2,1,0:T(8,128)(2,1)S(1)}, bf16[8,32,576]{2,1,0:T(8,128)(2,1)}, u32[]{:S(2)}) copy-start(bf16[8,32,576]{2,1,0:T(8,128)(2,1)} %own_s.1) | copy-start | bytes 884740
  9.1 11.2 %copy-start.20 = (s32[8]{0:T(128)S(1)}, s32[8]{0:T(128)}, u32[]{:S(2)}) copy-start(s32[8]{0:T(128)} %owner_ref.1) | copy-start | bytes 100
  9.1 17.7 %copy-start.28 = (f32[1280]{0:T(1024)S(1)}, f32[1280]{0:T(1024)}, u32[]{:S(2)}) copy-start(f32[1280]{0:T(1024)} %param.14) | copy-start | bytes 15364
  9.2 35.4 %copy-start.1 = (bf16[1280,768]{1,0:T(8,128)(2,1)S(1)}, bf16[1280,768]{1,0:T(8,128)(2,1)}, u32[]{:S(2)}) copy-start(bf16[1280,768]{1,0:T(8,128)(2,1)} %refs_10_.1) | copy-start | bytes 5898244
  9.2 35.4 %copy-start.3 = (bf16[1280,576]{0,1:T(8,128)(2,1)S(1)}, bf16[1280,576]{0,1:T(8,128)(2,1)}, u32[]{:S(2)}) copy-start(bf16[1280,576]{0,1:T(8,128)(2,1)} %param.19) | copy-start | bytes 4423684
  9.2 35.3 %copy-start.5 = (bf16[576,1152]{1,0:T(8,128)(2,1)S(1)}, bf16[576,1152]{1,0:T(8,128)(2,1)}, u32[]{:S(2)}) copy-start(bf16[576,1152]{1,0:T(8,128)(2,1)} %refs_8_.1) | copy-start | bytes 3981316
  9.2 35.3 %copy-start.7 = (bf16[1,256,1280]{2,1,0:T(8,128)(2,1)S(1)}, bf16[1,256,1280]{2,1,0:T(8,128)(2,1)}, u32[]{:S(2)}) copy-start(bf16[1,256,1280]{2,1,0:T(8,128)(2,1)} %param.12) | copy-start | bytes 1966084
  20.3 24.3 %copy-start = (bf16[768,1536]{1,0:T(8,128)(2,1)S(1)}, bf16[768,1536]{1,0:T(8,128)(2,1)}, u32[]{:S(2)}) copy-start(bf16[768,1536]{1,0:T(8,128)(2,1)} %refs_7_.1) | copy-start | bytes 7077892
  21.6 5.2 %collective-permute-start.4 = (bf16[4,32,2688]{2,1,0:T(8,128)(2,1)S(1)}, bf16[4,32,2688]{2,1,0:T(8,128)(2,1)S(1)}, u32[]{:S(2)}, u32[]{:S(2)}) collective-permute-start(bf16[4,32,2688]{2,1,0:T(8,128)(2,1)S(1)} %get-tuple-element.62), channel_id=1, source_target_pairs={{0,1},{1,0},{2,3},{3,2},{4,5},{5,4},{6,7},{7,6},{8,9},{9,8},{10,11... | collective-permute-start | bytes 2064392 | tf_op jit(solution)/shard_map/ppermute | solution.py:364
  21.7 17.4 %collective-permute-start.5 = (bf16[256,1280]{1,0:T(8,128)(2,1)}, bf16[256,1280]{1,0:T(8,128)(2,1)S(1)}, u32[]{:S(2)}, u32[]{:S(2)}) collective-permute-start(bf16[256,1280]{1,0:T(8,128)(2,1)} %get-tuple-element.71.refs_0_), channel_id=1, source_target_pairs={{0,2},{2,0},{1,3},{3,1},{4,6},{6,4},{5,7},{7,5},{8,10},{10,8},{9,1... | collective-permute-start | bytes 1966088 | tf_op jit(solution)/shard_map/ppermute | solution.py:364
  23.3 32.1 %collective-permute-start.3 = (bf16[256,1280]{1,0:T(8,128)(2,1)}, bf16[256,1280]{1,0:T(8,128)(2,1)}, u32[]{:S(2)}, u32[]{:S(2)}) collective-permute-start(bf16[256,1280]{1,0:T(8,128)(2,1)} %collective-permute-done), channel_id=1, source_target_pairs={{0,12},{4,0},{8,4},{12,8},{1,13},{5,1},{9,5},{13,9},{2,14},{6,2},{... | collective-permute-start | bytes 1966088 | tf_op jit(solution)/shard_map/ppermute | solution.py:364
  39.1 16.8 %collective-permute-start.6 = (bf16[2,32,2688]{2,1,0:T(8,128)(2,1)S(1)}, bf16[2,32,2688]{2,1,0:T(8,128)(2,1)S(1)}, u32[]{:S(2)}, u32[]{:S(2)}) collective-permute-start(bf16[2,32,2688]{2,1,0:T(8,128)(2,1)S(1)} %get-tuple-element.68), channel_id=1, source_target_pairs={{0,4},{4,8},{8,12},{12,0},{1,5},{5,9},{9,13},{13,1},{2,6},{6,10},{... | collective-permute-start | bytes 1032200 | tf_op jit(solution)/shard_map/ppermute | solution.py:364
  40.6 24.9 %collective-permute-start.7 = (bf16[2,32,2688]{2,1,0:T(8,128)(2,1)S(1)}, bf16[2,32,2688]{2,1,0:T(8,128)(2,1)S(1)}, u32[]{:S(2)}, u32[]{:S(2)}) collective-permute-start(bf16[2,32,2688]{2,1,0:T(8,128)(2,1)S(1)} %get-tuple-element.69), channel_id=1, source_target_pairs={{0,8},{4,12},{8,0},{12,4},{1,9},{5,13},{9,1},{13,5},{2,10},{6,14},... | collective-permute-start | bytes 1032200 | tf_op jit(solution)/shard_map/ppermute | solution.py:364
  43.2 22.3 %collective-permute-start.8 = (bf16[2,32,2688]{2,1,0:T(8,128)(2,1)S(1)}, bf16[2,32,2688]{2,1,0:T(8,128)(2,1)S(1)}, u32[]{:S(2)}, u32[]{:S(2)}) collective-permute-start(bf16[2,32,2688]{2,1,0:T(8,128)(2,1)S(1)} %get-tuple-element.70), channel_id=1, source_target_pairs={{0,12},{4,0},{8,4},{12,8},{1,13},{5,1},{9,5},{13,9},{2,14},{6,2},{... | collective-permute-start | bytes 1032200 | tf_op jit(solution)/shard_map/ppermute | solution.py:364
  44.5 1.1 copy-start.17
  50.2 1.1 copy-start.13
  51.2 0.9 copy-start.15
  52.1 0.9 copy-start.21
  53.0 0.9 copy-start.23
  53.8 34.3 %collective-permute-start.10 = (bf16[256,1536]{1,0:T(8,128)(2,1)}, bf16[256,1536]{1,0:T(8,128)(2,1)}, u32[]{:S(2)}, u32[]{:S(2)}) collective-permute-start(bf16[256,1536]{1,0:T(8,128)(2,1)} %get-tuple-element.73.refs_0_), channel_id=1, source_target_pairs={{0,2},{2,0},{1,3},{3,1},{4,6},{6,4},{5,7},{7,5},{8,10},{10,8},{9,1... | collective-permute-start | bytes 2359304 | tf_op jit(solution)/shard_map/ppermute | solution.py:364
  55.3 29.8 %collective-permute-start.11 = (bf16[256,1152]{1,0:T(8,128)(2,1)}, bf16[256,1152]{1,0:T(8,128)(2,1)}, u32[]{:S(2)}, u32[]{:S(2)}) collective-permute-start(bf16[256,1152]{1,0:T(8,128)(2,1)} %get-tuple-element.75.refs_0_), channel_id=1, source_target_pairs={{0,2},{2,0},{1,3},{3,1},{4,6},{6,4},{5,7},{7,5},{8,10},{10,8},{9,1... | collective-permute-start | bytes 1769480 | tf_op jit(solution)/shard_map/ppermute | solution.py:364
  65.5 0.7 copy-start.10
  66.2 29.6 %collective-permute-start.9 = (bf16[256,1280]{1,0:T(8,128)(2,1)}, bf16[256,1280]{1,0:T(8,128)(2,1)}, u32[]{:S(2)}, u32[]{:S(2)}) collective-permute-start(bf16[256,1280]{1,0:T(8,128)(2,1)} %collective-permute-done.3), channel_id=1, source_target_pairs={{0,12},{4,0},{8,4},{12,8},{1,13},{5,1},{9,5},{13,9},{2,14},{6,2},{... | collective-permute-start | bytes 1966088 | tf_op jit(solution)/shard_map/ppermute | solution.py:364
  75.8 12.3 %copy-start.2 = (bf16[1280,768]{1,0:T(8,128)(2,1)S(1)}, bf16[1280,768]{1,0:T(8,128)(2,1)}, u32[]{:S(2)}) copy-start(bf16[1280,768]{1,0:T(8,128)(2,1)} %refs_10_.1) | copy-start | bytes 5898244
  85.2 1.0 copy-start.11
  86.1 2.0 copy-start.12
  86.1 2.0 copy-start.16
  88.1 1.4 copy-start.4
  89.5 1.3 copy-start.6
  90.8 6.6 %copy-start.22 = (bf16[256,1344]{1,0:T(8,128)(2,1)S(1)}, bf16[256,1344]{1,0:T(8,128)(2,1)}, u32[]{:S(2)}) copy-start(bf16[256,1344]{1,0:T(8,128)(2,1)} %copy-done.21) | copy-start | bytes 2064388
  95.8 7.7 %copy-start.14 = (f32[256,1280]{1,0:T(8,128)S(1)}, f32[256,1280]{1,0:T(8,128)}, u32[]{:S(2)}) copy-start(f32[256,1280]{1,0:T(8,128)} %copy-done.13) | copy-start | bytes 3932164
  95.8 7.7 %collective-permute-start.12 = (bf16[128,1280]{1,0:T(8,128)(2,1)S(1)}, bf16[128,1280]{1,0:T(8,128)(2,1)S(1)}, u32[]{:S(2)}, u32[]{:S(2)}) collective-permute-start(bf16[128,1280]{1,0:T(8,128)(2,1)S(1)} %constant_dynamic-slice_fusion), channel_id=1, source_target_pairs={{0,2},{2,0},{1,3},{3,1},{4,6},{6,4},{5,7},{7,5},{8,10},{10,8},{9,1... | collective-permute-start | bytes 983048 | tf_op jit(solution)/shard_map/ppermute | solution.py:364
  97.4 6.6 %copy-start.24 = (bf16[256,1280]{1,0:T(8,128)(2,1)S(1)}, bf16[256,1280]{1,0:T(8,128)(2,1)}, u32[]{:S(2)}) copy-start(bf16[256,1280]{1,0:T(8,128)(2,1)} %copy-done.23) | copy-start | bytes 1966084
  107.6 1.2 copy-start.8
  108.9 10.3 %collective-permute-start.15 = (bf16[4,160,1344]{2,1,0:T(8,128)(2,1)}, bf16[4,160,1344]{2,1,0:T(8,128)(2,1)}, u32[]{:S(2)}, u32[]{:S(2)}) collective-permute-start(bf16[4,160,1344]{2,1,0:T(8,128)(2,1)} %get-tuple-element.92), channel_id=1, source_target_pairs={{0,1},{1,0},{2,3},{3,2},{4,5},{5,4},{6,7},{7,6},{8,9},{9,8},{10,11... | collective-permute-start | bytes 5160968 | tf_op jit(solution)/shard_map/ppermute | solution.py:364
  108.9 10.1 %collective-permute-start.16 = (bf16[128,1280]{1,0:T(8,128)(2,1)S(1)}, bf16[128,1280]{1,0:T(8,128)(2,1)S(1)}, u32[]{:S(2)}, u32[]{:S(2)}) collective-permute-start(bf16[128,1280]{1,0:T(8,128)(2,1)S(1)} %shard_map.170), channel_id=1, source_target_pairs={{0,2},{2,0},{1,3},{3,1},{4,6},{6,4},{5,7},{7,5},{8,10},{10,8},{9,1... | collective-permute-start | bytes 983048 | tf_op jit(solution)/shard_map/ppermute | solution.py:364
  110.4 10.9 %collective-permute-start.14 = (bf16[4,192,1344]{2,1,0:T(8,128)(2,1)}, bf16[4,192,1344]{2,1,0:T(8,128)(2,1)}, u32[]{:S(2)}, u32[]{:S(2)}) collective-permute-start(bf16[4,192,1344]{2,1,0:T(8,128)(2,1)} %get-tuple-element.88), channel_id=1, source_target_pairs={{0,1},{1,0},{2,3},{3,2},{4,5},{5,4},{6,7},{7,6},{8,9},{9,8},{10,11... | collective-permute-start | bytes 6193160 | tf_op jit(solution)/shard_map/ppermute | solution.py:364
  110.6 8.6 %copy-start.9 = (bf16[4,160,1344]{2,1,0:T(8,128)(2,1)S(1)}, bf16[4,160,1344]{2,1,0:T(8,128)(2,1)}, u32[]{:S(2)}) copy-start(bf16[4,160,1344]{2,1,0:T(8,128)(2,1)} %copy-done.8) | copy-start | bytes 5160964
  110.6 13.1 %collective-permute-start.13 = (bf16[128,1280]{1,0:T(8,128)(2,1)S(1)}, bf16[128,1280]{1,0:T(8,128)(2,1)S(1)}, u32[]{:S(2)}, u32[]{:S(2)}) collective-permute-start(bf16[128,1280]{1,0:T(8,128)(2,1)S(1)} %shard_map.170), channel_id=1, source_target_pairs={{0,12},{4,0},{8,4},{12,8},{1,13},{5,1},{9,5},{13,9},{2,14},{6,2},{... | collective-permute-start | bytes 983048 | tf_op jit(solution)/shard_map/ppermute | solution.py:364
  123.4 10.3 %slice-start = ((s8[6553600]{0:T(1024)(128)(4,1)}), s8[4194304]{0:T(1024)(128)(4,1)S(1)}, s32[]{:S(2)}) async-start(s8[6553600]{0:T(1024)(128)(4,1)} %bitcast.36), calls=%async_computation | async-start | bytes 8388608
  123.6 6.3 %copy-start.27 = (f32[1280]{0:T(1024)S(1)}, f32[1280]{0:T(1024)}, u32[]{:S(2)}) copy-start(f32[1280]{0:T(1024)} %param.13) | copy-start | bytes 15364
  123.7 10.0 %slice-start.1 = ((s8[6553600]{0:T(1024)(128)(4,1)}), s8[2359296]{0:T(1024)(128)(4,1)S(1)}, s32[]{:S(2)}) async-start(s8[6553600]{0:T(1024)(128)(4,1)} %bitcast.36), calls=%async_computation.1 | async-start | bytes 4718592
  123.7 21.0 %collective-permute-start.18 = (bf16[128,1280]{1,0:T(8,128)(2,1)S(1)}, bf16[128,1280]{1,0:T(8,128)(2,1)S(1)}, u32[]{:S(2)}, u32[]{:S(2)}) collective-permute-start(bf16[128,1280]{1,0:T(8,128)(2,1)S(1)} %collective-permute-done.13), channel_id=1, source_target_pairs={{0,12},{4,0},{8,4},{12,8},{1,13},{5,1},{9,5},{13,9},{2,14},{6,2},{... | collective-permute-start | bytes 983048 | tf_op jit(solution)/shard_map/ppermute | solution.py:364
  124.5 20.1 %collective-permute-start.17 = (bf16[128,1280]{1,0:T(8,128)(2,1)S(1)}, bf16[128,1280]{1,0:T(8,128)(2,1)S(1)}, u32[]{:S(2)}, u32[]{:S(2)}) collective-permute-start(bf16[128,1280]{1,0:T(8,128)(2,1)S(1)} %collective-permute-done.13), channel_id=1, source_target_pairs={{0,2},{2,0},{1,3},{3,1},{4,6},{6,4},{5,7},{7,5},{8,10},{10,8},{9,1... | collective-permute-start | bytes 983048 | tf_op jit(solution)/shard_map/ppermute | solution.py:364
  132.1 24.9 %collective-permute-start.19 = (bf16[352,1344]{1,0:T(8,128)(2,1)S(1)}, bf16[352,1344]{1,0:T(8,128)(2,1)S(1)}, u32[]{:S(2)}, u32[]{:S(2)}) collective-permute-start(bf16[352,1344]{1,0:T(8,128)(2,1)S(1)} %pad_maximum_fusion.4), channel_id=1, source_target_pairs={{0,4},{4,8},{8,12},{12,0},{1,5},{5,9},{9,13},{13,1},{2,6},{6,10},{... | collective-permute-start | bytes 2838536 | tf_op jit(solution)/shard_map/ppermute | solution.py:364
  156.9 29.1 %collective-permute-start.21 = (bf16[128,1280]{1,0:T(8,128)(2,1)S(1)}, bf16[128,1280]{1,0:T(8,128)(2,1)S(1)}, u32[]{:S(2)}, u32[]{:S(2)}) collective-permute-start(bf16[128,1280]{1,0:T(8,128)(2,1)S(1)} %collective-permute-done.18), channel_id=1, source_target_pairs={{0,12},{4,0},{8,4},{12,8},{1,13},{5,1},{9,5},{13,9},{2,14},{6,2},{... | collective-permute-start | bytes 983048 | tf_op jit(solution)/shard_map/ppermute | solution.py:364
  156.9 8.5 %collective-permute-start.20 = (bf16[128,1280]{1,0:T(8,128)(2,1)S(1)}, bf16[128,1280]{1,0:T(8,128)(2,1)S(1)}, u32[]{:S(2)}, u32[]{:S(2)}) collective-permute-start(bf16[128,1280]{1,0:T(8,128)(2,1)S(1)} %collective-permute-done.18), channel_id=1, source_target_pairs={{0,2},{2,0},{1,3},{3,1},{4,6},{6,4},{5,7},{7,5},{8,10},{10,8},{9,1... | collective-permute-start | bytes 983048 | tf_op jit(solution)/shard_map/ppermute | solution.py:364
  158.6 27.4 %collective-permute-start.22 = (bf16[352,1344]{1,0:T(8,128)(2,1)S(1)}, bf16[352,1344]{1,0:T(8,128)(2,1)S(1)}, u32[]{:S(2)}, u32[]{:S(2)}) collective-permute-start(bf16[352,1344]{1,0:T(8,128)(2,1)S(1)} %add_convert_fusion.4), channel_id=1, source_target_pairs={{0,4},{4,8},{8,12},{12,0},{1,5},{5,9},{9,13},{13,1},{2,6},{6,10},{... | collective-permute-start | bytes 2838536 | tf_op jit(solution)/shard_map/ppermute | solution.py:364
  165.5 27.8 %copy-start.31 = (bf16[768,2560]{1,0:T(8,128)(2,1)S(1)}, bf16[768,2560]{1,0:T(8,128)(2,1)}, u32[]{:S(2)}) copy-start(bf16[768,2560]{1,0:T(8,128)(2,1)} %get-tuple-element.104) | copy-start | bytes 11796484
  165.6 27.7 %copy-start.29 = (bf16[256,2560]{1,0:T(8,128)(2,1)S(1)}, bf16[256,2560]{1,0:T(8,128)(2,1)}, u32[]{:S(2)}) copy-start(bf16[256,2560]{1,0:T(8,128)(2,1)} %get-tuple-element.102) | copy-start | bytes 3932164
  186.0 7.1 %collective-permute-start.23 = (bf16[128,1280]{1,0:T(8,128)(2,1)S(1)}, bf16[128,1280]{1,0:T(8,128)(2,1)S(1)}, u32[]{:S(2)}, u32[]{:S(2)}) collective-permute-start(bf16[128,1280]{1,0:T(8,128)(2,1)S(1)} %collective-permute-done.21), channel_id=1, source_target_pairs={{0,2},{2,0},{1,3},{3,1},{4,6},{6,4},{5,7},{7,5},{8,10},{10,8},{9,1... | collective-permute-start | bytes 983048 | tf_op jit(solution)/shard_map/ppermute | solution.py:364
  187.4 23.7 %collective-permute-start.26 = (bf16[352,1344]{1,0:T(8,128)(2,1)S(1)}, bf16[352,1344]{1,0:T(8,128)(2,1)S(1)}, u32[]{:S(2)}, u32[]{:S(2)}) collective-permute-start(bf16[352,1344]{1,0:T(8,128)(2,1)S(1)} %add_convert_fusion.3), channel_id=1, source_target_pairs={{0,4},{4,8},{8,12},{12,0},{1,5},{5,9},{9,13},{13,1},{2,6},{6,10},{... | collective-permute-start | bytes 2838536 | tf_op jit(solution)/shard_map/ppermute | solution.py:364
  193.1 3.1 %slice-start.2 = ((s8[6553600]{0:T(1024)(128)(4,1)}), s8[4194304]{0:T(1024)(128)(4,1)S(1)}, s32[]{:S(2)}) async-start(s8[6553600]{0:T(1024)(128)(4,1)} %bitcast.38), calls=%async_computation.2 | async-start | bytes 8388608
  193.3 1.9 copy-start.26
  193.3 3.7 %slice-start.3 = ((s8[6553600]{0:T(1024)(128)(4,1)}), s8[2359296]{0:T(1024)(128)(4,1)S(1)}, s32[]{:S(2)}) async-start(s8[6553600]{0:T(1024)(128)(4,1)} %bitcast.38), calls=%async_computation.3 | async-start | bytes 4718592
  193.3 4.0 %copy-start.30 = (bf16[256,2560]{1,0:T(8,128)(2,1)S(1)}, bf16[256,2560]{1,0:T(8,128)(2,1)}, u32[]{:S(2)}) copy-start(bf16[256,2560]{1,0:T(8,128)(2,1)} %get-tuple-element.97) | copy-start | bytes 3932164
  195.1 19.4 %collective-permute-start.25 = (bf16[2560,160]{0,1:T(8,128)(2,1)S(1)}, bf16[2560,160]{0,1:T(8,128)(2,1)S(1)}, u32[]{:S(2)}, u32[]{:S(2)}) collective-permute-start(bf16[2560,160]{0,1:T(8,128)(2,1)S(1)} %convolution_convert_fusion), channel_id=1, source_target_pairs={{0,1},{1,0},{2,3},{3,2},{4,5},{5,4},{6,7},{7,6},{8,9},{9,8},{10,11... | collective-permute-start | bytes 2457608 | tf_op jit(solution)/shard_map/ppermute | solution.py:364
  197.3 9.6 %copy-start.25 = (bf16[256,1280]{1,0:T(8,128)(2,1)S(1)}, bf16[256,1280]{1,0:T(8,128)(2,1)}, u32[]{:S(2)}) copy-start(bf16[256,1280]{1,0:T(8,128)(2,1)} %get-tuple-element.55) | copy-start | bytes 1966084
  208.3 10.1 %collective-permute-start.24 = (bf16[160,2560]{1,0:T(8,128)(2,1)S(1)}, bf16[160,2560]{1,0:T(8,128)(2,1)S(1)}, u32[]{:S(2)}, u32[]{:S(2)}) collective-permute-start(bf16[160,2560]{1,0:T(8,128)(2,1)S(1)} %convolution_convert_fusion.1), channel_id=1, source_target_pairs={{0,1},{1,0},{2,3},{3,2},{4,5},{5,4},{6,7},{7,6},{8,9},{9,8},{10,11... | collective-permute-start | bytes 2457608 | tf_op jit(solution)/shard_map/ppermute | solution.py:364
  211.2 3.4 %copy-start.32 = (bf16[768,2560]{1,0:T(8,128)(2,1)S(1)}, bf16[768,2560]{1,0:T(8,128)(2,1)}, u32[]{:S(2)}) copy-start(bf16[768,2560]{1,0:T(8,128)(2,1)} %get-tuple-element.104) | copy-start | bytes 11796484
